TPU v7x, 32 devices: a whole 2x2x4 slice. The times are simulated.
32 devices in a mesh: wide: 8 (over z, y), narrow: 4 (over x, core).
Axes of the slice: x: 2, y: 2, z: 4, core: 2. Of those that a mesh axis runs over, the one named last changes fastest.
Arguments:
- inputs: bfloat16 [16384, 768], P(('wide', 'narrow')), may hold values from -6 to 6
- gain_attn: bfloat16 [768], P(('wide', 'narrow')), may hold values from 0.5 to 1.5
- w_query: bfloat16 [768, 768], P(('wide', 'narrow')), may hold values from -0.21875 to 0.21875
- w_key: bfloat16 [768, 768], P(('wide', 'narrow')), may hold values from -0.21875 to 0.21875
- w_value: bfloat16 [768, 768], P(('wide', 'narrow')), may hold values from -0.21875 to 0.21875
- w_output: bfloat16 [768, 768], P(('wide', 'narrow')), may hold values from -2.5 to 2.5
- rel_bias: float32 [32, 12], replicated, may hold values from -4 to 4
- gain_ffn: bfloat16 [768], P(('wide', 'narrow')), may hold values from 0.5 to 1.5
- w_router: bfloat16 [768, 32], P(('wide', 'narrow')), may hold values from -0.21875 to 0.21875
- expert_in: bfloat16 [32, 768, 3072], P('wide', None, 'narrow'), may hold values from -0.21875 to 0.21875
- expert_out: bfloat16 [32, 3072, 768], P('wide', 'narrow'), may hold values from -6 to 6
- routes: int32 [16384, 1], P(('wide', 'narrow')), may hold values from 0 to 31
- capacity: int32 [32], P(('wide', 'narrow')), may hold values from 1 to 2, as said below
- cotangent: bfloat16 [16384, 768], P(('wide', 'narrow')), may hold values from -6 to 6
Outputs:
- result: bfloat16 [16384, 768], P(('wide', 'narrow'))
- grad_inputs: float32 [16384, 768], P(('wide', 'narrow'))
- grad_gain_attn: float32 [768], P(('wide', 'narrow'))
- grad_query: float32 [768, 768], P(('wide', 'narrow'))
- grad_key: float32 [768, 768], P(('wide', 'narrow'))
- grad_value: float32 [768, 768], P(('wide', 'narrow'))
- grad_output: float32 [768, 768], P(('wide', 'narrow'))
- grad_rel_bias: float32 [32, 12], replicated
- grad_gain_ffn: float32 [768], P(('wide', 'narrow'))
- grad_router: float32 [768, 32], P(('wide', 'narrow'))
- grad_expert_in: float32 [32, 768, 3072], P('wide', None, 'narrow')
- grad_expert_out: float32 [32, 3072, 768], P('wide', 'narrow')
Inputs may be any that keep to these rules, and one draw needn't show every extreme that they name: `capacity`: each group of 512 tokens has its own factor; both values occur.
All inputs are finite; a program needn't handle non-finite values.
Results may differ from a plain program's by a relative error of at most 0.019.
Values may be sent and summed in bfloat16 or wider, within the bound.
A program may use at most 320 MiB of HBM per device.

v0:
```python
import jax
import jax.numpy as jnp
import numpy as np
from jax import lax
from jax.sharding import PartitionSpec as P

HEADS = 12
SEQ_LEN = 512


EPSILON = 1e-06
HIGHEST = lax.Precision.HIGHEST
ROOT_TWO_PI = 0.7978845608028654
CUBIC = 0.044715


def bucket_offsets(length, bucket_count):
    offsets = np.arange(-(length - 1), length)
    half_count = bucket_count // 2
    exact_count = half_count // 2
    distance = np.abs(offsets)
    scaled = exact_count + np.floor(
        np.log(np.maximum(distance, 1) / exact_count)
        / np.log(128.0 / exact_count)
        * (half_count - exact_count)
    ).astype(np.int64)
    scaled = np.minimum(scaled, half_count - 1)
    return ((offsets > 0) * half_count + np.where(distance < exact_count, distance, scaled)).astype(
        np.int32
    )


def offset_index(row_start, row_count, length):
    return (
        np.arange(length)[None, :]
        - np.arange(row_start, row_start + row_count)[:, None]
        + length
        - 1
    ).astype(np.int32)


def offset_bias(rel_bias, length):
    buckets_seen = jnp.asarray(bucket_offsets(length, rel_bias.shape[0]))
    picks = (
        buckets_seen[:, None] == jnp.arange(rel_bias.shape[0], dtype=jnp.int32)[None, :]
    ).astype(jnp.float32)
    return jnp.dot(picks, rel_bias, precision=HIGHEST).T


def gelu_value(values):
    return jax.nn.gelu(values, approximate=True)


def gelu_slope(values):
    inner = jnp.tanh(ROOT_TWO_PI * (values + CUBIC * values * values * values))
    return 0.5 * (1.0 + inner) + 0.5 * values * (1.0 - inner * inner) * ROOT_TWO_PI * (
        1.0 + 3.0 * CUBIC * values * values
    )


def inverse_rms(values):
    return lax.rsqrt(jnp.mean(values * values, axis=-1, keepdims=True) + EPSILON)


def norm_backward(values, inverse, gain, grad_normed):
    scaled = grad_normed * gain
    grad_gain = jnp.sum(grad_normed * values * inverse, axis=0)
    inner = jnp.mean(scaled * values, axis=-1, keepdims=True)
    return (inverse * (scaled - values * inverse * inverse * inner), grad_gain)


def block_scores(query_block, key_seq, bias_rows, row_start, block_rows, length):
    index = jnp.asarray(offset_index(row_start, block_rows, length))
    scores = (
        jnp.einsum("ihd,jhd->hij", query_block, key_seq, preferred_element_type=jnp.float32) * 0.125
    )
    return scores + jnp.take(bias_rows, index, axis=1)


def attention_forward(query_seqs, key_seqs, value_seqs, bias_rows, block_rows):
    length = query_seqs.shape[1]

    def one_sequence(packed):
        query_seq, key_seq, value_seq = packed
        scores = block_scores(query_seq, key_seq, bias_rows, 0, block_rows, length)
        row_peak = jnp.max(scores, axis=-1, keepdims=True)
        exponent = jnp.exp(scores - row_peak)
        row_total = jnp.sum(exponent, axis=-1, keepdims=True)
        weights = (exponent / row_total).astype(jnp.bfloat16)
        outputs = [
            jnp.einsum(
                "hij,jhd->ihd", weights, value_seq, preferred_element_type=jnp.float32
            ).astype(jnp.bfloat16)
        ]
        totals = [(row_peak + jnp.log(row_total))[:, :, 0]]
        return (jnp.concatenate(outputs, axis=0), jnp.concatenate(totals, axis=1))

    return lax.map(one_sequence, (query_seqs, key_seqs, value_seqs))


def attention_backward(
    query_seqs, key_seqs, value_seqs, grad_seqs, log_sums, bias_rows, block_rows, bucket_count
):
    length = query_seqs.shape[1]
    table = bucket_offsets(length, bucket_count)

    def one_sequence(packed):
        query_seq, key_seq, value_seq, grad_seq, sums_seq = packed
        grad_keys = jnp.zeros(key_seq.shape, jnp.float32)
        grad_values = jnp.zeros(value_seq.shape, jnp.float32)
        grad_bias = jnp.zeros((key_seq.shape[1], bucket_count), jnp.float32)
        scores = block_scores(query_seq, key_seq, bias_rows, 0, block_rows, length)
        weights = jnp.exp(scores - sums_seq[:, 0:block_rows, None])
        grad_weights = jnp.einsum(
            "ihd,jhd->hij", grad_seq, value_seq, preferred_element_type=jnp.float32
        )
        inner = jnp.sum(weights * grad_weights, axis=-1, keepdims=True)
        grad_scores = (weights * (grad_weights - inner)).astype(jnp.bfloat16)
        grad_queries = [
            jnp.einsum("hij,jhd->ihd", grad_scores, key_seq, preferred_element_type=jnp.float32)
            * 0.125
        ]
        grad_keys = (
            grad_keys
            + jnp.einsum("hij,ihd->jhd", grad_scores, query_seq, preferred_element_type=jnp.float32)
            * 0.125
        )
        grad_values = grad_values + jnp.einsum(
            "hij,ihd->jhd",
            weights.astype(jnp.bfloat16),
            grad_seq,
            preferred_element_type=jnp.float32,
        )
        block_buckets = jnp.asarray(table[offset_index(0, block_rows, length)])
        picks = (
            block_buckets[:, :, None] == jnp.arange(bucket_count, dtype=jnp.int32)[None, None, :]
        ).astype(jnp.bfloat16)
        grad_bias = grad_bias + jnp.einsum(
            "hij,ijb->hb", grad_scores, picks, preferred_element_type=jnp.float32
        )
        return (jnp.concatenate(grad_queries, axis=0), grad_keys, grad_values, grad_bias)

    return lax.map(one_sequence, (query_seqs, key_seqs, value_seqs, grad_seqs, log_sums))


def shards(
    inputs,
    gain_attn,
    w_query,
    w_key,
    w_value,
    w_output,
    rel_bias,
    gain_ffn,
    w_router,
    expert_in,
    expert_out,
    routes,
    capacity,
    cotangent,
):
    query_w, key_w, value_w, output_w, router_w, attn_gain, ffn_gain = (
        lax.all_gather(w_query, ("wide", "narrow"), axis=0, tiled=True),
        lax.all_gather(w_key, ("wide", "narrow"), axis=0, tiled=True),
        lax.all_gather(w_value, ("wide", "narrow"), axis=0, tiled=True),
        lax.all_gather(w_output, ("wide", "narrow"), axis=0, tiled=True),
        lax.all_gather(w_router, ("wide", "narrow"), axis=0, tiled=True),
        lax.all_gather(gain_attn, ("wide", "narrow"), axis=0, tiled=True),
        lax.all_gather(gain_ffn, ("wide", "narrow"), axis=0, tiled=True),
    )
    tok_count, width = inputs.shape
    head_dim = width // HEADS
    wide_count = lax.axis_size("wide")
    expert_count = router_w.shape[1]
    local_experts = expert_in.shape[0]
    slots = 2 * tok_count // expert_count
    seq_shape = (tok_count // SEQ_LEN, SEQ_LEN, HEADS, head_dim)
    block_rows = min(512, SEQ_LEN)
    attn_scale = attn_gain.astype(jnp.float32)
    ffn_scale = ffn_gain.astype(jnp.float32)
    tokens = inputs.astype(jnp.float32)
    inverse_attn = inverse_rms(tokens)
    normed_attn = (tokens * inverse_attn * attn_scale).astype(jnp.bfloat16)
    query_rows = jnp.dot(normed_attn, query_w, preferred_element_type=jnp.float32).astype(
        jnp.bfloat16
    )
    key_rows = jnp.dot(normed_attn, key_w, preferred_element_type=jnp.float32).astype(jnp.bfloat16)
    value_rows = jnp.dot(normed_attn, value_w, preferred_element_type=jnp.float32).astype(
        jnp.bfloat16
    )
    bias_rows = offset_bias(rel_bias, SEQ_LEN)
    attended, log_sums = attention_forward(
        query_rows.reshape(seq_shape),
        key_rows.reshape(seq_shape),
        value_rows.reshape(seq_shape),
        bias_rows,
        block_rows,
    )
    attended = attended.reshape(tok_count, width)
    mixed = tokens + jnp.dot(attended, output_w, preferred_element_type=jnp.float32)
    inverse_ffn = inverse_rms(mixed)
    normed_ffn = (mixed * inverse_ffn * ffn_scale).astype(jnp.bfloat16)
    logits = jnp.dot(normed_ffn, router_w, preferred_element_type=jnp.float32)
    router_peak = jnp.max(logits, axis=-1, keepdims=True)
    router_exp = jnp.exp(logits - router_peak)
    router_probs = router_exp / jnp.sum(router_exp, axis=-1, keepdims=True)
    route_ids = routes[:, 0]
    chosen = route_ids[:, None] == jnp.arange(expert_count, dtype=jnp.int32)[None, :]
    gate = jnp.sum(jnp.where(chosen, router_probs, 0.0), axis=-1)
    running = jnp.cumsum(chosen.astype(jnp.int32), axis=0, dtype=jnp.int32)
    position = jnp.sum(jnp.where(chosen, running, 0), axis=1, dtype=jnp.int32) - 1
    limit = capacity[0] * tok_count // expert_count
    kept = position < limit
    slot_ids = jnp.where(kept, route_ids * slots + position, expert_count * slots)
    owners = (
        jnp.full((expert_count * slots + 1,), tok_count, jnp.int32)
        .at[slot_ids]
        .set(jnp.arange(tok_count, dtype=jnp.int32))[:-1]
    )
    zero_row = jnp.zeros((1, width), jnp.bfloat16)
    dispatched = jnp.take(jnp.concatenate([normed_ffn, zero_row], axis=0), owners, axis=0)
    received = lax.all_to_all(
        dispatched.reshape(wide_count, local_experts * slots, width),
        "wide",
        split_axis=0,
        concat_axis=0,
        tiled=True,
    )
    gathered = lax.all_gather(received, "narrow", axis=0, tiled=True)
    piece = gathered.reshape(wide_count * lax.axis_size("narrow"), local_experts, slots, width)
    pre = jnp.einsum("secd,edf->secf", piece, expert_in, preferred_element_type=jnp.float32)
    hidden = gelu_value(pre).astype(jnp.bfloat16)
    expert_result = lax.psum_scatter(
        jnp.einsum("secf,efd->secd", hidden, expert_out, preferred_element_type=jnp.float32)
        .reshape(wide_count * lax.axis_size("narrow"), local_experts * slots, width)
        .astype(jnp.bfloat16),
        "narrow",
        scatter_dimension=0,
        tiled=True,
    )
    returned = lax.all_to_all(expert_result, "wide", split_axis=0, concat_axis=0, tiled=True)
    combined = jnp.take(
        jnp.concatenate([returned.reshape(expert_count * slots, width), zero_row], axis=0),
        slot_ids,
        axis=0,
    ).astype(jnp.float32)
    result = (mixed + gate[:, None] * combined).astype(jnp.bfloat16)
    grad_result = cotangent.astype(jnp.float32)
    token_grads = (gate[:, None] * grad_result).astype(jnp.bfloat16)
    slot_grads = jnp.take(jnp.concatenate([token_grads, zero_row], axis=0), owners, axis=0)
    grad_gate = jnp.sum(grad_result * combined, axis=-1)
    grad_logits = (
        router_probs * (jnp.where(chosen, grad_gate[:, None], 0.0) - (gate * grad_gate)[:, None])
    ).astype(jnp.bfloat16)
    grad_router_part = jnp.einsum(
        "td,te->de", normed_ffn, grad_logits, preferred_element_type=jnp.float32
    )
    grad_normed_ffn = jnp.dot(grad_logits, router_w.T, preferred_element_type=jnp.float32)
    slot_received = lax.all_to_all(
        slot_grads.reshape(wide_count, local_experts * slots, width),
        "wide",
        split_axis=0,
        concat_axis=0,
        tiled=True,
    )
    grads_all = lax.all_gather(slot_received, "narrow", axis=0, tiled=True)
    row_total = grads_all.shape[0]
    pieces = gathered.reshape(row_total, local_experts, slots, width)
    grad_pieces = grads_all.reshape(row_total, local_experts, slots, width)
    pre_all = jnp.einsum("secd,edf->secf", pieces, expert_in, preferred_element_type=jnp.float32)
    hidden_all = gelu_value(pre_all).astype(jnp.bfloat16)
    grad_hidden = jnp.einsum(
        "secd,efd->secf", grad_pieces, expert_out, preferred_element_type=jnp.float32
    )
    grad_pre = (grad_hidden * gelu_slope(pre_all)).astype(jnp.bfloat16)
    grad_expert_out = jnp.einsum(
        "secf,secd->efd", hidden_all, grad_pieces, preferred_element_type=jnp.float32
    )
    grad_expert_in = jnp.einsum(
        "secd,secf->edf", pieces, grad_pre, preferred_element_type=jnp.float32
    )
    input_grads = lax.psum_scatter(
        jnp.einsum("secf,edf->secd", grad_pre, expert_in, preferred_element_type=jnp.float32)
        .reshape(wide_count * lax.axis_size("narrow"), local_experts * slots, width)
        .astype(jnp.bfloat16),
        "narrow",
        scatter_dimension=0,
        tiled=True,
    )
    grads_back = lax.all_to_all(input_grads, "wide", split_axis=0, concat_axis=0, tiled=True)
    grad_normed_ffn = grad_normed_ffn + jnp.take(
        jnp.concatenate([grads_back.reshape(expert_count * slots, width), zero_row], axis=0),
        slot_ids,
        axis=0,
    ).astype(jnp.float32)
    grad_norm_ffn, grad_gain_ffn = norm_backward(mixed, inverse_ffn, ffn_scale, grad_normed_ffn)
    grad_mixed = grad_result + grad_norm_ffn
    grad_branch = grad_mixed.astype(jnp.bfloat16)
    grad_output_part = jnp.einsum(
        "td,te->de", attended, grad_branch, preferred_element_type=jnp.float32
    )
    grad_attended = jnp.dot(grad_branch, output_w.T, preferred_element_type=jnp.float32).astype(
        jnp.bfloat16
    )
    grad_q, grad_k, grad_v, grad_bias = attention_backward(
        query_rows.reshape(seq_shape),
        key_rows.reshape(seq_shape),
        value_rows.reshape(seq_shape),
        grad_attended.reshape(seq_shape),
        log_sums,
        bias_rows,
        block_rows,
        rel_bias.shape[0],
    )
    grad_q = grad_q.reshape(tok_count, width).astype(jnp.bfloat16)
    grad_k = grad_k.reshape(tok_count, width).astype(jnp.bfloat16)
    grad_v = grad_v.reshape(tok_count, width).astype(jnp.bfloat16)
    grad_query_part = jnp.einsum(
        "td,te->de", normed_attn, grad_q, preferred_element_type=jnp.float32
    )
    grad_key_part = jnp.einsum("td,te->de", normed_attn, grad_k, preferred_element_type=jnp.float32)
    grad_value_part = jnp.einsum(
        "td,te->de", normed_attn, grad_v, preferred_element_type=jnp.float32
    )
    grad_normed_attn = (
        jnp.dot(grad_q, query_w.T, preferred_element_type=jnp.float32)
        + jnp.dot(grad_k, key_w.T, preferred_element_type=jnp.float32)
        + jnp.dot(grad_v, value_w.T, preferred_element_type=jnp.float32)
    )
    grad_norm_attn, grad_gain_attn = norm_backward(
        tokens, inverse_attn, attn_scale, grad_normed_attn
    )
    grad_inputs = grad_mixed + grad_norm_attn
    grad_query, grad_key, grad_value, grad_output, grad_router, gain_attn_grad, gain_ffn_grad = (
        lax.psum_scatter(grad_query_part, ("wide", "narrow"), scatter_dimension=0, tiled=True),
        lax.psum_scatter(grad_key_part, ("wide", "narrow"), scatter_dimension=0, tiled=True),
        lax.psum_scatter(grad_value_part, ("wide", "narrow"), scatter_dimension=0, tiled=True),
        lax.psum_scatter(grad_output_part, ("wide", "narrow"), scatter_dimension=0, tiled=True),
        lax.psum_scatter(grad_router_part, ("wide", "narrow"), scatter_dimension=0, tiled=True),
        lax.psum_scatter(grad_gain_attn, ("wide", "narrow"), scatter_dimension=0, tiled=True),
        lax.psum_scatter(grad_gain_ffn, ("wide", "narrow"), scatter_dimension=0, tiled=True),
    )
    grad_rel_bias = lax.psum(jnp.sum(grad_bias, axis=0).T, ("wide", "narrow"))
    return (
        result,
        grad_inputs,
        gain_attn_grad,
        grad_query,
        grad_key,
        grad_value,
        grad_output,
        grad_rel_bias,
        gain_ffn_grad,
        grad_router,
        grad_expert_in,
        grad_expert_out,
    )


def solution(mesh):
    return jax.shard_map(
        shards,
        mesh=mesh,
        in_specs=(
            P(("wide", "narrow"), None),
            P(("wide", "narrow")),
            P(("wide", "narrow"), None),
            P(("wide", "narrow"), None),
            P(("wide", "narrow"), None),
            P(("wide", "narrow"), None),
            P(),
            P(("wide", "narrow")),
            P(("wide", "narrow"), None),
            P("wide", None, "narrow"),
            P("wide", "narrow", None),
            P(("wide", "narrow"), None),
            P(("wide", "narrow")),
            P(("wide", "narrow"), None),
        ),
        out_specs=(
            P(("wide", "narrow"), None),
            P(("wide", "narrow"), None),
            P(("wide", "narrow")),
            P(("wide", "narrow"), None),
            P(("wide", "narrow"), None),
            P(("wide", "narrow"), None),
            P(("wide", "narrow"), None),
            P(),
            P(("wide", "narrow")),
            P(("wide", "narrow"), None),
            P("wide", None, "narrow"),
            P("wide", "narrow", None),
        ),
        check_vma=False,
    )
```

profile of v0, /device:TPU:0, one launch (start us, length us, event | category | flops | bytes accessed | tf_op | source)
XLA Modules:
  0.0 1986.5 jit_solution(1597662001279030171)
XLA Ops:
  18.5 42.5 %all-reduce.10 = (bf16[768]{0:T(1024)(128)(2,1)S(1)}, bf16[768]{0:T(1024)(128)(2,1)S(1)}) all-reduce(bf16[768]{0:T(1024)(128)(2,1)S(1)} %dynamic-update-slice, bf16[768]{0:T(1024)(128)(2,1)S(1)} %dynamic-update-slice.1), channel_id=1, replica_groups=mesh['wide'=8,'narrow'=4] {'wide','narrow'}, use_global_device_ids=true, to_apply=%add.4 | all-reduce | flops 1536 | bytes 6144
  63.9 860.0 %gather_fusion = f32[262144,12]{1,0:T(8,128)} fusion(f32[12,1023]{0,1:T(8,128)S(1)} %copy.73, s32[262144]{0:T(1024)S(1)} %broadcast_clamp_fusion), kind=kCustom, calls=%fused_computation.clone | custom fusion | bytes 26214400 | tf_op jit(solution)/shard_map/while/body/eval_jaxpr/jit(_take)/gather | solution.py:77
  923.9 73.5 %copy.75 = f32[512,512,12]{0,1,2:T(8,128)} copy(f32[512,512,12]{2,1,0:T(8,128)} %bitcast.4) | data formatting | bytes 25165824 | tf_op jit(solution)/shard_map/while/body/eval_jaxpr/jit(_take)/gather | solution.py:77
  1007.2 6.1 fusion.97
  1024.2 5.2 gather_fusion.1
  1031.1 40.6 %all_to_all.20 = bf16[8,128,768]{2,1,0:T(8,128)(2,1)} all-to-all(bf16[8,128,768]{2,1,0:T(8,128)(2,1)S(1)} %bitcast.146), channel_id=1, replica_groups=mesh['wide'=8,'narrow'=4] {'wide'}, dimensions={0} | all-to-all | bytes 3145728 | tf_op jit(solution)/shard_map/all_to_all | solution.py:222
  1072.1 44.7 %all-gather.15.cloned.1.call-done = bf16[32,128,768]{2,1,0:T(8,128)(2,1)} async-done(((bf16[8,128,768]{2,1,0:T(8,128)(2,1)}), bf16[32,128,768]{2,1,0:T(8,128)(2,1)}) %all-gather.15.cloned.1.call-update) | async-done | bytes 6291472 | tf_op jit(solution)/shard_map/all_gather | solution.py:229
  1116.8 11.4 fusion.25
  1128.2 8.9 convert_bitcast_fusion.1
  1140.4 58.5 %reduce-scatter.10.cloned.1.call-done = bf16[8,128,768]{2,1,0:T(8,128)(2,1)} async-done(((bf16[32,128,768]{2,1,0:T(8,128)(2,1)}), bf16[8,128,768]{2,1,0:T(8,128)(2,1)}) %reduce-scatter.10.cloned.1.call-update) | async-done | bytes 1572880 | tf_op jit(solution)/shard_map/reduce_scatter | solution.py:233
  1198.9 5.5 all-to-all-start.1
  1204.4 61.7 %all_gather.33 = bf16[768,32]{1,0:T(8,128)(2,1)S(1)} all-gather(bf16[24,32]{1,0:T(8,128)(2,1)S(1)} %copy-done.31), channel_id=1, replica_groups=mesh['wide'=8,'narrow'=4] {'wide','narrow'}, dimensions={0}, use_global_device_ids=true | all-gather | bytes 50688 | tf_op jit(solution)/shard_map/all_gather | solution.py:167
  1274.1 5.2 gather_fusion.3
  1281.0 41.5 %all_to_all.21 = bf16[8,128,768]{2,1,0:T(8,128)(2,1)} all-to-all(bf16[8,128,768]{2,1,0:T(8,128)(2,1)S(1)} %bitcast.145), channel_id=1, replica_groups=mesh['wide'=8,'narrow'=4] {'wide'}, dimensions={0} | all-to-all | bytes 3145728 | tf_op jit(solution)/shard_map/all_to_all | solution.py:259
  1322.6 44.6 %all-gather.17.cloned.1.call-done = bf16[32,128,768]{2,1,0:T(8,128)(2,1)} async-done(((bf16[8,128,768]{2,1,0:T(8,128)(2,1)}), bf16[32,128,768]{2,1,0:T(8,128)(2,1)}) %all-gather.17.cloned.1.call-update) | async-done | bytes 6291472 | tf_op jit(solution)/shard_map/all_gather | solution.py:266
  1367.2 17.4 fusion.16
  1384.6 8.4 convert_bitcast_fusion
  1396.3 58.5 %reduce-scatter.12.cloned.1.call-done = bf16[8,128,768]{2,1,0:T(8,128)(2,1)} async-done(((bf16[32,128,768]{2,1,0:T(8,128)(2,1)}), bf16[8,128,768]{2,1,0:T(8,128)(2,1)}) %reduce-scatter.12.cloned.1.call-update) | async-done | bytes 1572880 | tf_op jit(solution)/shard_map/reduce_scatter | solution.py:282
  1454.8 5.5 all-to-all-start.3
  1461.8 35.5 %all-to-all-done.3 = bf16[8,128,768]{2,1,0:T(8,128)(2,1)S(1)} async-done(((bf16[8,128,768]{2,1,0:T(8,128)(2,1)}), bf16[8,128,768]{2,1,0:T(8,128)(2,1)S(1)}, u32[]{:S(2)}, u32[]{:S(2)}) %all-to-all-start.3) | async-done | bytes 1572896 | tf_op jit(solution)/shard_map/all_to_all | solution.py:290
  1509.9 10.7 multiply_reduce_fusion
  1522.8 6.9 multiply_convert_fusion
  1535.8 5.1 multiply_convert_fusion.1
  1544.2 6.7 fusion.68
  1554.6 13.8 fusion.47
  1570.7 11.3 fusion.50
  1582.0 14.8 copy.86
  1608.8 37.7 %all-reduce.9 = (f32[768]{0:T(1024)S(1)}, f32[32,12]{0,1:T(8,128)}, f32[768]{0:T(1024)S(1)}) all-reduce(f32[768]{0:T(1024)S(1)} %get-tuple-element.67, f32[32,12]{0,1:T(8,128)S(1)} %fusion.72, f32[768]{0:T(1024)S(1)} %copy-done.26), channel_id=4, replica_groups=mesh['wide'=8,'narrow'=4] {'wide','narrow'}, use_global_device_ids=true, to_apply=%region_18.22.clone | all-reduce | flops 1920 | bytes 15360
  1650.8 16.2 reduce-scatter.14.cloned.1.call-done
  1667.0 104.0 %reduce-scatter.16.cloned.1.call-done = f32[24,768]{1,0:T(8,128)} async-done(((f32[768,768]{1,0:T(8,128)}), f32[24,768]{1,0:T(8,128)}) %reduce-scatter.16.cloned.1.call-update) | async-done | bytes 73744 | tf_op jit(solution)/shard_map/reduce_scatter | solution.py:336
  1771.0 104.6 %reduce-scatter.18.cloned.1.call-done = f32[24,768]{1,0:T(8,128)} async-done(((f32[768,768]{1,0:T(8,128)}), f32[24,768]{1,0:T(8,128)}) %reduce-scatter.18.cloned.1.call-update) | async-done | bytes 73744 | tf_op jit(solution)/shard_map/reduce_scatter | solution.py:337
  1875.6 103.9 %reduce-scatter.20.cloned.1.call-done = f32[24,768]{1,0:T(8,128)} async-done(((f32[768,768]{1,0:T(8,128)}), f32[24,768]{1,0:T(8,128)}) %reduce-scatter.20.cloned.1.call-update) | async-done | bytes 73744 | tf_op jit(solution)/shard_map/reduce_scatter | solution.py:338
  (190 shorter events, 99.8 us)
Async XLA Ops:
  7.2 55.2 %copy-start = (f32[32,12]{0,1:T(8,128)S(1)}, f32[32,12]{0,1:T(8,128)}, u32[]{:S(2)}) copy-start(f32[32,12]{0,1:T(8,128)} %param.30) | copy-start | bytes 4612
  7.2 56.6 %copy-start.22 = (s32[262144]{0:T(1024)S(1)}, s32[262144]{0:T(1024)}, u32[]{:S(2)}) copy-start(s32[262144]{0:T(1024)} %constant.176) | copy-start | bytes 3145732
  7.2 990.2 %all-gather.7.cloned.1.call-start = ((), (), s32[]{:S(2)}) async-start(), calls=%async_computation.11 | async-start | bytes 1216512 | tf_op jit(solution)/shard_map/all_gather | solution.py:165
  7.9 991.9 %all-gather.9.cloned.1.call-start = ((), (), s32[]{:S(2)}) async-start(), calls=%async_computation.12 | async-start | bytes 1216512 | tf_op jit(solution)/shard_map/all_gather | solution.py:163
  8.7 993.8 %all-gather.11.cloned.1.call-start = ((), (), s32[]{:S(2)}) async-start(), calls=%async_computation.13 | async-start | bytes 1216512 | tf_op jit(solution)/shard_map/all_gather | solution.py:164
  9.4 1010.9 %all-gather.13.cloned.1.call-start = ((), (), s32[]{:S(2)}) async-start(), calls=%async_computation.14 | async-start | bytes 1216512 | tf_op jit(solution)/shard_map/all_gather | solution.py:166
  10.0 1106.8 %all-gather.15.cloned.1.call-start = ((), (), s32[]{:S(2)}) async-start(), calls=%async_computation.15 | async-start | bytes 7864320 | tf_op jit(solution)/shard_map/all_gather | solution.py:229
  923.9 73.5 %copy-start.4 = (bf16[512,768]{1,0:T(8,128)(2,1)S(1)}, bf16[512,768]{1,0:T(8,128)(2,1)}, u32[]{:S(2)}) copy-start(bf16[512,768]{1,0:T(8,128)(2,1)} %param.24) | copy-start | bytes 2359300
  999.8 15.4 copy-start.17
  1031.1 97.1 %slice-start.3 = ((s8[4718592]{0:T(1024)(128)(4,1)}), s8[524288]{0:T(1024)(128)(4,1)S(1)}, s32[]{:S(2)}) async-start(s8[4718592]{0:T(1024)(128)(4,1)} %bitcast.167), calls=%async_computation.27 | async-start | bytes 1048576
  1071.7 127.2 %reduce-scatter.10.cloned.1.call-start = ((), (), s32[]{:S(2)}) async-start(), calls=%async_computation.16 | async-start | bytes 7864320 | tf_op jit(solution)/shard_map/reduce_scatter | solution.py:233
  1116.8 11.4 slice-start.4
  1140.4 64.1 %copy-start.31 = (bf16[24,32]{1,0:T(8,128)(2,1)S(1)}, bf16[24,32]{1,0:T(8,128)(2,1)}, u32[]{:S(2)}) copy-start(bf16[24,32]{1,0:T(8,128)(2,1)} %param.32) | copy-start | bytes 4612
  1140.4 125.8 %copy-start.25 = (s32[512,1]{0,1:T(1,128)S(1)}, s32[512,1]{0,1:T(1,128)}, u32[]{:S(2)}) copy-start(s32[512,1]{0,1:T(1,128)} %param.35) | copy-start | bytes 6148
  1198.9 67.8 %all-to-all-start.1 = ((bf16[8,128,768]{2,1,0:T(8,128)(2,1)}), bf16[8,128,768]{2,1,0:T(8,128)(2,1)S(1)}, u32[]{:S(2)}, u32[]{:S(2)}) async-start(bf16[8,128,768]{2,1,0:T(8,128)(2,1)} %reduce-scatter.10.cloned.1.call-done), calls=%async_computation.2 | async-start | bytes 3145728 | tf_op jit(solution)/shard_map/all_to_all | solution.py:241
  1204.4 162.8 %all-gather.17.cloned.1.call-start = ((), (), s32[]{:S(2)}) async-start(), calls=%async_computation.17 | async-start | bytes 7864320 | tf_op jit(solution)/shard_map/all_gather | solution.py:266
  1279.4 105.2 %slice-start.5 = ((s8[4718592]{0:T(1024)(128)(4,1)}), s8[524288]{0:T(1024)(128)(4,1)S(1)}, s32[]{:S(2)}) async-start(s8[4718592]{0:T(1024)(128)(4,1)} %bitcast.169), calls=%async_computation.29 | async-start | bytes 1048576
  1322.6 132.3 %reduce-scatter.12.cloned.1.call-start = ((), (), s32[]{:S(2)}) async-start(), calls=%async_computation.18 | async-start | bytes 7864320 | tf_op jit(solution)/shard_map/reduce_scatter | solution.py:282
  1367.2 17.4 slice-start.6
  1454.8 42.5 %all-to-all-start.3 = ((bf16[8,128,768]{2,1,0:T(8,128)(2,1)}), bf16[8,128,768]{2,1,0:T(8,128)(2,1)S(1)}, u32[]{:S(2)}, u32[]{:S(2)}) async-start(bf16[8,128,768]{2,1,0:T(8,128)(2,1)} %reduce-scatter.12.cloned.1.call-done), calls=%async_computation.5 | async-start | bytes 3145728 | tf_op jit(solution)/shard_map/all_to_all | solution.py:290
  1460.3 190.4 %reduce-scatter.22.cloned.1.call-start = ((), (), s32[]{:S(2)}) async-start(), calls=%async_computation.23 | async-start | bytes 405504
  1460.4 39.6 %copy-start.28 = (s32[1024]{0:T(1024)S(1)}, s32[1024]{0:T(1024)}, u32[]{:S(2)}) copy-start(s32[1024]{0:T(1024)} %copy-done.27) | copy-start | bytes 12292
  1461.6 205.4 %reduce-scatter.14.cloned.1.call-start = ((), (), s32[]{:S(2)}) async-start(), calls=%async_computation.19 | async-start | bytes 2433024 | tf_op jit(solution)/shard_map/reduce_scatter | solution.py:335
  1509.9 10.7 slice-start
  1509.9 11.7 slice-start.1
  1509.9 12.9 slice-start.2
  1535.7 235.2 %reduce-scatter.16.cloned.1.call-start = ((), (), s32[]{:S(2)}) async-start(), calls=%async_computation.20 | async-start | bytes 2433024 | tf_op jit(solution)/shard_map/reduce_scatter | solution.py:336
  1544.2 331.4 %reduce-scatter.18.cloned.1.call-start = ((), (), s32[]{:S(2)}) async-start(), calls=%async_computation.21 | async-start | bytes 2433024 | tf_op jit(solution)/shard_map/reduce_scatter | solution.py:337
  1554.3 14.0 copy-start.24
  1554.3 425.2 %reduce-scatter.20.cloned.1.call-start = ((), (), s32[]{:S(2)}) async-start(), calls=%async_computation.22 | async-start | bytes 2433024 | tf_op jit(solution)/shard_map/reduce_scatter | solution.py:338
  1582.0 18.2 copy-start.13
  1647.7 331.9 %copy-start.1 = (f32[32,12]{0,1:T(8,128)S(1)}, f32[32,12]{0,1:T(8,128)}, u32[]{:S(2)}) copy-start(f32[32,12]{0,1:T(8,128)} %param.30) | copy-start | bytes 4612
  (25 other events, 79.2 us)
Sparse Core Ops, SparseCore 0:
  10.9 56.8 all-gather.6
  70.7 53.1 all-gather.8
  126.8 52.9 all-gather.10
  182.6 52.9 all-gather.12
  1071.8 44.9 all-gather.14
  1140.5 58.3 reduce-scatter.9
  1322.7 44.4 all-gather.16
  1396.4 58.3 reduce-scatter.11
  1466.7 95.3 reduce-scatter.21
  1568.6 98.3 reduce-scatter.13
  1672.9 98.0 reduce-scatter.15
  1777.5 98.0 reduce-scatter.17
  1881.5 98.0 reduce-scatter.19
where the time goes:
time: 2000 us; the launch traced here: 1990 us
  local copies, waits for them, and re-layouts  996 us (50%)
  waiting for transfers between devices  573 us (29%)
  blocking collectives  224 us (11%)
  matrix products  141 us (7%)
  other arithmetic  24 us (1%)
    gather x2, local copies, waits for them, and re-layouts, block_scores(): return scores + jnp.take(bias_rows, index, axis=1)  933 us
    reduce_scatter x1, waiting for transfers between devices, shards(): lax.psum_scatter(grad_value_part, ('wide', 'narrow'), scatter_dimension=0...  105 us
    reduce_scatter x1, waiting for transfers between devices, shards(): lax.psum_scatter(grad_key_part, ('wide', 'narrow'), scatter_dimension=0,...  104 us
    reduce_scatter x1, waiting for transfers between devices, shards(): lax.psum_scatter(grad_output_part, ('wide', 'narrow'), scatter_dimension=...  104 us
    unnamed x2, blocking collectives  80.2 us
    all_gather x1, blocking collectives, shards(): lax.all_gather(w_router, ('wide', 'narrow'), axis=0, tiled=True)  61.7 us
    reduce_scatter x1, waiting for transfers between devices, shards(): lax.psum_scatter(jnp.einsum('secf,edf->secd', grad_pre, expert_in, prefer...  58.5 us
    reduce_scatter x1, waiting for transfers between devices, shards(): lax.psum_scatter(jnp.einsum('secf,efd->secd', hidden, expert_out, preferr...  58.5 us
  transfers between devices with their start and end apart: 15, of which 9 were waited for; matrix products, arithmetic and copies ran while one was open for 54% of the time, Pallas kernels for 0%

commit v1 on v0

v1 whole, which is shorter than its diff:
```python
import jax
import jax.numpy as jnp
import numpy as np
from jax import lax
from jax.experimental import pallas as pl
from jax.experimental.pallas import tpu as pltpu
from jax.sharding import PartitionSpec as P

HEADS = 12
SEQ_LEN = 512
BLOCK = 128
EPSILON = 1e-06
HIGHEST = lax.Precision.HIGHEST
ROOT_TWO_PI = 0.7978845608028654
CUBIC = 0.044715
BOTH = ("wide", "narrow")
F32 = jnp.float32
BF16 = jnp.bfloat16


def bucket_of(offsets, bucket_count):
    half_count = bucket_count // 2
    exact_count = half_count // 2
    distance = np.abs(offsets)
    scaled = exact_count + np.floor(
        np.log(np.maximum(distance, 1) / exact_count)
        / np.log(128.0 / exact_count)
        * (half_count - exact_count)
    ).astype(np.int64)
    scaled = np.minimum(scaled, half_count - 1)
    return ((offsets > 0) * half_count + np.where(distance < exact_count, distance, scaled)).astype(
        np.int32
    )


def near_picks(bucket_count, sign):
    offsets = sign * (np.arange(4 * BLOCK) - (2 * BLOCK - 1))
    picks = (bucket_of(offsets, bucket_count)[:, None] == np.arange(bucket_count)[None, :]).astype(
        np.float32
    )
    picks[-1] = 0.0
    return picks


def dot_nn(left, right):
    return lax.dot_general(left, right, (((1,), (0,)), ((), ())), preferred_element_type=F32)


def dot_nt(left, right):
    return lax.dot_general(left, right, (((1,), (1,)), ((), ())), preferred_element_type=F32)


def dot_tn(left, right):
    return lax.dot_general(left, right, (((0,), (0,)), ((), ())), preferred_element_type=F32)


def inverse_rms(values):
    return lax.rsqrt(jnp.mean(values * values, axis=-1, keepdims=True) + EPSILON)


def norm_backward(values, inverse, gain, grad_normed):
    scaled = grad_normed * gain
    grad_gain = jnp.sum(grad_normed * values * inverse, axis=0, keepdims=True)
    inner = jnp.mean(scaled * values, axis=-1, keepdims=True)
    return (inverse * (scaled - values * inverse * inverse * inner), grad_gain)


def softmax_lanes(logits):
    peak = jnp.max(logits, axis=-1, keepdims=True)
    exponent = jnp.exp(logits - peak)
    return exponent / jnp.sum(exponent, axis=-1, keepdims=True)


def toeplitz_near(near_row):
    spread = jnp.broadcast_to(near_row, (BLOCK, 4 * BLOCK))
    return pltpu.roll(spread, 3 * BLOCK + 1, 1, stride=1, stride_axis=0)[:, : 3 * BLOCK]


def bias_rows(near, far_low, far_high, row, blocks):
    pieces = []
    for column in range(blocks):
        distance = column - row
        if distance <= -2:
            pieces.append(jnp.full((BLOCK, BLOCK), far_low, F32))
        elif distance >= 2:
            pieces.append(jnp.full((BLOCK, BLOCK), far_high, F32))
        else:
            pieces.append(near[:, (distance + 1) * BLOCK : (distance + 2) * BLOCK])
    return jnp.concatenate(pieces, axis=1)


def diagonal_sums(near_sum):
    padded = jnp.concatenate([near_sum, jnp.zeros((BLOCK, BLOCK), F32)], axis=1)
    groups = jnp.zeros((8, 4 * BLOCK), F32)
    for at in range(0, BLOCK, 8):
        groups = groups + pltpu.roll(padded[at : at + 8, :], BLOCK - 8 - at, 1)
    sums = groups[7:8, :]
    for at in range(7):
        sums = sums + pltpu.roll(groups[at : at + 1, :], 7 - at, 1)
    return sums


def slot_places(routes_ref, row_ref, limit, experts, slots, count):
    lower = lax.broadcasted_iota(jnp.int32, (count, count), 0)
    upper = lax.broadcasted_iota(jnp.int32, (count, count), 1)
    col = routes_ref[...]
    chosen = lax.broadcasted_iota(jnp.int32, (count, experts), 1) == col
    running = dot_nn((upper <= lower).astype(BF16), chosen.astype(BF16))
    place = jnp.sum(jnp.where(chosen, running, 0.0), axis=1, keepdims=True).astype(jnp.int32) - 1
    slot_col = jnp.where(place < limit, col * slots + place, -1)
    row = row_ref[...]
    chosen_t = lax.broadcasted_iota(jnp.int32, (experts, count), 0) == row
    running_t = dot_nn(chosen_t.astype(BF16), (lower <= upper).astype(BF16))
    place_t = (
        jnp.sum(jnp.where(chosen_t, running_t, 0.0), axis=0, keepdims=True).astype(jnp.int32) - 1
    )
    slot_row = jnp.where(place_t < limit, row * slots + place_t, -1)
    return slot_col, slot_row


def place_kernel(slots, experts, capacity_ref, routes_ref, row_ref, cot_ref, slot_col, slot_row, cot_out):
    count = routes_ref.shape[0]
    limit = capacity_ref[0] * count // experts
    col, row = slot_places(routes_ref, row_ref, limit, experts, slots, count)
    slot_col[...] = col
    slot_row[...] = row
    picks = (lax.broadcasted_iota(jnp.int32, (experts * slots, count), 0) == row).astype(BF16)
    cot_out[...] = dot_nn(picks, cot_ref[...]).astype(BF16)


def forward_kernel(
    rel_ref, x_ref, w_ref, gain_a, gain_f, router_ref, near_ref, slot_row,
    normed_ref, q_ref, k_ref, v_ref, att_ref, lse_ref, mixed_ref, normed_f, sent_ref,
):
    count, width = x_ref.shape
    head_dim = width // HEADS
    blocks = count // BLOCK
    bucket_count = rel_ref.shape[0]
    tokens = x_ref[...].astype(F32)
    normed = (tokens * inverse_rms(tokens) * gain_a[...]).astype(BF16)
    normed_ref[...] = normed
    for out, at in ((q_ref, 0), (k_ref, 1), (v_ref, 2)):
        out[...] = dot_nn(normed, w_ref[:, at * width : (at + 1) * width]).astype(BF16)
    lse_ref[...] = jnp.zeros_like(lse_ref)
    first = lax.broadcasted_iota(jnp.int32, (1, BLOCK), 1) < head_dim
    lanes = lax.broadcasted_iota(jnp.int32, (1, BLOCK), 1)

    def pair(at, carry):
        cols = pl.ds(pl.multiple_of(at * BLOCK, BLOCK), BLOCK)
        k_pair, v_pair = k_ref[:, cols], v_ref[:, cols]
        nears = [toeplitz_near(near_ref[pl.ds(2 * at + half, 1), :]) for half in range(2)]
        for row in range(blocks):
            rows = slice(row * BLOCK, (row + 1) * BLOCK)
            q_rows = q_ref[rows, cols] * jnp.asarray(head_dim**-0.5, BF16)
            found = []
            log_sums = lse_ref[rows, :]
            for half in range(2):
                head = 2 * at + half
                low, high = rel_ref[bucket_count // 2 - 1, head], rel_ref[bucket_count - 1, head]
                mask = first if half == 0 else jnp.logical_not(first)
                scores = dot_nt(jnp.where(mask, q_rows, jnp.zeros_like(q_rows)), k_pair)
                scores = scores + bias_rows(nears[half], low, high, row, blocks)
                peak = jnp.max(scores, axis=-1, keepdims=True)
                exponent = jnp.exp(scores - peak)
                total = jnp.sum(exponent, axis=-1, keepdims=True)
                found.append(dot_nn((exponent * (1.0 / total)).astype(BF16), v_pair))
                log_sums = jnp.where(lanes == head, peak + jnp.log(total), log_sums)
            lse_ref[rows, :] = log_sums
            att_ref[rows, cols] = jnp.where(first, found[0], found[1]).astype(BF16)
        return carry

    lax.fori_loop(0, HEADS // 2, pair, 0)
    mixed = tokens + dot_nn(att_ref[...], w_ref[:, 3 * width : 4 * width])
    mixed_ref[...] = mixed
    normed_2 = (mixed * inverse_rms(mixed) * gain_f[...]).astype(BF16)
    normed_f[...] = normed_2
    total_slots = sent_ref.shape[0]
    picks = (lax.broadcasted_iota(jnp.int32, (total_slots, count), 0) == slot_row[...]).astype(BF16)
    sent_ref[...] = dot_nn(picks, normed_2).astype(BF16)


def expert_kernel(
    first_ref, rows_ref, cot_ref, in_ref, out_ref, router_ref,
    back_ref, grows_ref, gin_ref, gout_ref, hidden_ref, gpre_ref, sg_ref,
):
    sources, _, slots, width = rows_ref.shape
    total = sources * slots
    step = min(256, total)
    expert = first_ref[0] + pl.program_id(0)

    def chunk(at, carry):
        these = pl.ds(pl.multiple_of(at * (step // slots), step // slots), step // slots)
        flat = pl.ds(pl.multiple_of(at * step, step), step)
        rows = rows_ref[these, 0].reshape(step, width)
        probs = softmax_lanes(dot_nn(rows, router_ref[...]))
        here = lax.broadcasted_iota(jnp.int32, probs.shape, 1) == expert
        gate = jnp.sum(jnp.where(here, probs, 0.0), axis=-1, keepdims=True)
        sg = (cot_ref[these, 0].reshape(step, width).astype(F32) * gate).astype(BF16)
        sg_ref[flat, :] = sg
        pre = dot_nn(rows, in_ref[0])
        square = pre * pre
        inner = jnp.tanh(pre * (ROOT_TWO_PI + ROOT_TWO_PI * CUBIC * square))
        half = 0.5 * (1.0 + inner)
        hidden = (pre * half).astype(BF16)
        hidden_ref[flat, :] = hidden
        slope = half + 0.5 * pre * (1.0 - inner * inner) * (
            ROOT_TWO_PI + 3.0 * ROOT_TWO_PI * CUBIC * square
        )
        gpre = (dot_nt(sg, out_ref[0]) * slope).astype(BF16)
        gpre_ref[flat, :] = gpre
        back_ref[these, 0] = dot_nn(hidden, out_ref[0]).astype(BF16).reshape(-1, slots, width)
        grows_ref[these, 0] = dot_nt(gpre, in_ref[0]).astype(BF16).reshape(-1, slots, width)
        return carry

    lax.fori_loop(0, total // step, chunk, 0)
    gout_ref[0] = dot_tn(hidden_ref[...], sg_ref[...])
    gin_ref[0] = dot_tn(rows_ref[:, 0].reshape(total, width), gpre_ref[...])


def backward_kernel(
    rel_ref, x_ref, w_ref, gain_a, gain_f, router_ref, near_ref, slot_col, routes_ref,
    normed_ref, q_ref, k_ref, v_ref, att_ref, lse_ref, mixed_ref, normed_f, cot_ref, outs_ref, grows_ref,
    result_ref, gx_ref, gw_ref, grouter_ref, gnear_ref, gfar_ref, ggain_ref,
    q_t, k_t, normed_t, datt, datt_t, delta, lse_t, gq, gk, gv, gmixed, dst,
):
    count, width = x_ref.shape
    head_dim = width // HEADS
    blocks = count // BLOCK
    bucket_count = rel_ref.shape[0]
    experts = router_ref.shape[1]
    picks = (
        lax.broadcasted_iota(jnp.int32, (count, outs_ref.shape[0]), 1) == slot_col[...]
    ).astype(BF16)
    combined = dot_nn(picks, outs_ref[...])
    mixed = mixed_ref[...]
    cot = cot_ref[...].astype(F32)
    probs = softmax_lanes(dot_nn(normed_f[...], router_ref[...]))
    chosen = lax.broadcasted_iota(jnp.int32, (count, experts), 1) == routes_ref[...]
    gate = jnp.sum(jnp.where(chosen, probs, 0.0), axis=-1, keepdims=True)
    result_ref[...] = (mixed + gate * combined).astype(BF16)
    grad_gate = jnp.sum(cot * combined, axis=-1, keepdims=True)
    grad_logits = (probs * (jnp.where(chosen, grad_gate, 0.0) - gate * grad_gate)).astype(BF16)
    grouter_ref[...] = dot_tn(normed_f[...], grad_logits)
    grad_normed = dot_nt(grad_logits, router_ref[...]) + dot_nn(picks, grows_ref[...])
    grad_norm, ggain_ref[1:2, :] = norm_backward(mixed, inverse_rms(mixed), gain_f[...], grad_normed)
    grad_mixed = cot + grad_norm
    gmixed[...] = grad_mixed
    branch = grad_mixed.astype(BF16)
    gw_ref[:, 3 * width : 4 * width] = dot_tn(att_ref[...], branch).astype(BF16)
    datt[...] = dot_nt(branch, w_ref[:, 3 * width : 4 * width]).astype(BF16)
    datt_t[...] = datt[...].T
    q_t[...] = (q_ref[...] * jnp.asarray(head_dim**-0.5, BF16)).T
    k_t[...] = k_ref[...].T
    normed_t[...] = normed_ref[...].T
    products = datt_t[...].astype(F32) * att_ref[...].T.astype(F32)
    delta[...] = jnp.sum(products.reshape(HEADS, head_dim, count), axis=1)
    lse_t[...] = lse_ref[...].T
    first = lax.broadcasted_iota(jnp.int32, (1, BLOCK), 1) < head_dim

    def pair(at, carry):
        cols = pl.ds(pl.multiple_of(at * BLOCK, BLOCK), BLOCK)
        q_pair, datt_pair = q_ref[:, cols], datt[:, cols]
        gq_parts, gk_parts, gv_parts = [], [], []
        for half in range(2):
            head = 2 * at + half
            low, high = rel_ref[bucket_count // 2 - 1, head], rel_ref[bucket_count - 1, head]
            mask = first if half == 0 else jnp.logical_not(first)
            near = toeplitz_near(near_ref[pl.ds(head, 1), :])
            lse_row, delta_row = lse_t[pl.ds(head, 1), :], delta[pl.ds(head, 1), :]
            near_sum = jnp.zeros((BLOCK, 3 * BLOCK), F32)
            low_sum, high_sum = jnp.zeros((BLOCK, BLOCK), F32), jnp.zeros((BLOCK, BLOCK), F32)
            gk_rows, gv_rows = [], []
            for row in range(blocks):
                rows = slice(row * BLOCK, (row + 1) * BLOCK)
                k_rows, v_rows = k_ref[rows, cols], v_ref[rows, cols]
                zeros = jnp.zeros_like(k_rows)
                scores = dot_nn(jnp.where(mask, k_rows, zeros), q_t[cols, :])
                scores = scores + bias_rows(near, high, low, row, blocks)
                weights = jnp.exp(scores - lse_row)
                grad_weights = dot_nn(jnp.where(mask, v_rows, zeros), datt_t[cols, :])
                grad_scores = weights * (grad_weights - delta_row)
                gv_rows.append(dot_nn(weights.astype(BF16), datt_pair))
                low_bits = grad_scores.astype(BF16)
                dst[rows, :] = low_bits
                gk_rows.append(dot_nn(low_bits, q_pair))
                for column in range(blocks):
                    piece = grad_scores[:, column * BLOCK : (column + 1) * BLOCK]
                    distance = column - row
                    if distance <= -2:
                        high_sum = high_sum + piece
                    elif distance >= 2:
                        low_sum = low_sum + piece
                    else:
                        pads = [jnp.zeros((BLOCK, BLOCK), F32)] * 3
                        pads[distance + 1] = piece
                        near_sum = near_sum + jnp.concatenate(pads, axis=1)
            gq_parts.append(
                dot_nn(k_t[pl.ds(pl.multiple_of(head * head_dim, head_dim), head_dim), :], dst[...])
            )
            gk_parts.append(jnp.concatenate(gk_rows, axis=0))
            gv_parts.append(jnp.concatenate(gv_rows, axis=0))
            gnear_ref[pl.ds(head, 1), :] = diagonal_sums(near_sum)
            gfar_ref[pl.ds(head, 1), :] = jnp.concatenate(
                [jnp.sum(low_sum, axis=0, keepdims=True), jnp.sum(high_sum, axis=0, keepdims=True)], axis=1
            )
        scale = head_dim**-0.5
        gq[:, cols] = (jnp.concatenate(gq_parts, axis=0).T * scale).astype(BF16)
        gk[:, cols] = (jnp.where(first, gk_parts[0], gk_parts[1]) * scale).astype(BF16)
        gv[:, cols] = jnp.where(first, gv_parts[0], gv_parts[1]).astype(BF16)
        return carry

    lax.fori_loop(0, HEADS // 2, pair, 0)
    grad_normed = jnp.zeros((count, width), F32)
    for at, grad in enumerate((gq, gk, gv)):
        gw_ref[:, at * width : (at + 1) * width] = dot_nn(normed_t[...], grad[...]).astype(BF16)
        grad_normed = grad_normed + dot_nt(grad[...], w_ref[:, at * width : (at + 1) * width])
    tokens = x_ref[...].astype(F32)
    grad_norm, ggain_ref[0:1, :] = norm_backward(tokens, inverse_rms(tokens), gain_a[...], grad_normed)
    gx_ref[...] = gmixed[...] + grad_norm


def in_vmem(count):
    return [pl.BlockSpec(memory_space=pltpu.VMEM)] * count


def shards(
    inputs, gain_attn, w_query, w_key, w_value, w_output, rel_bias, gain_ffn, w_router,
    expert_in, expert_out, routes, capacity, cotangent,
):
    count, width = inputs.shape
    experts = w_router.shape[1]
    local, _, hidden_width = expert_in.shape
    wide, narrow = lax.axis_size("wide"), lax.axis_size("narrow")
    slots = 2 * count // experts
    total = experts * slots
    bucket_count = rel_bias.shape[0]
    params = pltpu.CompilerParams(vmem_limit_bytes=60 << 20)
    smem = pl.BlockSpec(memory_space=pltpu.SMEM)

    packed = jnp.concatenate([w_query, w_key, w_value, w_output], axis=1)
    weights = lax.all_gather(packed, BOTH, axis=0, tiled=True)
    small = lax.all_gather(
        jnp.concatenate([w_router, gain_attn[:, None], gain_ffn[:, None]], axis=1), BOTH, axis=0, tiled=True
    )
    router = small[:, :experts]
    gain_a = small[:, experts].astype(F32)[None, :]
    gain_f = small[:, experts + 1].astype(F32)[None, :]
    near = jnp.dot(near_picks(bucket_count, 1), rel_bias, precision=HIGHEST).T
    near_back = jnp.dot(near_picks(bucket_count, -1), rel_bias, precision=HIGHEST).T

    slot_col, slot_row, cot_sent = pl.pallas_call(
        lambda *refs: place_kernel(slots, experts, *refs),
        out_shape=(
            jax.ShapeDtypeStruct((count, 1), jnp.int32),
            jax.ShapeDtypeStruct((1, count), jnp.int32),
            jax.ShapeDtypeStruct((total, width), BF16),
        ),
        in_specs=[smem] + in_vmem(3),
        out_specs=tuple(in_vmem(3)),
        compiler_params=params,
        name="places",
    )(capacity, routes, routes.reshape(1, count), cotangent)

    def spread(rows):
        taken = lax.all_to_all(
            rows.reshape(wide, local * slots, width), "wide", split_axis=0, concat_axis=0, tiled=True
        )
        held = lax.all_gather(taken, "narrow", axis=0, tiled=True)
        return held.reshape(wide * narrow, local, slots, width)

    def collect(rows):
        own = lax.psum_scatter(
            rows.reshape(wide * narrow, local * slots, width), "narrow", scatter_dimension=0, tiled=True
        )
        back = lax.all_to_all(own, "wide", split_axis=0, concat_axis=0, tiled=True)
        return back.reshape(total, width)

    cot_all = spread(cot_sent)

    rows_t = lambda dtype, cols=width: jax.ShapeDtypeStruct((count, cols), dtype)
    normed, q, k, v, att, lse, mixed, normed_f, sent = pl.pallas_call(
        forward_kernel,
        out_shape=(
            rows_t(BF16), rows_t(BF16), rows_t(BF16), rows_t(BF16), rows_t(BF16), rows_t(F32, BLOCK),
            rows_t(F32), rows_t(BF16), jax.ShapeDtypeStruct((total, width), BF16),
        ),
        in_specs=[smem] + in_vmem(7),
        out_specs=tuple(in_vmem(9)),
        compiler_params=params,
        name="forward",
    )(rel_bias, inputs, weights, gain_a, gain_f, router, near, slot_row)

    rows_all = spread(sent)
    sources = wide * narrow
    block = pl.BlockSpec((sources, 1, slots, width), lambda e: (0, e, 0, 0))
    w_in_spec = pl.BlockSpec((1, width, hidden_width), lambda e: (e, 0, 0))
    w_out_spec = pl.BlockSpec((1, hidden_width, width), lambda e: (e, 0, 0))
    first_expert = (lax.axis_index("wide") * local).astype(jnp.int32)[None]
    back, grows, gin, gout = pl.pallas_call(
        expert_kernel,
        grid=(local,),
        out_shape=(
            jax.ShapeDtypeStruct(rows_all.shape, BF16),
            jax.ShapeDtypeStruct(rows_all.shape, BF16),
            jax.ShapeDtypeStruct(expert_in.shape, F32),
            jax.ShapeDtypeStruct(expert_out.shape, F32),
        ),
        in_specs=[
            smem, block, block, w_in_spec, w_out_spec, pl.BlockSpec((width, experts), lambda e: (0, 0)),
        ],
        out_specs=(block, block, w_in_spec, w_out_spec),
        scratch_shapes=[
            pltpu.VMEM((sources * slots, hidden_width), BF16),
            pltpu.VMEM((sources * slots, hidden_width), BF16),
            pltpu.VMEM((sources * slots, width), BF16),
        ],
        compiler_params=params,
        name="experts",
    )(first_expert, rows_all, cot_all, expert_in, expert_out, router)
    outs_back = collect(back)
    grows_back = collect(grows)

    wide_t = lambda dtype: pltpu.VMEM((width, count), dtype)
    tall = lambda dtype: pltpu.VMEM((count, width), dtype)
    result, grad_inputs, gw, grouter, gnear, gfar, ggain = pl.pallas_call(
        backward_kernel,
        out_shape=(
            rows_t(BF16), rows_t(F32), jax.ShapeDtypeStruct((width, 4 * width), BF16),
            jax.ShapeDtypeStruct((width, experts), F32), jax.ShapeDtypeStruct((HEADS, 4 * BLOCK), F32),
            jax.ShapeDtypeStruct((HEADS, 2 * BLOCK), F32), jax.ShapeDtypeStruct((2, width), F32),
        ),
        in_specs=[smem] + in_vmem(19),
        out_specs=tuple(in_vmem(7)),
        scratch_shapes=[
            wide_t(BF16), wide_t(BF16), wide_t(BF16), tall(BF16), wide_t(BF16),
            pltpu.VMEM((HEADS, count), F32), pltpu.VMEM((BLOCK, count), F32),
            tall(BF16), tall(BF16), tall(BF16), tall(F32), pltpu.VMEM((count, count), BF16),
        ],
        compiler_params=params,
        name="backward",
    )(
        rel_bias, inputs, weights, gain_a, gain_f, router, near_back, slot_col, routes,
        normed, q, k, v, att, lse, mixed, normed_f, cotangent, outs_back, grows_back,
    )

    gw = lax.psum_scatter(gw, BOTH, scatter_dimension=0, tiled=True).astype(F32)
    grad_query, grad_key, grad_value, grad_output = (gw[:, i * width : (i + 1) * width] for i in range(4))
    gsmall = lax.psum_scatter(
        jnp.concatenate([grouter, ggain.T], axis=1), BOTH, scatter_dimension=0, tiled=True
    )
    grad_rel = jnp.dot(near_picks(bucket_count, -1).T, gnear.T, precision=HIGHEST)
    low, high = jnp.sum(gfar[:, :BLOCK], axis=1), jnp.sum(gfar[:, BLOCK:], axis=1)
    grad_rel = grad_rel.at[bucket_count // 2 - 1].add(low).at[bucket_count - 1].add(high)
    grad_rel = lax.psum(grad_rel, BOTH)
    return (
        result, grad_inputs, gsmall[:, experts], grad_query, grad_key, grad_value, grad_output,
        grad_rel, gsmall[:, experts + 1], gsmall[:, :experts], gin, gout,
    )


def solution(mesh):
    return jax.shard_map(
        shards,
        mesh=mesh,
        in_specs=(
            P(BOTH, None),
            P(BOTH),
            P(BOTH, None),
            P(BOTH, None),
            P(BOTH, None),
            P(BOTH, None),
            P(),
            P(BOTH),
            P(BOTH, None),
            P("wide", None, "narrow"),
            P("wide", "narrow", None),
            P(BOTH, None),
            P(BOTH),
            P(BOTH, None),
        ),
        out_specs=(
            P(BOTH, None),
            P(BOTH, None),
            P(BOTH),
            P(BOTH, None),
            P(BOTH, None),
            P(BOTH, None),
            P(BOTH, None),
            P(),
            P(BOTH),
            P(BOTH, None),
            P("wide", None, "narrow"),
            P("wide", "narrow", None),
        ),
        check_vma=False,
    )
```

time: 2000 us -> 713 us (0.36)
  local copies, waits for them, and re-layouts: 996 us -> 11.8 us
  waiting for transfers between devices: 573 us -> 391 us
  matrix products: 141 us -> 2.09 us
  Pallas kernels: 0 us -> 104 us
  blocking collectives: 224 us -> 174 us
  other arithmetic: 24 us -> 2.81 us
    gather x6 -> x0, local copies, waits for them, and re-layouts: 949 us -> none  [the longest x2 933 us: block_scores(): return scores + jnp.take(bias_rows, index, axis=1)]
    reduce_scatter x6 -> x3, waiting for transfers between devices: 446 us -> 223 us  [the longest x2 113 us: collect(): lax.psum_scatter(rows.reshape(wide * narrow, local * slots, width), 'narr...]
    dot_general x29 -> x3, matrix products: 141 us -> 2.09 us  [the longest x1 0.97 us: shards(): jnp.dot(near_picks(bucket_count, -1), rel_bias, precision=HIGHEST)]
    pallas_call x0 -> x4, Pallas kernels: none -> 104 us  [the longest x1 43.5 us: shards(): pl.pallas_call(expert_kernel, grid=(local,), out_shape=(jax.ShapeDtypeStr...]
    unnamed x14 -> x8, waiting for transfers between devices: 2.73 us -> 87.9 us
    unnamed x2 -> x0, blocking collectives: 80.2 us -> none
    all_gather x6 -> x3, waiting for transfers between devices: 89.4 us -> 44.6 us  [the longest x2 44.6 us: spread(): held = lax.all_gather(taken, 'narrow', axis=0, tiled=True)]
    psum x0 -> x1, blocking collectives: none -> 37.6 us  [shards(): grad_rel = lax.psum(grad_rel, BOTH)]
  transfers between devices with their start and end apart: 15 -> 9, of which waited for: 9 -> 6; matrix products, arithmetic and copies ran while one was open for 54% -> 1% of each run, Pallas kernels for 0% -> 4%
where the time goes in v1:
time: 713 us; the launch traced here: 712 us
  waiting for transfers between devices  391 us (55%)
  blocking collectives  174 us (24%)
  Pallas kernels  104 us (15%)
  between operations  15 us (2%)
  local copies, waits for them, and re-layouts  11.8 us (2%)
  starting transfers between devices  11.3 us (2%)
    reduce_scatter x2, waiting for transfers between devices, collect(): lax.psum_scatter(rows.reshape(wide * narrow, local * slots, width), 'narr...  113 us
    reduce_scatter x1, waiting for transfers between devices, shards(): gw = lax.psum_scatter(gw, BOTH, scatter_dimension=0, tiled=True).astype(F32)  110 us
    all_to_all x2, blocking collectives, spread(): lax.all_to_all(rows.reshape(wide, local * slots, width), 'wide', split_ax...  95.9 us
    unnamed x8, waiting for transfers between devices  87.9 us
    all_gather x2, waiting for transfers between devices, spread(): held = lax.all_gather(taken, 'narrow', axis=0, tiled=True)  44.6 us
    pallas_call x1, Pallas kernels, shards(): pl.pallas_call(expert_kernel, grid=(local,), out_shape=(jax.ShapeDtypeStr...  43.5 us
    all_gather x1, blocking collectives, shards(): lax.all_gather(jnp.concatenate([w_router, gain_attn[:, None], gain_ffn[:,...  40.6 us
    psum x1, blocking collectives, shards(): grad_rel = lax.psum(grad_rel, BOTH)  37.6 us
  transfers between devices with their start and end apart: 9, of which 6 were waited for; matrix products, arithmetic and copies ran while one was open for 1% of the time, Pallas kernels for 4%

profile of v1, /device:TPU:0, one launch (start us, length us, event | category | flops | bytes accessed | tf_op | source)
XLA Modules:
  0.0 712.4 jit_solution(10296041357453341672)
XLA Ops:
  7.3 1.5 pad_maximum_fusion
  8.9 1.5 copy.62.refs_1_.routes_ref
  11.1 3.7 places.1
  14.8 53.9 %all_to_all.20 = bf16[8,128,768]{2,1,0:T(8,128)(2,1)} all-to-all(bf16[8,128,768]{2,1,0:T(8,128)(2,1)} %bitcast.40), channel_id=1, replica_groups=mesh['wide'=8,'narrow'=4] {'wide'}, dimensions={0} | all-to-all | bytes 3145728 | tf_op jit(solution)/shard_map/all_to_all | solution.py:365
  69.0 40.6 %all_gather.13 = bf16[768,34]{1,0:T(8,128)(2,1)S(1)} all-gather(bf16[24,34]{1,0:T(8,128)(2,1)S(1)} %pad_maximum_fusion.2), channel_id=1, replica_groups=mesh['wide'=8,'narrow'=4] {'wide','narrow'}, dimensions={0}, use_global_device_ids=true | all-gather | bytes 53856 | tf_op jit(solution)/shard_map/all_gather | solution.py:342
  110.0 0.6 reshape.150.gain_a
  110.6 0.6 reshape.151.gain_f
  111.1 0.7 copy.64.rel_ref
  111.8 1.0 convolution_bitcast_fusion.near_ref
  112.8 25.9 %forward.1 = (bf16[512,768]{1,0:T(8,128)(2,1)}, bf16[512,768]{1,0:T(8,128)(2,1)}, bf16[512,768]{1,0:T(8,128)(2,1)}, bf16[512,768]{1,0:T(8,128)(2,1)}, bf16[512,7...) custom-call(f32[32,12]{1,0:T(8,128)} %copy.64.rel_ref, ...), custom_call_target="tpu_custom_call" | custom-call | tf_op jit(solution)/shard_map/forward/pallas_call | solution.py:381
  138.7 42.0 %all_to_all.21 = bf16[8,128,768]{2,1,0:T(8,128)(2,1)} all-to-all(bf16[8,128,768]{2,1,0:T(8,128)(2,1)} %bitcast.39), channel_id=1, replica_groups=mesh['wide'=8,'narrow'=4] {'wide'}, dimensions={0} | all-to-all | bytes 3145728 | tf_op jit(solution)/shard_map/all_to_all | solution.py:365
  180.8 44.6 %all-gather.6.cloned.1.call-done = bf16[32,128,768]{2,1,0:T(8,128)(2,1)} async-done(((bf16[8,128,768]{2,1,0:T(8,128)(2,1)}), bf16[32,128,768]{2,1,0:T(8,128)(2,1)}) %all-gather.6.cloned.1.call-update) | async-done | bytes 6291472 | tf_op jit(solution)/shard_map/all_gather | solution.py:368
  225.4 43.5 %experts.1 = (bf16[32,4,32,768]{3,2,1,0:T(8,128)(2,1)}, bf16[32,4,32,768]{3,2,1,0:T(8,128)(2,1)}, f32[4,768,768]{2,1,0:T(8,128)}, f32[4,768,768]{2,1,0:T(8,128)}) custom-call(s32[1]{0:T(128)} %bitcast.5.first_ref, bf16[32,4,32,768]{3,2,1,0:T(8,128)(2,1)} %bitcast.38, bf16[32,4,32,768]{3,2,1,0:T(8,128)(2,1)} %bitcast.37, bf16[4,768,768]{2,1,0:T(8,128)(2,1)} %in_ref.1, ...), custom_call_target="tpu_custom_call" | custom-call | tf_op jit(solution)/shard_map/experts/pallas_call | solution.py:399
  269.0 0.5 reduce-scatter.6.cloned.1.call-update
  269.5 57.9 %reduce-scatter.4.cloned.1.call-done = bf16[8,128,768]{2,1,0:T(8,128)(2,1)} async-done(((bf16[32,128,768]{2,1,0:T(8,128)(2,1)}), bf16[8,128,768]{2,1,0:T(8,128)(2,1)}) %reduce-scatter.4.cloned.1.call-update) | async-done | bytes 1572880 | tf_op jit(solution)/shard_map/reduce_scatter | solution.py:372
  327.4 5.5 all-to-all-start.2
  332.9 55.4 %reduce-scatter.6.cloned.1.call-done = bf16[8,128,768]{2,1,0:T(8,128)(2,1)} async-done(((bf16[32,128,768]{2,1,0:T(8,128)(2,1)}), bf16[8,128,768]{2,1,0:T(8,128)(2,1)}) %reduce-scatter.6.cloned.1.call-update) | async-done | bytes 1572880 | tf_op jit(solution)/shard_map/reduce_scatter | solution.py:372
  388.4 5.5 all-to-all-start.3
  393.9 1.0 convolution_bitcast_fusion.1.near_ref
  394.9 36.0 %all-to-all-done.3 = bf16[8,128,768]{2,1,0:T(8,128)(2,1)S(1)} async-done(((bf16[8,128,768]{2,1,0:T(8,128)(2,1)}), bf16[8,128,768]{2,1,0:T(8,128)(2,1)S(1)}, u32[]{:S(2)}, u32[]{:S(2)}) %all-to-all-start.3) | async-done | bytes 1572896 | tf_op jit(solution)/shard_map/all_to_all | solution.py:375
  430.9 1.1 copy-done.2
  432.0 30.9 %backward.1 = (bf16[512,768]{1,0:T(8,128)(2,1)}, f32[512,768]{1,0:T(8,128)}, bf16[768,3072]{1,0:T(8,128)(2,1)}, f32[768,32]{1,0:T(8,128)}, f32[12,512]{1,0:T(8,1...) custom-call(f32[32,12]{1,0:T(8,128)} %copy.64.rel_ref, bf16[512,768]{1,0:T(8,128)(2,1)} %x_ref.3, ...), custom_call_target="tpu_custom_call" | custom-call | tf_op jit(solution)/shard_map/backward/pallas_call | solution.py:425
  463.0 1.2 copy.66
  464.1 0.7 pad_maximum_fusion.1
  464.8 0.9 copy.67
  465.8 0.7 reduce-scatter.8.cloned.1.call-update
  467.5 37.6 %psum.7 = f32[32,12]{0,1:T(8,128)} all-reduce(f32[32,12]{0,1:T(8,128)S(1)} %scatter-add.9), channel_id=1, replica_groups=mesh['wide'=8,'narrow'=4] {'wide','narrow'}, use_global_device_ids=true, to_apply=%region_6.0 | all-reduce | flops 384 | bytes 3072 | tf_op jit(solution)/shard_map/psum | solution.py:454
  505.1 86.5 %all-reduce.3.cloned.1.call-done = f32[768,34]{1,0:T(8,128)} async-done(((f32[768,34]{1,0:T(8,128)}), f32[768,34]{1,0:T(8,128)}) %all-reduce.3.cloned.1.call-update) | async-done | bytes 104464
  591.6 1.5 dynamic-slice_reduce_fusion
  593.1 1.3 constant_dynamic-slice_fusion
  594.4 109.6 %reduce-scatter.8.cloned.1.call-done = bf16[24,3072]{1,0:T(8,128)(2,1)} async-done(((bf16[768,3072]{1,0:T(8,128)(2,1)}), bf16[24,3072]{1,0:T(8,128)(2,1)}) %reduce-scatter.8.cloned.1.call-update) | async-done | bytes 147472 | tf_op jit(solution)/shard_map/reduce_scatter | solution.py:446
  704.0 1.5 fusion
  (51 shorter events, 1.9 us)
Async XLA Ops:
  7.2 104.7 %copy-start.4 = (f32[512,32]{1,0:T(8,128)S(1)}, f32[512,32]{1,0:T(8,128)}, u32[]{:S(2)}) copy-start(f32[512,32]{1,0:T(8,128)} %constant.73.clone) | copy-start | bytes 196612
  7.2 61.5 %copy-start.10 = (bf16[24]{0:T(256)(128)(2,1)S(1)}, bf16[24]{0:T(256)(128)(2,1)}, u32[]{:S(2)}) copy-start(bf16[24]{0:T(256)(128)(2,1)} %param.22) | copy-start | bytes 148
  7.2 61.6 %copy-start.11 = (bf16[24]{0:T(256)(128)(2,1)S(1)}, bf16[24]{0:T(256)(128)(2,1)}, u32[]{:S(2)}) copy-start(bf16[24]{0:T(256)(128)(2,1)} %param.28) | copy-start | bytes 148
  7.2 61.7 %copy-start.9 = (bf16[24,32]{1,0:T(8,128)(2,1)S(1)}, bf16[24,32]{1,0:T(8,128)(2,1)}, u32[]{:S(2)}) copy-start(bf16[24,32]{1,0:T(8,128)(2,1)} %param.29) | copy-start | bytes 4612
  7.2 103.9 %copy-start.5 = (f32[32,12]{0,1:T(8,128)S(1)}, f32[32,12]{0,1:T(8,128)}, u32[]{:S(2)}) copy-start(f32[32,12]{0,1:T(8,128)} %param.27) | copy-start | bytes 4612
  7.2 105.6 %all-gather.4.cloned.1.call-start = ((), (), s32[]{:S(2)}) async-start(), calls=%async_computation.7 | async-start | bytes 4866048 | tf_op jit(solution)/shard_map/all_gather | solution.py:341
  8.8 171.9 %all-gather.8.cloned.1.call-start = ((), (), s32[]{:S(2)}) async-start(), calls=%async_computation.9 | async-start | bytes 7864320 | tf_op jit(solution)/shard_map/all_gather | solution.py:368
  68.7 156.7 %all-gather.6.cloned.1.call-start = ((), (), s32[]{:S(2)}) async-start(), calls=%async_computation.8 | async-start | bytes 7864320 | tf_op jit(solution)/shard_map/all_gather | solution.py:368
  109.7 3.1 copy-start
  180.7 146.7 %reduce-scatter.4.cloned.1.call-start = ((), (), s32[]{:S(2)}) async-start(), calls=%async_computation.10 | async-start | bytes 7864320 | tf_op jit(solution)/shard_map/reduce_scatter | solution.py:372
  268.9 119.4 %reduce-scatter.6.cloned.1.call-start = ((), (), s32[]{:S(2)}) async-start(), calls=%async_computation.11 | async-start | bytes 7864320 | tf_op jit(solution)/shard_map/reduce_scatter | solution.py:372
  269.5 124.4 %copy-start.3 = (f32[512,32]{1,0:T(8,128)S(1)}, f32[512,32]{1,0:T(8,128)}, u32[]{:S(2)}) copy-start(f32[512,32]{1,0:T(8,128)} %constant.74.clone) | copy-start | bytes 196612
  327.4 60.9 %all-to-all-start.2 = ((bf16[8,128,768]{2,1,0:T(8,128)(2,1)}), bf16[8,128,768]{2,1,0:T(8,128)(2,1)S(1)}, u32[]{:S(2)}, u32[]{:S(2)}) async-start(bf16[8,128,768]{2,1,0:T(8,128)(2,1)} %reduce-scatter.4.cloned.1.call-done), calls=%async_computation.3 | async-start | bytes 3145728 | tf_op jit(solution)/shard_map/all_to_all | solution.py:375
  388.4 42.5 %copy-start.1 = (bf16[8,128,768]{2,1,0:T(8,128)(2,1)}, bf16[8,128,768]{2,1,0:T(8,128)(2,1)S(1)}, u32[]{:S(2)}) copy-start(bf16[8,128,768]{2,1,0:T(8,128)(2,1)S(1)} %all-to-all-done.2) | copy-start | bytes 4718596
  388.4 42.5 %all-to-all-start.3 = ((bf16[8,128,768]{2,1,0:T(8,128)(2,1)}), bf16[8,128,768]{2,1,0:T(8,128)(2,1)S(1)}, u32[]{:S(2)}, u32[]{:S(2)}) async-start(bf16[8,128,768]{2,1,0:T(8,128)(2,1)} %reduce-scatter.6.cloned.1.call-done), calls=%async_computation.5 | async-start | bytes 3145728 | tf_op jit(solution)/shard_map/all_to_all | solution.py:375
  393.9 197.7 %all-reduce.3.cloned.1.call-start = ((), (), s32[]{:S(2)}) async-start(), calls=%async_computation.13 | async-start | bytes 786432
  430.9 1.1 copy-start.2
  462.9 3.6 copy-start.6
  462.9 3.6 copy-start.7
  462.9 4.0 copy-start.8
  465.8 238.2 %reduce-scatter.8.cloned.1.call-start = ((), (), s32[]{:S(2)}) async-start(), calls=%async_computation.12 | async-start | bytes 4866048 | tf_op jit(solution)/shard_map/reduce_scatter | solution.py:446
Sparse Core Ops, SparseCore 0:
  11.5 74.6 all-gather.3
  87.8 45.6 all-gather.7
  180.8 44.4 all-gather.5
  269.0 58.3 reduce-scatter.3
  330.0 58.3 reduce-scatter.5
  465.9 125.6 all-reduce.2
  598.0 105.9 reduce-scatter.7

commit v2 on v1

--- a/solution.py
+++ b/solution.py
@@ -217,9 +217,356 @@
     gin_ref[0] = dot_tn(rows_ref[:, 0].reshape(total, width), gpre_ref[...])
 
 
+def remote(source, target, send, receive, device):
+    return pltpu.make_async_remote_copy(
+        src_ref=source,
+        dst_ref=target,
+        send_sem=send,
+        recv_sem=receive,
+        device_id=device,
+        device_id_type=pl.DeviceIdType.MESH,
+    )
+
+
+def greet(devices):
+    barrier = pltpu.get_barrier_semaphore()
+    for device in devices:
+        pl.semaphore_signal(barrier, inc=1, device_id=device, device_id_type=pl.DeviceIdType.MESH)
+    pl.semaphore_wait(barrier, len(devices))
+
+
+class Place:
+    def __init__(self, wide):
+        self.wide = wide
+        self.w, self.n = lax.axis_index("wide"), lax.axis_index("narrow")
+        self.x, self.c = self.n // 2, lax.rem(self.n, 2)
+        self.core = (self.w, self.x * 2 + 1 - self.c)
+        self.side = (self.w, (1 - self.x) * 2 + self.c)
+
+    def at(self, step):
+        return lax.rem(self.w + step, self.wide)
+
+    def peer(self, step):
+        return (self.at(step), self.n)
+
+    def partners(self):
+        return [self.peer(k) for k in range(1, self.wide)] + [self.core, self.side]
+
+
+class Spread:
+    def __init__(self, place, sent, held, wide_s, wide_r, side_s, side_r, core_s, core_r):
+        self.place, self.sent, self.held = place, sent, held
+        self.wide_s, self.wide_r, self.side_s, self.side_r = wide_s, wide_r, side_s, side_r
+        self.core_s, self.core_r = core_s, core_r
+
+    def hop(self, e, k):
+        p = self.place
+        return remote(
+            self.sent.at[p.at(k), e], self.held.at[e, p.n, p.w], self.wide_s.at[e, k], self.wide_r.at[e, k], p.peer(k)
+        )
+
+    def start(self, e):
+        for k in range(1, self.place.wide):
+            self.hop(e, k).start()
+
+    def half(self, e, h):
+        p = self.place
+        run = p.wide // 2
+        rows = self.held.at[e, p.n, pl.ds(h * run, run)]
+        return remote(rows, rows, self.side_s.at[e, h], self.side_r.at[e, h], p.side)
+
+    def over(self, e, far):
+        p = self.place
+        m = (1 - p.x) * 2 + p.c if far else p.n
+        return remote(
+            self.held.at[e, m], self.held.at[e, m], self.core_s.at[e, far], self.core_r.at[e, far], p.core
+        )
+
+    def forward(self, e):
+        p = self.place
+        run = p.wide // 2
+        for other in range(2):
+            h = p.w // run
+            h = 1 - h if other else h
+            for k in range(1, p.wide):
+                mine = (p.at(p.wide - k) // run) == h
+
+                @pl.when(mine)
+                def _():
+                    self.hop(e, k).wait_recv()
+
+            self.half(e, h).start()
+        self.over(e, 0).start()
+
+    def pass_on(self, e):
+        for h in range(2):
+            self.half(e, h).wait_recv()
+        self.over(e, 1).start()
+
+    def arrive(self, e):
+        self.over(e, 0).wait_recv()
+        self.over(e, 1).wait_recv()
+
+    def drain(self, e):
+        for k in range(1, self.place.wide):
+            self.hop(e, k).wait_send()
+        for h in range(2):
+            self.half(e, h).wait_send()
+            self.over(e, h).wait_send()
+
+
+def moving_expert_kernel(
+    sent, cot_hbm, in_hbm, out_hbm, router_ref,
+    rows_o, sg_o, hidden_o, gpre_o, outs_o, back_o, gate_o,
+    held, cot, w_in, w_out, sg, hidden, gpre, outs, to_core, from_core, to_side, from_side, near_sum, ready,
+    gate_sum, gate_core, gate_from_core, gate_side, gate_from_side, gate_ready,
+    load_s, store_s, wide_s, wide_r, side_s, side_r, core_s, core_r,
+    rc_s, rc_r, rx_s, rx_r, rw_s, rw_r, gc_s, gc_r, gx_s, gx_r, gw_s, gw_r,
+):
+    wide, local, slots, width = sent.shape
+    narrow = held.shape[1]
+    step = wide * slots
+    p = Place(wide)
+    moves = Spread(p, sent, held, wide_s, wide_r, side_s, side_r, core_s, core_r)
+    greet(p.partners())
+    for e in range(local):
+        moves.start(e)
+
+    def loads(e):
+        return [
+            pltpu.make_async_copy(in_hbm.at[e], w_in.at[e], load_s.at[e, 0]),
+            pltpu.make_async_copy(out_hbm.at[e], w_out.at[e], load_s.at[e, 1]),
+            pltpu.make_async_copy(cot_hbm.at[e], cot.at[e], load_s.at[e, 2]),
+        ]
+
+    def stores(e):
+        b = lax.rem(e, 2)
+        return [
+            pltpu.make_async_copy(held.at[e], rows_o.at[e], store_s.at[e, 0]),
+            pltpu.make_async_copy(sg.at[b], sg_o.at[e], store_s.at[e, 1]),
+            pltpu.make_async_copy(hidden.at[b], hidden_o.at[e], store_s.at[e, 2]),
+            pltpu.make_async_copy(gpre.at[b], gpre_o.at[e], store_s.at[e, 3]),
+            pltpu.make_async_copy(outs.at[b], outs_o.at[e], store_s.at[e, 4]),
+        ]
+
+    for e in range(local):
+        for copy in loads(e):
+            copy.start()
+        held[e, p.n, p.w] = sent[p.w, e]
+    gate_sum[...] = jnp.zeros_like(gate_sum)
+    moves.forward(0)
+    moves.pass_on(0)
+
+    def chunk(e, m):
+        b = lax.rem(e, 2)
+        rows = held[e, m].reshape(step, width)
+        probs = softmax_lanes(dot_nn(rows, router_ref[...]))
+        here = lax.broadcasted_iota(jnp.int32, probs.shape, 1) == p.w * local + e
+        gate = jnp.sum(jnp.where(here, probs, 0.0), axis=-1, keepdims=True)
+        cot_rows = cot[e, m].reshape(step, width).astype(F32)
+        sg_rows = (cot_rows * gate).astype(BF16)
+        sg[b, m] = sg_rows
+        pre = dot_nn(rows, w_in[e])
+        square = pre * pre
+        inner = jnp.tanh(pre * (ROOT_TWO_PI + ROOT_TWO_PI * CUBIC * square))
+        half = 0.5 * (1.0 + inner)
+        hidden_rows = (pre * half).astype(BF16)
+        hidden[b, m] = hidden_rows
+        slope = half + 0.5 * pre * (1.0 - inner * inner) * (
+            ROOT_TWO_PI + 3.0 * ROOT_TWO_PI * CUBIC * square
+        )
+        gpre_rows = (dot_nt(sg_rows, w_out[e]) * slope).astype(BF16)
+        gpre[b, m] = gpre_rows
+        out_rows = dot_nn(hidden_rows, w_out[e])
+        outs[b, m] = out_rows.astype(BF16)
+        gate_rows = jnp.sum(out_rows * cot_rows, axis=-1, keepdims=True)
+        row = lax.broadcasted_iota(jnp.int32, (step, local * slots), 0)
+        lane = lax.broadcasted_iota(jnp.int32, (step, local * slots), 1)
+        spread = jnp.where(lane == e * slots + lax.rem(row, slots), gate_rows, 0.0)
+        gate_sum[m] += jnp.sum(spread.reshape(wide, slots, local * slots), axis=1)
+        return dot_nt(gpre_rows, w_in[e])
+
+    def core_copy(e, far):
+        return remote(to_core.at[e, far], from_core.at[e, far], rc_s.at[e, far], rc_r.at[e, far], p.core)
+
+    def side_copy(e):
+        return remote(to_side.at[e], from_side.at[e], rx_s.at[e], rx_r.at[e], p.side)
+
+    def back_copy(e, k):
+        return remote(ready.at[e, p.at(k)], back_o.at[p.w, e], rw_s.at[e, k], rw_r.at[e, k], p.peer(k))
+
+    def finish(e):
+        side_copy(e).wait_recv()
+        ready[e] = (near_sum[...] + from_side[e].astype(F32)).astype(BF16).reshape(wide, slots, width)
+        for k in range(1, wide):
+            back_copy(e, k).start()
+        back_o[p.w, e] = ready[e, p.w]
+
+    far_x = (1 - p.x) * 2
+
+    def expert(e, carry):
+        for copy in loads(e):
+            copy.wait()
+
+        @pl.when(e >= 2)
+        def _():
+            for copy in stores(e - 2)[1:]:
+                copy.wait()
+
+        moves.arrive(e)
+        to_core[e, 1] = chunk(e, far_x + 1 - p.c).astype(BF16)
+        core_copy(e, 1).start()
+
+        @pl.when(e + 1 < local)
+        def _():
+            moves.forward(e + 1)
+
+        far_part = chunk(e, far_x + p.c)
+        core_copy(e, 1).wait_recv()
+        to_side[e] = (far_part + from_core[e, 1].astype(F32)).astype(BF16)
+        side_copy(e).start()
+
+        @pl.when(e > 0)
+        def _():
+            finish(e - 1)
+
+        to_core[e, 0] = chunk(e, p.x * 2 + 1 - p.c).astype(BF16)
+        core_copy(e, 0).start()
+
+        @pl.when(e + 1 < local)
+        def _():
+            moves.pass_on(e + 1)
+
+        near_part = chunk(e, p.n)
+        core_copy(e, 0).wait_recv()
+        near_sum[...] = near_part + from_core[e, 0].astype(F32)
+        for copy in stores(e):
+            copy.start()
+        return carry
+
+    lax.fori_loop(0, local, expert, 0)
+    gate_core[0] = gate_sum[p.x * 2 + 1 - p.c]
+    gate_core[1] = gate_sum[far_x + 1 - p.c]
+    gates_core = remote(gate_core, gate_from_core, gc_s, gc_r, p.core)
+    gates_core.start()
+    gates_core.wait_recv()
+    gate_side[...] = gate_sum[far_x + p.c] + gate_from_core[1]
+    gates_side = remote(gate_side, gate_from_side, gx_s, gx_r, p.side)
+    gates_side.start()
+    finish(local - 1)
+    gates_side.wait_recv()
+    gates = gate_sum[p.n] + gate_from_core[0] + gate_from_side[...]
+    for v in range(wide):
+        gate_ready[v] = gates[v : v + 1, :]
+    gates_wide = [
+        remote(gate_ready.at[p.at(k)], gate_o.at[p.w], gw_s.at[k], gw_r.at[k], p.peer(k)) for k in range(1, wide)
+    ]
+    for copy in gates_wide:
+        copy.start()
+    gate_o[p.w] = gate_ready[p.w]
+    gates_core.wait_send()
+    gates_side.wait_send()
+
+    def drain(e, carry):
+        moves.drain(e)
+        core_copy(e, 0).wait_send()
+        core_copy(e, 1).wait_send()
+        side_copy(e).wait_send()
+        stores(e)[0].wait()
+
+        @pl.when(e >= local - 2)
+        def _():
+            for copy in stores(e)[1:]:
+                copy.wait()
+
+        for k in range(1, wide):
+            back_copy(e, k).wait()
+        return carry
+
+    lax.fori_loop(0, local, drain, 0)
+    for copy in gates_wide:
+        copy.wait()
+
+
+def weight_grad_kernel(rows_ref, sg_ref, hidden_ref, gpre_ref, gin_ref, gout_ref):
+    gout_ref[0] = dot_tn(hidden_ref[0], sg_ref[0])
+    gin_ref[0] = dot_tn(rows_ref[0], gpre_ref[0])
+
+
+def moving_experts(sent, cot_all, expert_in, expert_out, router, wide, narrow):
+    _, local, slots, width = sent.shape
+    hidden_width = expert_in.shape[2]
+    step = wide * slots
+    sds = jax.ShapeDtypeStruct
+    any_spec, vmem_spec = pl.BlockSpec(memory_space=pl.ANY), pl.BlockSpec(memory_space=pltpu.VMEM)
+    dma = pltpu.SemaphoreType.DMA
+    rows, sg, hidden, gpre, outs, back, gates = pl.pallas_call(
+        moving_expert_kernel,
+        out_shape=(
+            sds((local, narrow, wide, slots, width), BF16),
+            sds((local, narrow, step, width), BF16),
+            sds((local, narrow, step, hidden_width), BF16),
+            sds((local, narrow, step, hidden_width), BF16),
+            sds((local, narrow, step, width), BF16),
+            sds((wide, local, slots, width), BF16),
+            sds((wide, 1, local * slots), F32),
+        ),
+        in_specs=[vmem_spec, any_spec, any_spec, any_spec, vmem_spec],
+        out_specs=(any_spec,) * 5 + (vmem_spec,) * 2,
+        scratch_shapes=[
+            pltpu.VMEM((local, narrow, wide, slots, width), BF16),
+            pltpu.VMEM((local, narrow, wide, slots, width), BF16),
+            pltpu.VMEM(expert_in.shape, BF16),
+            pltpu.VMEM(expert_out.shape, BF16),
+            pltpu.VMEM((2, narrow, step, width), BF16),
+            pltpu.VMEM((2, narrow, step, hidden_width), BF16),
+            pltpu.VMEM((2, narrow, step, hidden_width), BF16),
+            pltpu.VMEM((2, narrow, step, width), BF16),
+            pltpu.VMEM((local, 2, step, width), BF16),
+            pltpu.VMEM((local, 2, step, width), BF16),
+            pltpu.VMEM((local, step, width), BF16),
+            pltpu.VMEM((local, step, width), BF16),
+            pltpu.VMEM((step, width), F32),
+            pltpu.VMEM((local, wide, slots, width), BF16),
+            pltpu.VMEM((narrow, wide, local * slots), F32),
+            pltpu.VMEM((2, wide, local * slots), F32),
+            pltpu.VMEM((2, wide, local * slots), F32),
+            pltpu.VMEM((wide, local * slots), F32),
+            pltpu.VMEM((wide, local * slots), F32),
+            pltpu.VMEM((wide, 1, local * slots), F32),
+            dma((local, 3)), dma((local, 5)), dma((local, wide)), dma((local, wide)),
+            dma((local, 2)), dma((local, 2)), dma((local, 2)), dma((local, 2)),
+            dma((local, 2)), dma((local, 2)), dma((local,)), dma((local,)), dma((local, wide)), dma((local, wide)),
+            dma, dma, dma, dma, dma((wide,)), dma((wide,)),
+        ],
+        compiler_params=pltpu.CompilerParams(
+            collective_id=2, has_side_effects=True, vmem_limit_bytes=62 << 20
+        ),
+        name="experts",
+    )(sent, cot_all, expert_in, expert_out, router)
+    total = narrow * step
+    spec = lambda cols: pl.BlockSpec((1, total, cols), lambda e: (e, 0, 0))
+    gin, gout = pl.pallas_call(
+        weight_grad_kernel,
+        grid=(local,),
+        out_shape=(sds(expert_in.shape, F32), sds(expert_out.shape, F32)),
+        in_specs=[spec(width), spec(width), spec(hidden_width), spec(hidden_width)],
+        out_specs=(
+            pl.BlockSpec((1, width, hidden_width), lambda e: (e, 0, 0)),
+            pl.BlockSpec((1, hidden_width, width), lambda e: (e, 0, 0)),
+        ),
+        compiler_params=pltpu.CompilerParams(vmem_limit_bytes=60 << 20),
+        name="weight_grads",
+    )(
+        rows.reshape(local, total, width), sg.reshape(local, total, width),
+        hidden.reshape(local, total, hidden_width), gpre.reshape(local, total, hidden_width),
+    )
+    return outs, back, gates, gin, gout
+
+
 def backward_kernel(
     rel_ref, x_ref, w_ref, gain_a, gain_f, router_ref, near_ref, slot_col, routes_ref,
-    normed_ref, q_ref, k_ref, v_ref, att_ref, lse_ref, mixed_ref, normed_f, cot_ref, outs_ref, grows_ref,
+    normed_ref, q_ref, k_ref, v_ref, att_ref, lse_ref, mixed_ref, normed_f, cot_ref, outs_ref, grows_ref, gates_ref,
     result_ref, gx_ref, gw_ref, grouter_ref, gnear_ref, gfar_ref, ggain_ref,
     q_t, k_t, normed_t, datt, datt_t, delta, lse_t, gq, gk, gv, gmixed, dst,
 ):
@@ -228,9 +575,8 @@
     blocks = count // BLOCK
     bucket_count = rel_ref.shape[0]
     experts = router_ref.shape[1]
-    picks = (
-        lax.broadcasted_iota(jnp.int32, (count, outs_ref.shape[0]), 1) == slot_col[...]
-    ).astype(BF16)
+    owned = lax.broadcasted_iota(jnp.int32, (count, outs_ref.shape[0]), 1) == slot_col[...]
+    picks = owned.astype(BF16)
     combined = dot_nn(picks, outs_ref[...])
     mixed = mixed_ref[...]
     cot = cot_ref[...].astype(F32)
@@ -238,7 +584,7 @@
     chosen = lax.broadcasted_iota(jnp.int32, (count, experts), 1) == routes_ref[...]
     gate = jnp.sum(jnp.where(chosen, probs, 0.0), axis=-1, keepdims=True)
     result_ref[...] = (mixed + gate * combined).astype(BF16)
-    grad_gate = jnp.sum(cot * combined, axis=-1, keepdims=True)
+    grad_gate = jnp.sum(jnp.where(owned, gates_ref[...], 0.0), axis=-1, keepdims=True)
     grad_logits = (probs * (jnp.where(chosen, grad_gate, 0.0) - gate * grad_gate)).astype(BF16)
     grouter_ref[...] = dot_tn(normed_f[...], grad_logits)
     grad_normed = dot_nt(grad_logits, router_ref[...]) + dot_nn(picks, grows_ref[...])
@@ -390,35 +736,48 @@
         name="forward",
     )(rel_bias, inputs, weights, gain_a, gain_f, router, near, slot_row)
 
-    rows_all = spread(sent)
-    sources = wide * narrow
-    block = pl.BlockSpec((sources, 1, slots, width), lambda e: (0, e, 0, 0))
-    w_in_spec = pl.BlockSpec((1, width, hidden_width), lambda e: (e, 0, 0))
-    w_out_spec = pl.BlockSpec((1, hidden_width, width), lambda e: (e, 0, 0))
-    first_expert = (lax.axis_index("wide") * local).astype(jnp.int32)[None]
-    back, grows, gin, gout = pl.pallas_call(
-        expert_kernel,
-        grid=(local,),
-        out_shape=(
-            jax.ShapeDtypeStruct(rows_all.shape, BF16),
-            jax.ShapeDtypeStruct(rows_all.shape, BF16),
-            jax.ShapeDtypeStruct(expert_in.shape, F32),
-            jax.ShapeDtypeStruct(expert_out.shape, F32),
-        ),
-        in_specs=[
-            smem, block, block, w_in_spec, w_out_spec, pl.BlockSpec((width, experts), lambda e: (0, 0)),
-        ],
-        out_specs=(block, block, w_in_spec, w_out_spec),
-        scratch_shapes=[
-            pltpu.VMEM((sources * slots, hidden_width), BF16),
-            pltpu.VMEM((sources * slots, hidden_width), BF16),
-            pltpu.VMEM((sources * slots, width), BF16),
-        ],
-        compiler_params=params,
-        name="experts",
-    )(first_expert, rows_all, cot_all, expert_in, expert_out, router)
-    outs_back = collect(back)
-    grows_back = collect(grows)
+    if narrow == 4 and wide % 2 == 0 and slots % 16 == 0 and local * slots % BLOCK == 0:
+        outs, back, gates, gin, gout = moving_experts(
+            sent.reshape(wide, local, slots, width),
+            jnp.moveaxis(cot_all.reshape(narrow, wide, local, slots, width), 2, 0),
+            expert_in, expert_out, router, wide, narrow,
+        )
+        grows_back = back.reshape(total, width)
+        gates = gates.reshape(1, total)
+        outs_back = collect(
+            jnp.moveaxis(outs.reshape(local, narrow * wide, slots, width), 0, 1)
+        )
+    else:
+        rows_all = spread(sent)
+        sources = wide * narrow
+        block = pl.BlockSpec((sources, 1, slots, width), lambda e: (0, e, 0, 0))
+        w_in_spec = pl.BlockSpec((1, width, hidden_width), lambda e: (e, 0, 0))
+        w_out_spec = pl.BlockSpec((1, hidden_width, width), lambda e: (e, 0, 0))
+        first_expert = (lax.axis_index("wide") * local).astype(jnp.int32)[None]
+        back, grows, gin, gout = pl.pallas_call(
+            expert_kernel,
+            grid=(local,),
+            out_shape=(
+                jax.ShapeDtypeStruct(rows_all.shape, BF16),
+                jax.ShapeDtypeStruct(rows_all.shape, BF16),
+                jax.ShapeDtypeStruct(expert_in.shape, F32),
+                jax.ShapeDtypeStruct(expert_out.shape, F32),
+            ),
+            in_specs=[
+                smem, block, block, w_in_spec, w_out_spec, pl.BlockSpec((width, experts), lambda e: (0, 0)),
+            ],
+            out_specs=(block, block, w_in_spec, w_out_spec),
+            scratch_shapes=[
+                pltpu.VMEM((sources * slots, hidden_width), BF16),
+                pltpu.VMEM((sources * slots, hidden_width), BF16),
+                pltpu.VMEM((sources * slots, width), BF16),
+            ],
+            compiler_params=params,
+            name="experts",
+        )(first_expert, rows_all, cot_all, expert_in, expert_out, router)
+        outs_back = collect(back)
+        grows_back = collect(grows)
+        gates = jnp.sum(outs_back.astype(F32) * cot_sent.astype(F32), axis=1)[None, :]
 
     wide_t = lambda dtype: pltpu.VMEM((width, count), dtype)
     tall = lambda dtype: pltpu.VMEM((count, width), dtype)
@@ -429,7 +788,7 @@
             jax.ShapeDtypeStruct((width, experts), F32), jax.ShapeDtypeStruct((HEADS, 4 * BLOCK), F32),
             jax.ShapeDtypeStruct((HEADS, 2 * BLOCK), F32), jax.ShapeDtypeStruct((2, width), F32),
         ),
-        in_specs=[smem] + in_vmem(19),
+        in_specs=[smem] + in_vmem(20),
         out_specs=tuple(in_vmem(7)),
         scratch_shapes=[
             wide_t(BF16), wide_t(BF16), wide_t(BF16), tall(BF16), wide_t(BF16),
@@ -440,7 +799,7 @@
         name="backward",
     )(
         rel_bias, inputs, weights, gain_a, gain_f, router, near_back, slot_col, routes,
-        normed, q, k, v, att, lse, mixed, normed_f, cotangent, outs_back, grows_back,
+        normed, q, k, v, att, lse, mixed, normed_f, cotangent, outs_back, grows_back, gates,
     )
 
     gw = lax.psum_scatter(gw, BOTH, scatter_dimension=0, tiled=True).astype(F32)

time: 713 us -> 632 us (0.89)
  waiting for transfers between devices: 391 us -> 272 us
  Pallas kernels: 104 us -> 178 us
  blocking collectives: 174 us -> 132 us
  local copies, waits for them, and re-layouts: 11.8 us -> 24.2 us
    pallas_call x1 -> x2, Pallas kernels: 43.5 us -> 117 us  [the longest x1 99.5 us: moving_experts(): pl.pallas_call(moving_expert_kernel, out_shape=(sds((local, narrow, wide,...]
    reduce_scatter x2 -> x1, waiting for transfers between devices: 113 us -> 57.7 us  [collect(): lax.psum_scatter(rows.reshape(wide * narrow, local * slots, width), 'narr...]
    all_gather x2 -> x1, waiting for transfers between devices: 44.6 us -> 0.01 us  [spread(): held = lax.all_gather(taken, 'narrow', axis=0, tiled=True)]
    all_to_all x2 -> x1, blocking collectives: 95.9 us -> 53.9 us  [spread(): lax.all_to_all(rows.reshape(wide, local * slots, width), 'wide', split_ax...]
    unnamed x8 -> x6, waiting for transfers between devices: 87.9 us -> 69.5 us
    all_to_all x2 -> x1, waiting for transfers between devices: 36 us -> 36 us  [collect(): back = lax.all_to_all(own, 'wide', split_axis=0, concat_axis=0, tiled=True)]
  transfers between devices with their start and end apart: 9 -> 6, of which waited for: 6 -> 4; matrix products, arithmetic and copies ran while one was open for 1% -> 2% of each run, Pallas kernels for 4% -> 8%
where the time goes in v2:
time: 632 us; the launch traced here: 631 us
  waiting for transfers between devices  272 us (43%)
  Pallas kernels  178 us (28%)
  blocking collectives  132 us (21%)
  local copies, waits for them, and re-layouts  24.2 us (4%)
  between operations  14.6 us (2%)
    reduce_scatter x1, waiting for transfers between devices, shards(): gw = lax.psum_scatter(gw, BOTH, scatter_dimension=0, tiled=True).astype(F32)  109 us
    pallas_call x1, Pallas kernels, moving_experts(): pl.pallas_call(moving_expert_kernel, out_shape=(sds((local, narrow, wide,...  99.5 us
    unnamed x6, waiting for transfers between devices  69.5 us
    reduce_scatter x1, waiting for transfers between devices, collect(): lax.psum_scatter(rows.reshape(wide * narrow, local * slots, width), 'narr...  57.7 us
    all_to_all x1, blocking collectives, spread(): lax.all_to_all(rows.reshape(wide, local * slots, width), 'wide', split_ax...  53.9 us
    all_gather x1, blocking collectives, shards(): lax.all_gather(jnp.concatenate([w_router, gain_attn[:, None], gain_ffn[:,...  40.6 us
    psum x1, blocking collectives, shards(): grad_rel = lax.psum(grad_rel, BOTH)  37.4 us
    all_to_all x1, waiting for transfers between devices, collect(): back = lax.all_to_all(own, 'wide', split_axis=0, concat_axis=0, tiled=True)  36 us
  transfers between devices with their start and end apart: 6, of which 4 were waited for; matrix products, arithmetic and copies ran while one was open for 2% of the time, Pallas kernels for 8%

profile of v2, /device:TPU:0, one launch (start us, length us, event | category | flops | bytes accessed | tf_op | source)
XLA Modules:
  0.0 631.3 jit_solution(10332904660503639007)
XLA Ops:
  7.3 1.5 pad_maximum_fusion
  8.9 1.5 copy.67.refs_1_.routes_ref
  11.1 3.7 places.1
  14.8 53.9 %all_to_all.10 = bf16[8,128,768]{2,1,0:T(8,128)(2,1)} all-to-all(bf16[8,128,768]{2,1,0:T(8,128)(2,1)} %bitcast.52), channel_id=1, replica_groups=mesh['wide'=8,'narrow'=4] {'wide'}, dimensions={0} | all-to-all | bytes 3145728 | tf_op jit(solution)/shard_map/all_to_all | solution.py:711
  69.0 40.6 %all_gather.10 = bf16[768,34]{1,0:T(8,128)(2,1)S(1)} all-gather(bf16[24,34]{1,0:T(8,128)(2,1)S(1)} %pad_maximum_fusion.2), channel_id=1, replica_groups=mesh['wide'=8,'narrow'=4] {'wide','narrow'}, dimensions={0}, use_global_device_ids=true | all-gather | bytes 53856 | tf_op jit(solution)/shard_map/all_gather | solution.py:688
  109.7 0.3 convert_reduce_fusion
  110.0 0.6 reshape.162.gain_a
  110.6 0.6 reshape.163.gain_f
  111.1 0.7 copy.71.rel_ref
  111.8 1.0 convolution_bitcast_fusion.near_ref
  112.8 26.0 %forward.1 = (bf16[512,768]{1,0:T(8,128)(2,1)}, bf16[512,768]{1,0:T(8,128)(2,1)}, bf16[512,768]{1,0:T(8,128)(2,1)}, bf16[512,768]{1,0:T(8,128)(2,1)}, bf16[512,7...) custom-call(f32[32,12]{1,0:T(8,128)} %copy.71.rel_ref, ...), custom_call_target="tpu_custom_call" | custom-call | tf_op jit(solution)/shard_map/forward/pallas_call | solution.py:727
  138.9 6.2 copy.78
  145.1 99.5 %experts.1 = (bf16[4,4,8,32,768]{4,3,2,1,0:T(8,128)(2,1)}, bf16[4,4,256,768]{3,2,1,0:T(8,128)(2,1)}, bf16[4,4,256,768]{3,2,1,0:T(8,128)(2,1)}, bf16[4,4,256,768]...) custom-call(bf16[8,4,32,768]{3,2,1,0:T(8,128)(2,1)} %bitcast.51, ...), custom_call_target="tpu_custom_call" | custom-call | tf_op jit(solution)/shard_map/experts/pallas_call | solution.py:503
  244.6 6.2 copy.70
  250.9 57.7 %reduce-scatter.3.cloned.1.call-done = bf16[8,128,768]{2,1,0:T(8,128)(2,1)} async-done(((bf16[32,128,768]{2,1,0:T(8,128)(2,1)}), bf16[8,128,768]{2,1,0:T(8,128)(2,1)}) %reduce-scatter.3.cloned.1.call-update) | async-done | bytes 1572880 | tf_op jit(solution)/shard_map/reduce_scatter | solution.py:718
  308.6 5.5 all-to-all-start.1
  314.2 1.0 convolution_bitcast_fusion.1.near_ref
  315.1 36.0 %all-to-all-done.1 = bf16[8,128,768]{2,1,0:T(8,128)(2,1)S(1)} async-done(((bf16[8,128,768]{2,1,0:T(8,128)(2,1)}), bf16[8,128,768]{2,1,0:T(8,128)(2,1)S(1)}, u32[]{:S(2)}, u32[]{:S(2)}) %all-to-all-start.1) | async-done | bytes 1572896 | tf_op jit(solution)/shard_map/all_to_all | solution.py:721
  351.1 1.1 copy-done.1
  352.2 31.1 %backward.1 = (bf16[512,768]{1,0:T(8,128)(2,1)}, f32[512,768]{1,0:T(8,128)}, bf16[768,3072]{1,0:T(8,128)(2,1)}, f32[768,32]{1,0:T(8,128)}, f32[12,512]{1,0:T(8,1...) custom-call(f32[32,12]{1,0:T(8,128)} %copy.71.rel_ref, bf16[512,768]{1,0:T(8,128)(2,1)} %x_ref.3, ...), custom_call_target="tpu_custom_call" | custom-call | tf_op jit(solution)/shard_map/backward/pallas_call | solution.py:784
  383.3 1.1 copy.73
  384.5 0.7 pad_maximum_fusion.1
  385.2 0.9 copy.74
  386.2 0.5 reduce-scatter.5.cloned.1.call-update
  386.8 17.8 %weight_grads.1 = (f32[4,768,768]{2,1,0:T(8,128)}, f32[4,768,768]{2,1,0:T(8,128)}) custom-call(bf16[4,1024,768]{2,1,0:T(8,128)(2,1)} %bitcast.46, bf16[4,1024,768]{2,1,0:T(8,128)(2,1)} %bitcast.47, bf16[4,1024,768]{2,1,0:T(8,128)(2,1)} %bitcast.48, bf16[4,1024,768]{2,1,0:T(8,128)(2,1)} %bitcast.49), custom_call_target="tpu_custom_call" | custom-call | tf_op jit(solution)/shard_map/weight_grads/pallas_call | solution.py:549
  404.8 0.2 slice_reduce_fusion
  405.5 37.4 %psum.7 = f32[32,12]{0,1:T(8,128)} all-reduce(f32[32,12]{0,1:T(8,128)S(1)} %scatter-add.9), channel_id=1, replica_groups=mesh['wide'=8,'narrow'=4] {'wide','narrow'}, use_global_device_ids=true, to_apply=%region_5.0 | all-reduce | flops 384 | bytes 3072 | tf_op jit(solution)/shard_map/psum | solution.py:813
  443.0 68.9 %all-reduce.3.cloned.1.call-done = f32[768,34]{1,0:T(8,128)} async-done(((f32[768,34]{1,0:T(8,128)}), f32[768,34]{1,0:T(8,128)}) %all-reduce.3.cloned.1.call-update) | async-done | bytes 104464
  511.9 1.5 dynamic-slice_reduce_fusion
  513.4 1.3 constant_dynamic-slice_fusion
  514.7 108.6 %reduce-scatter.5.cloned.1.call-done = bf16[24,3072]{1,0:T(8,128)(2,1)} async-done(((bf16[768,3072]{1,0:T(8,128)(2,1)}), bf16[24,3072]{1,0:T(8,128)(2,1)}) %reduce-scatter.5.cloned.1.call-update) | async-done | bytes 147472 | tf_op jit(solution)/shard_map/reduce_scatter | solution.py:805
  623.2 1.5 fusion
  (43 shorter events, 1.3 us)
Async XLA Ops:
  7.2 104.7 %copy-start.3 = (f32[512,32]{1,0:T(8,128)S(1)}, f32[512,32]{1,0:T(8,128)}, u32[]{:S(2)}) copy-start(f32[512,32]{1,0:T(8,128)} %constant.65.clone) | copy-start | bytes 196612
  7.2 61.5 %copy-start.9 = (bf16[24]{0:T(256)(128)(2,1)S(1)}, bf16[24]{0:T(256)(128)(2,1)}, u32[]{:S(2)}) copy-start(bf16[24]{0:T(256)(128)(2,1)} %param.22) | copy-start | bytes 148
  7.2 61.6 %copy-start.10 = (bf16[24]{0:T(256)(128)(2,1)S(1)}, bf16[24]{0:T(256)(128)(2,1)}, u32[]{:S(2)}) copy-start(bf16[24]{0:T(256)(128)(2,1)} %param.28) | copy-start | bytes 148
  7.2 61.7 %copy-start.8 = (bf16[24,32]{1,0:T(8,128)(2,1)S(1)}, bf16[24,32]{1,0:T(8,128)(2,1)}, u32[]{:S(2)}) copy-start(bf16[24,32]{1,0:T(8,128)(2,1)} %param.29) | copy-start | bytes 4612
  7.2 103.9 %copy-start.4 = (f32[32,12]{0,1:T(8,128)S(1)}, f32[32,12]{0,1:T(8,128)}, u32[]{:S(2)}) copy-start(f32[32,12]{0,1:T(8,128)} %param.27) | copy-start | bytes 4612
  7.2 105.6 %all-gather.3.cloned.1.call-start = ((), (), s32[]{:S(2)}) async-start(), calls=%async_computation.4 | async-start | bytes 4866048 | tf_op jit(solution)/shard_map/all_gather | solution.py:687
  8.8 130.0 %all-gather.5.cloned.1.call-start = ((), (), s32[]{:S(2)}) async-start(), calls=%async_computation.5 | async-start | bytes 7864320 | tf_op jit(solution)/shard_map/all_gather | solution.py:714
  68.7 239.9 %reduce-scatter.3.cloned.1.call-start = ((), (), s32[]{:S(2)}) async-start(), calls=%async_computation.6 | async-start | bytes 7864320 | tf_op jit(solution)/shard_map/reduce_scatter | solution.py:718
  109.7 3.1 copy-start
  250.9 63.3 %copy-start.2 = (f32[512,32]{1,0:T(8,128)S(1)}, f32[512,32]{1,0:T(8,128)}, u32[]{:S(2)}) copy-start(f32[512,32]{1,0:T(8,128)} %constant.66.clone) | copy-start | bytes 196612
  308.6 42.5 %all-to-all-start.1 = ((bf16[8,128,768]{2,1,0:T(8,128)(2,1)}), bf16[8,128,768]{2,1,0:T(8,128)(2,1)S(1)}, u32[]{:S(2)}, u32[]{:S(2)}) async-start(bf16[8,128,768]{2,1,0:T(8,128)(2,1)} %reduce-scatter.3.cloned.1.call-done), calls=%async_computation.2 | async-start | bytes 3145728 | tf_op jit(solution)/shard_map/all_to_all | solution.py:721
  314.1 197.8 %all-reduce.3.cloned.1.call-start = ((), (), s32[]{:S(2)}) async-start(), calls=%async_computation.8 | async-start | bytes 786432
  351.1 1.1 copy-start.1
  386.1 237.1 %reduce-scatter.5.cloned.1.call-start = ((), (), s32[]{:S(2)}) async-start(), calls=%async_computation.7 | async-start | bytes 4866048 | tf_op jit(solution)/shard_map/reduce_scatter | solution.py:805
  386.7 17.9 %copy-start.5 = (f32[32,512]{1,0:T(8,128)S(1)}, f32[32,512]{1,0:T(8,128)}, u32[]{:S(2)}) copy-start(f32[32,512]{1,0:T(8,128)} %constant.67.clone) | copy-start | bytes 196612
  386.7 17.9 %copy-start.6 = (f32[12,512]{1,0:T(8,128)S(1)}, f32[12,512]{1,0:T(8,128)}, u32[]{:S(2)}) copy-start(f32[12,512]{1,0:T(8,128)} %get-tuple-element.84) | copy-start | bytes 73732
  386.7 18.2 %copy-start.7 = (f32[12,256]{1,0:T(8,128)S(1)}, f32[12,256]{1,0:T(8,128)}, u32[]{:S(2)}) copy-start(f32[12,256]{1,0:T(8,128)} %get-tuple-element.85) | copy-start | bytes 36868
Sparse Core Ops, SparseCore 0:
  11.5 74.6 all-gather.2
  87.8 45.6 all-gather.4
  251.0 57.5 reduce-scatter.2
  386.2 125.5 all-reduce.2
  517.2 105.9 reduce-scatter.4

commit v3 on v2

--- a/solution.py
+++ b/solution.py
@@ -242,6 +242,9 @@
         self.x, self.c = self.n // 2, lax.rem(self.n, 2)
         self.core = (self.w, self.x * 2 + 1 - self.c)
         self.side = (self.w, (1 - self.x) * 2 + self.c)
+        self.deep = wide // 2
+        self.z, self.y = self.w // 2, lax.rem(self.w, 2)
+        self.row = (self.z * 2 + 1 - self.y, self.n)
 
     def at(self, step):
         return lax.rem(self.w + step, self.wide)
@@ -564,36 +567,28 @@
     return outs, back, gates, gin, gout
 
 
-def backward_kernel(
-    rel_ref, x_ref, w_ref, gain_a, gain_f, router_ref, near_ref, slot_col, routes_ref,
-    normed_ref, q_ref, k_ref, v_ref, att_ref, lse_ref, mixed_ref, normed_f, cot_ref, outs_ref, grows_ref, gates_ref,
-    result_ref, gx_ref, gw_ref, grouter_ref, gnear_ref, gfar_ref, ggain_ref,
-    q_t, k_t, normed_t, datt, datt_t, delta, lse_t, gq, gk, gv, gmixed, dst,
-):
-    count, width = x_ref.shape
-    head_dim = width // HEADS
-    blocks = count // BLOCK
-    bucket_count = rel_ref.shape[0]
-    experts = router_ref.shape[1]
-    owned = lax.broadcasted_iota(jnp.int32, (count, outs_ref.shape[0]), 1) == slot_col[...]
-    picks = owned.astype(BF16)
-    combined = dot_nn(picks, outs_ref[...])
-    mixed = mixed_ref[...]
-    cot = cot_ref[...].astype(F32)
+def routed_gate(normed_f, router_ref, routes_ref):
     probs = softmax_lanes(dot_nn(normed_f[...], router_ref[...]))
-    chosen = lax.broadcasted_iota(jnp.int32, (count, experts), 1) == routes_ref[...]
-    gate = jnp.sum(jnp.where(chosen, probs, 0.0), axis=-1, keepdims=True)
-    result_ref[...] = (mixed + gate * combined).astype(BF16)
+    chosen = lax.broadcasted_iota(jnp.int32, probs.shape, 1) == routes_ref[...]
+    return probs, chosen, jnp.sum(jnp.where(chosen, probs, 0.0), axis=-1, keepdims=True)
+
+
+def slot_owners(slot_col, total):
+    return lax.broadcasted_iota(jnp.int32, (slot_col.shape[0], total), 1) == slot_col[...]
+
+
+def ffn_backward(probs, chosen, gate, owned, gates_ref, normed_f, router_ref, grows_ref, mixed, cot_ref, gain_f):
     grad_gate = jnp.sum(jnp.where(owned, gates_ref[...], 0.0), axis=-1, keepdims=True)
     grad_logits = (probs * (jnp.where(chosen, grad_gate, 0.0) - gate * grad_gate)).astype(BF16)
-    grouter_ref[...] = dot_tn(normed_f[...], grad_logits)
-    grad_normed = dot_nt(grad_logits, router_ref[...]) + dot_nn(picks, grows_ref[...])
-    grad_norm, ggain_ref[1:2, :] = norm_backward(mixed, inverse_rms(mixed), gain_f[...], grad_normed)
-    grad_mixed = cot + grad_norm
-    gmixed[...] = grad_mixed
-    branch = grad_mixed.astype(BF16)
-    gw_ref[:, 3 * width : 4 * width] = dot_tn(att_ref[...], branch).astype(BF16)
-    datt[...] = dot_nt(branch, w_ref[:, 3 * width : 4 * width]).astype(BF16)
+    grad_router = dot_tn(normed_f[...], grad_logits)
+    grad_normed = dot_nt(grad_logits, router_ref[...]) + dot_nn(owned.astype(BF16), grows_ref[...])
+    grad_norm, grad_gain = norm_backward(mixed, inverse_rms(mixed), gain_f[...], grad_normed)
+    return grad_router, cot_ref[...].astype(F32) + grad_norm, grad_gain
+
+
+def attention_setup(q_ref, k_ref, normed_ref, att_ref, lse_ref, datt, q_t, k_t, normed_t, datt_t, delta, lse_t):
+    count, width = q_ref.shape
+    head_dim = width // HEADS
     datt_t[...] = datt[...].T
     q_t[...] = (q_ref[...] * jnp.asarray(head_dim**-0.5, BF16)).T
     k_t[...] = k_ref[...].T
@@ -601,68 +596,452 @@
     products = datt_t[...].astype(F32) * att_ref[...].T.astype(F32)
     delta[...] = jnp.sum(products.reshape(HEADS, head_dim, count), axis=1)
     lse_t[...] = lse_ref[...].T
+
+
+def pair_backward(
+    at, rel_ref, near_ref, q_ref, k_ref, v_ref, q_t, k_t, datt, datt_t, delta, lse_t, dst, gq, gk, gv, gnear_ref, gfar_ref
+):
+    count, width = q_ref.shape
+    head_dim = width // HEADS
+    blocks = count // BLOCK
+    bucket_count = rel_ref.shape[0]
     first = lax.broadcasted_iota(jnp.int32, (1, BLOCK), 1) < head_dim
-
-    def pair(at, carry):
-        cols = pl.ds(pl.multiple_of(at * BLOCK, BLOCK), BLOCK)
-        q_pair, datt_pair = q_ref[:, cols], datt[:, cols]
-        gq_parts, gk_parts, gv_parts = [], [], []
-        for half in range(2):
-            head = 2 * at + half
-            low, high = rel_ref[bucket_count // 2 - 1, head], rel_ref[bucket_count - 1, head]
-            mask = first if half == 0 else jnp.logical_not(first)
-            near = toeplitz_near(near_ref[pl.ds(head, 1), :])
-            lse_row, delta_row = lse_t[pl.ds(head, 1), :], delta[pl.ds(head, 1), :]
-            near_sum = jnp.zeros((BLOCK, 3 * BLOCK), F32)
-            low_sum, high_sum = jnp.zeros((BLOCK, BLOCK), F32), jnp.zeros((BLOCK, BLOCK), F32)
-            gk_rows, gv_rows = [], []
-            for row in range(blocks):
-                rows = slice(row * BLOCK, (row + 1) * BLOCK)
-                k_rows, v_rows = k_ref[rows, cols], v_ref[rows, cols]
-                zeros = jnp.zeros_like(k_rows)
-                scores = dot_nn(jnp.where(mask, k_rows, zeros), q_t[cols, :])
-                scores = scores + bias_rows(near, high, low, row, blocks)
-                weights = jnp.exp(scores - lse_row)
-                grad_weights = dot_nn(jnp.where(mask, v_rows, zeros), datt_t[cols, :])
-                grad_scores = weights * (grad_weights - delta_row)
-                gv_rows.append(dot_nn(weights.astype(BF16), datt_pair))
-                low_bits = grad_scores.astype(BF16)
-                dst[rows, :] = low_bits
-                gk_rows.append(dot_nn(low_bits, q_pair))
-                for column in range(blocks):
-                    piece = grad_scores[:, column * BLOCK : (column + 1) * BLOCK]
-                    distance = column - row
-                    if distance <= -2:
-                        high_sum = high_sum + piece
-                    elif distance >= 2:
-                        low_sum = low_sum + piece
-                    else:
-                        pads = [jnp.zeros((BLOCK, BLOCK), F32)] * 3
-                        pads[distance + 1] = piece
-                        near_sum = near_sum + jnp.concatenate(pads, axis=1)
-            gq_parts.append(
-                dot_nn(k_t[pl.ds(pl.multiple_of(head * head_dim, head_dim), head_dim), :], dst[...])
-            )
-            gk_parts.append(jnp.concatenate(gk_rows, axis=0))
-            gv_parts.append(jnp.concatenate(gv_rows, axis=0))
-            gnear_ref[pl.ds(head, 1), :] = diagonal_sums(near_sum)
-            gfar_ref[pl.ds(head, 1), :] = jnp.concatenate(
-                [jnp.sum(low_sum, axis=0, keepdims=True), jnp.sum(high_sum, axis=0, keepdims=True)], axis=1
-            )
-        scale = head_dim**-0.5
-        gq[:, cols] = (jnp.concatenate(gq_parts, axis=0).T * scale).astype(BF16)
-        gk[:, cols] = (jnp.where(first, gk_parts[0], gk_parts[1]) * scale).astype(BF16)
-        gv[:, cols] = jnp.where(first, gv_parts[0], gv_parts[1]).astype(BF16)
-        return carry
-
-    lax.fori_loop(0, HEADS // 2, pair, 0)
+    cols = pl.ds(pl.multiple_of(at * BLOCK, BLOCK), BLOCK)
+    q_pair, datt_pair = q_ref[:, cols], datt[:, cols]
+    gq_parts, gk_parts, gv_parts = [], [], []
+    for half in range(2):
+        head = 2 * at + half
+        low, high = rel_ref[bucket_count // 2 - 1, head], rel_ref[bucket_count - 1, head]
+        mask = first if half == 0 else jnp.logical_not(first)
+        near = toeplitz_near(near_ref[pl.ds(head, 1), :])
+        lse_row, delta_row = lse_t[pl.ds(head, 1), :], delta[pl.ds(head, 1), :]
+        near_sum = jnp.zeros((BLOCK, 3 * BLOCK), F32)
+        low_sum, high_sum = jnp.zeros((BLOCK, BLOCK), F32), jnp.zeros((BLOCK, BLOCK), F32)
+        gk_rows, gv_rows = [], []
+        for row in range(blocks):
+            rows = slice(row * BLOCK, (row + 1) * BLOCK)
+            k_rows, v_rows = k_ref[rows, cols], v_ref[rows, cols]
+            zeros = jnp.zeros_like(k_rows)
+            scores = dot_nn(jnp.where(mask, k_rows, zeros), q_t[cols, :])
+            scores = scores + bias_rows(near, high, low, row, blocks)
+            weights = jnp.exp(scores - lse_row)
+            grad_weights = dot_nn(jnp.where(mask, v_rows, zeros), datt_t[cols, :])
+            grad_scores = weights * (grad_weights - delta_row)
+            gv_rows.append(dot_nn(weights.astype(BF16), datt_pair))
+            low_bits = grad_scores.astype(BF16)
+            dst[rows, :] = low_bits
+            gk_rows.append(dot_nn(low_bits, q_pair))
+            for column in range(blocks):
+                piece = grad_scores[:, column * BLOCK : (column + 1) * BLOCK]
+                distance = column - row
+                if distance <= -2:
+                    high_sum = high_sum + piece
+                elif distance >= 2:
+                    low_sum = low_sum + piece
+                else:
+                    pads = [jnp.zeros((BLOCK, BLOCK), F32)] * 3
+                    pads[distance + 1] = piece
+                    near_sum = near_sum + jnp.concatenate(pads, axis=1)
+        gq_parts.append(
+            dot_nn(k_t[pl.ds(pl.multiple_of(head * head_dim, head_dim), head_dim), :], dst[...])
+        )
+        gk_parts.append(jnp.concatenate(gk_rows, axis=0))
+        gv_parts.append(jnp.concatenate(gv_rows, axis=0))
+        gnear_ref[pl.ds(head, 1), :] = diagonal_sums(near_sum)
+        gfar_ref[pl.ds(head, 1), :] = jnp.concatenate(
+            [jnp.sum(low_sum, axis=0, keepdims=True), jnp.sum(high_sum, axis=0, keepdims=True)], axis=1
+        )
+    scale = head_dim**-0.5
+    gq[:, cols] = (jnp.concatenate(gq_parts, axis=0).T * scale).astype(BF16)
+    gk[:, cols] = (jnp.where(first, gk_parts[0], gk_parts[1]) * scale).astype(BF16)
+    gv[:, cols] = jnp.where(first, gv_parts[0], gv_parts[1]).astype(BF16)
+
+
+def input_backward(x_ref, w_ref, gain_a, gmixed, gq, gk, gv):
+    count, width = x_ref.shape
     grad_normed = jnp.zeros((count, width), F32)
     for at, grad in enumerate((gq, gk, gv)):
-        gw_ref[:, at * width : (at + 1) * width] = dot_nn(normed_t[...], grad[...]).astype(BF16)
         grad_normed = grad_normed + dot_nt(grad[...], w_ref[:, at * width : (at + 1) * width])
     tokens = x_ref[...].astype(F32)
-    grad_norm, ggain_ref[0:1, :] = norm_backward(tokens, inverse_rms(tokens), gain_a[...], grad_normed)
-    gx_ref[...] = gmixed[...] + grad_norm
+    grad_norm, grad_gain = norm_backward(tokens, inverse_rms(tokens), gain_a[...], grad_normed)
+    return gmixed[...] + grad_norm, grad_gain
+
+
+def backward_kernel(
+    rel_ref, x_ref, w_ref, gain_a, gain_f, router_ref, near_ref, slot_col, routes_ref,
+    normed_ref, q_ref, k_ref, v_ref, att_ref, lse_ref, mixed_ref, normed_f, cot_ref, outs_ref, grows_ref, gates_ref,
+    result_ref, gx_ref, gw_ref, grouter_ref, gnear_ref, gfar_ref, ggain_ref,
+    q_t, k_t, normed_t, datt, datt_t, delta, lse_t, gq, gk, gv, gmixed, dst,
+):
+    width = x_ref.shape[1]
+    probs, chosen, gate = routed_gate(normed_f, router_ref, routes_ref)
+    owned = slot_owners(slot_col, outs_ref.shape[0])
+    mixed = mixed_ref[...]
+    result_ref[...] = (mixed + gate * dot_nn(owned.astype(BF16), outs_ref[...])).astype(BF16)
+    grouter_ref[...], grad_mixed, ggain_ref[1:2, :] = ffn_backward(
+        probs, chosen, gate, owned, gates_ref, normed_f, router_ref, grows_ref, mixed, cot_ref, gain_f
+    )
+    gmixed[...] = grad_mixed
+    branch = grad_mixed.astype(BF16)
+    gw_ref[:, 3 * width : 4 * width] = dot_tn(att_ref[...], branch).astype(BF16)
+    datt[...] = dot_nt(branch, w_ref[:, 3 * width : 4 * width]).astype(BF16)
+    attention_setup(q_ref, k_ref, normed_ref, att_ref, lse_ref, datt, q_t, k_t, normed_t, datt_t, delta, lse_t)
+
+    def pair(at, carry):
+        pair_backward(
+            at, rel_ref, near_ref, q_ref, k_ref, v_ref, q_t, k_t, datt, datt_t, delta, lse_t, dst, gq, gk, gv,
+            gnear_ref, gfar_ref,
+        )
+        return carry
+
+    lax.fori_loop(0, HEADS // 2, pair, 0)
+    for at, grad in enumerate((gq, gk, gv)):
+        gw_ref[:, at * width : (at + 1) * width] = dot_nn(normed_t[...], grad[...]).astype(BF16)
+    gx_ref[...], ggain_ref[0:1, :] = input_backward(x_ref, w_ref, gain_a, gmixed, gq, gk, gv)
+
+
+class Sums:
+    def __init__(self, place, unit, buffers, semaphores, out):
+        self.p, self.unit, self.out = place, unit, out
+        self.send, self.core, self.kept, self.from_y, self.over_x, self.from_x, self.over_z, self.from_z, self.last = buffers
+        self.s, self.r = semaphores
+        self.deep = self.send.shape[1]
+
+    def to_core(self):
+        u, p = self.unit, self.p
+        return remote(self.send.at[u], self.core.at[u], self.s.at[u, 0], self.r.at[u, 0], p.core)
+
+    def to_y(self):
+        u, p = self.unit, self.p
+        return remote(self.kept.at[u, 1 - p.y], self.from_y.at[u], self.s.at[u, 1], self.r.at[u, 1], p.row)
+
+    def to_x(self):
+        u, p = self.unit, self.p
+        return remote(self.over_x.at[u, 1 - p.x], self.from_x.at[u], self.s.at[u, 2], self.r.at[u, 2], p.side)
+
+    def to_z(self, k):
+        u, p = self.unit, self.p
+        z = lax.rem(p.z + k, p.deep)
+        return remote(
+            self.over_z.at[u, z], self.from_z.at[u, k], self.s.at[u, 3 + k], self.r.at[u, 3 + k], (z * 2 + p.y, p.n)
+        )
+
+    def to_last(self):
+        u, p = self.unit, self.p
+        return remote(self.last.at[u, 1 - p.c], self.out.at[u, p.c], self.s.at[u, 3], self.r.at[u, 3], p.core)
+
+    def begin(self, part):
+        self.send[self.unit] = part.astype(BF16).reshape(self.send.shape[1:])
+        self.to_core().start()
+
+    def stage_core(self, part):
+        u = self.unit
+        self.to_core().wait_recv()
+        kept = part.reshape(self.core.shape[1:]) + self.core[u].astype(F32)
+        self.kept[u] = kept.astype(BF16)
+        self.to_y().start()
+
+    def stage_y(self):
+        u = self.unit
+        self.to_y().wait_recv()
+        self.over_x[u] = (self.kept[u, self.p.y].astype(F32) + self.from_y[u].astype(F32)).astype(BF16)
+        self.to_x().start()
+
+    def stage_x(self):
+        u = self.unit
+        self.to_x().wait_recv()
+        self.over_z[u] = (self.over_x[u, self.p.x].astype(F32) + self.from_x[u].astype(F32)).astype(BF16)
+        for k in range(1, self.p.deep):
+            self.to_z(k).start()
+
+    def stage_z(self):
+        u = self.unit
+        total = self.over_z[u, self.p.z].astype(F32)
+        for k in range(1, self.p.deep):
+            self.to_z(k).wait_recv()
+            total = total + self.from_z[u, k].astype(F32)
+        self.last[u] = total.reshape(self.last.shape[1:])
+        self.to_last().start()
+        self.out[u, self.p.c] = self.last[u, self.p.c]
+
+    def drain(self):
+        for copy in (self.to_core(), self.to_y(), self.to_x()):
+            copy.wait_send()
+        for k in range(1, self.p.deep):
+            self.to_z(k).wait_send()
+        self.to_last().wait()
+
+
+def sum_buffers(units, wide, rows, cols):
+    deep = wide // 2
+    vmem = lambda *shape, dtype=BF16: pltpu.VMEM((units, *shape), dtype)
+    return [
+        vmem(2, 2, deep, rows, cols), vmem(2, 2, deep, rows, cols), vmem(2, 2, deep, rows, cols),
+        vmem(2, deep, rows, cols), vmem(2, deep, rows, cols), vmem(deep, rows, cols), vmem(deep, rows, cols),
+        vmem(deep, rows, cols), vmem(2, rows // 2, cols, dtype=F32),
+        pltpu.SemaphoreType.DMA((units, 3 + deep)), pltpu.SemaphoreType.DMA((units, 3 + deep)),
+    ]
+
+
+def moving_backward_kernel(
+    rel_ref, x_ref, w_ref, gain_a, gain_f, router_ref, near_ref, slot_col, routes_ref,
+    normed_ref, q_ref, k_ref, v_ref, att_ref, lse_ref, mixed_ref, normed_f, cot_ref, outs_hbm, grows_ref, gates_ref, picks_ref,
+    result_ref, gx_ref, gw_out, go_out, small_out,
+    q_t, k_t, normed_t, datt, datt_t, delta, lse_t, gq, gk, gv, gmixed, dst, gnear, gfar,
+    own, from_core, to_side, from_side, near_sum, ready, returned, own_s, rc_s, rc_r, rx_s, rx_r, rw_s, rw_r,
+    u1, u2, u3, u4, u5, u6, u7, u8, u9, us, ur, o1, o2, o3, o4, o5, o6, o7, o8, o9, os, orr,
+    small, small_in, ss, sr,
+):
+    count, width = x_ref.shape
+    local, _, step, _ = outs_hbm.shape
+    wide, _, slots, _ = returned.shape
+    total = wide * local * slots
+    p = Place(wide)
+    far_x = (1 - p.x) * 2
+    greet(p.partners())
+
+    def core_copy(e, far):
+        m = (far_x if far else p.x * 2) + 1 - p.c
+        return remote(outs_hbm.at[e, m], from_core.at[e, far], rc_s.at[e, far], rc_r.at[e, far], p.core)
+
+    def own_copy(e, far):
+        m = (far_x if far else p.x * 2) + p.c
+        return pltpu.make_async_copy(outs_hbm.at[e, m], own.at[e, far], own_s.at[e, far])
+
+    def side_copy(e):
+        return remote(to_side.at[e], from_side.at[e], rx_s.at[e], rx_r.at[e], p.side)
+
+    def back_copy(e, k):
+        return remote(ready.at[e, p.at(k)], returned.at[p.w, e], rw_s.at[e, k], rw_r.at[e, k], p.peer(k))
+
+    for far in (1, 0):
+        for e in range(local):
+            core_copy(e, far).start()
+            own_copy(e, far).start()
+
+    def over_side(e):
+        core_copy(e, 1).wait_recv()
+        own_copy(e, 1).wait()
+        to_side[e] = (own[e, 1].astype(F32) + from_core[e, 1].astype(F32)).astype(BF16)
+        side_copy(e).start()
+
+    def nearby(e):
+        core_copy(e, 0).wait_recv()
+        own_copy(e, 0).wait()
+        near_sum[e] = own[e, 0].astype(F32) + from_core[e, 0].astype(F32)
+
+    def finish(e):
+        side_copy(e).wait_recv()
+        ready[e] = (near_sum[e] + from_side[e].astype(F32)).astype(BF16).reshape(wide, slots, width)
+        for k in range(1, wide):
+            back_copy(e, k).start()
+        returned[p.w, e] = ready[e, p.w]
+
+    probs, chosen, gate = routed_gate(normed_f, router_ref, routes_ref)
+    owned = slot_owners(slot_col, total)
+    grad_router, grad_mixed, grad_gain_f = ffn_backward(
+        probs, chosen, gate, owned, gates_ref, normed_f, router_ref, grows_ref, mixed_ref[...], cot_ref, gain_f
+    )
+    gmixed[...] = grad_mixed
+    small[0] = jnp.zeros_like(small[0])
+    small[0, HEADS : HEADS + 1, :] = grad_gain_f
+    for e in range(local):
+        over_side(e)
+    branch = grad_mixed.astype(BF16)
+    o_sums = Sums(p, 0, (o1, o2, o3, o4, o5, o6, o7, o8, o9), (os, orr), go_out)
+    half_cols = width // 2
+    router_cols = go_out.shape[-1] - half_cols
+    router_wide = jnp.concatenate(
+        [grad_router, jnp.zeros((width, router_cols - grad_router.shape[1]), F32)], axis=1
+    )
+
+    def output_part(core):
+        low, high = branch[:, :half_cols], branch[:, half_cols:]
+        part = dot_tn(att_ref[...], jnp.where(core == 0, low, high))
+        return order_rows(jnp.concatenate([part, jnp.where(core == 0, router_wide, 0.0)], axis=1), p)
+
+    o_sums.begin(output_part(1 - p.c))
+    datt[...] = dot_nt(branch, w_ref[:, 3 * width : 4 * width]).astype(BF16)
+    for e in range(local):
+        nearby(e)
+    o_sums.stage_core(output_part(p.c))
+    attention_setup(q_ref, k_ref, normed_ref, att_ref, lse_ref, datt, q_t, k_t, normed_t, datt_t, delta, lse_t)
+
+    def pair(at):
+        pair_backward(
+            at, rel_ref, near_ref, q_ref, k_ref, v_ref, q_t, k_t, datt, datt_t, delta, lse_t, dst, gq, gk, gv,
+            gnear, gfar,
+        )
+        cols = pl.ds(pl.multiple_of(at * BLOCK, BLOCK), BLOCK)
+        grads = jnp.concatenate([gq[:, cols], gk[:, cols], gv[:, cols]], axis=1)
+        return order_rows(dot_nn(normed_t[...], grads), p)
+
+    def unit(u):
+        return Sums(p, u, (u1, u2, u3, u4, u5, u6, u7, u8, u9), (us, ur), gw_out)
+
+    units = HEADS // 4
+
+    def pairs(u, carry):
+        unit(u).begin(pair(2 * u + 1 - p.c))
+
+        @pl.when(u == 0)
+        def _():
+            o_sums.stage_y()
+
+        @pl.when(u == 1)
+        def _():
+            o_sums.stage_z()
+
+        @pl.when(u >= 1)
+        def _():
+            unit(u - 1).stage_y()
+            finish(u - 1)
+
+        @pl.when(u >= 2)
+        def _():
+            unit(u - 2).stage_z()
+
+        unit(u).stage_core(pair(2 * u + p.c))
+
+        @pl.when(u == 0)
+        def _():
+            o_sums.stage_x()
+
+        @pl.when(u >= 1)
+        def _():
+            unit(u - 1).stage_x()
+
+        return carry
+
+    lax.fori_loop(0, units, pairs, 0)
+    near_grads = jnp.dot(gnear[...], picks_ref[...], precision=HIGHEST, preferred_element_type=F32)
+    buckets = lax.broadcasted_iota(jnp.int32, near_grads.shape, 1)
+    low_sum = jnp.sum(gfar[:, :BLOCK], axis=1, keepdims=True)
+    high_sum = jnp.sum(gfar[:, BLOCK:], axis=1, keepdims=True)
+    bucket_count = rel_ref.shape[0]
+    rel = near_grads + jnp.where(buckets == bucket_count // 2 - 1, low_sum, 0.0)
+    small[0, :HEADS, :BLOCK] = rel + jnp.where(buckets == bucket_count - 1, high_sum, 0.0)
+    gx_ref[...], grad_gain_a = input_backward(x_ref, w_ref, gain_a, gmixed, gq, gk, gv)
+    small[0, HEADS + 1 : HEADS + 2, :] = grad_gain_a
+
+    def small_copy(stage, device, slot):
+        return remote(small.at[stage], small_in.at[slot], ss.at[slot], sr.at[slot], device)
+
+    hops = [[p.core], [p.row], [p.side], [(lax.rem(p.z + k, p.deep) * 2 + p.y, p.n) for k in range(1, p.deep)]]
+    copies, slot = [], 0
+    for stage, devices in enumerate(hops):
+        copies.append([small_copy(stage, device, slot + at) for at, device in enumerate(devices)])
+        slot += len(devices)
+
+    def small_start(stage):
+        for copy in copies[stage]:
+            copy.start()
+
+    def small_end(stage):
+        slot = sum(len(c) for c in copies[:stage])
+        found = small[stage]
+        for at, copy in enumerate(copies[stage]):
+            copy.wait_recv()
+            found = found + small_in[slot + at]
+        return found
+
+    small_start(0)
+    last = unit(units - 1)
+    last.stage_y()
+    for e in range(units - 1, local):
+        finish(e)
+    small[1] = small_end(0)
+    small_start(1)
+    unit(units - 2).stage_z()
+    last.stage_x()
+    small[2] = small_end(1)
+    small_start(2)
+    small[3] = small_end(2)
+    small_start(3)
+    last.stage_z()
+    small_out[...] = small_end(3)
+    for e in range(local):
+        for k in range(1, wide):
+            back_copy(e, k).wait_recv()
+    combined = dot_nn(owned.astype(BF16), returned[...].reshape(total, width))
+    result_ref[...] = (mixed_ref[...] + gate * combined).astype(BF16)
+    for e in range(local):
+        core_copy(e, 0).wait_send()
+        core_copy(e, 1).wait_send()
+        side_copy(e).wait_send()
+        for k in range(1, wide):
+            back_copy(e, k).wait_send()
+    o_sums.drain()
+    for u in range(units):
+        unit(u).drain()
+    for stage in copies:
+        for copy in stage:
+            copy.wait_send()
+
+
+def order_rows(part, place):
+    width, cols = part.shape
+    rows = width // (place.deep * 4)
+    blocks = part.reshape(place.deep, 2, 2, rows, cols)
+    return jnp.transpose(blocks, (1, 2, 0, 3, 4)).reshape(width, cols)
+
+
+def moving_backward(
+    rel_bias, inputs, weights, gain_a, gain_f, router, near, slot_col, routes,
+    normed, q, k, v, att, lse, mixed, normed_f, cotangent, outs, grows, gates, wide, slots,
+):
+    count, width = inputs.shape
+    local, narrow, step, _ = outs.shape
+    experts = router.shape[1]
+    bucket_count = rel_bias.shape[0]
+    deep, rows = wide // 2, width // (wide * 2)
+    units = HEADS // 4
+    pair_cols, out_cols = 3 * BLOCK, width // 2 + BLOCK * -(-experts // BLOCK)
+    sds = jax.ShapeDtypeStruct
+    smem = pl.BlockSpec(memory_space=pltpu.SMEM)
+    any_spec = pl.BlockSpec(memory_space=pl.ANY)
+    picks = np.zeros((4 * BLOCK, BLOCK), np.float32)
+    picks[:, :bucket_count] = near_picks(bucket_count, -1)
+    wide_t = lambda dtype: pltpu.VMEM((width, count), dtype)
+    tall = lambda dtype: pltpu.VMEM((count, width), dtype)
+    vmem = lambda *shape, dtype=BF16: pltpu.VMEM(shape, dtype)
+    dma = pltpu.SemaphoreType.DMA
+    hops = 3 + deep - 1
+    result, grad_inputs, gw, go, small = pl.pallas_call(
+        moving_backward_kernel,
+        out_shape=(
+            sds((count, width), BF16), sds((count, width), F32), sds((units, 2, rows // 2, pair_cols), F32),
+            sds((1, 2, rows // 2, out_cols), F32), sds((16, width), F32),
+        ),
+        in_specs=[smem] + in_vmem(17) + [any_spec] + in_vmem(3),
+        out_specs=tuple(in_vmem(5)),
+        scratch_shapes=[
+            wide_t(BF16), wide_t(BF16), wide_t(BF16), tall(BF16), wide_t(BF16),
+            vmem(HEADS, count, dtype=F32), vmem(BLOCK, count, dtype=F32),
+            tall(BF16), tall(BF16), tall(BF16), tall(F32), vmem(count, count),
+            vmem(HEADS, 4 * BLOCK, dtype=F32), vmem(HEADS, 2 * BLOCK, dtype=F32),
+            vmem(local, 2, step, width), vmem(local, 2, step, width), vmem(local, step, width), vmem(local, step, width),
+            vmem(local, step, width, dtype=F32), vmem(local, wide, slots, width), vmem(wide, local, slots, width),
+            dma((local, 2)), dma((local, 2)), dma((local, 2)), dma((local,)), dma((local,)),
+            dma((local, wide)), dma((local, wide)),
+            *sum_buffers(units, wide, rows, pair_cols), *sum_buffers(1, wide, rows, out_cols),
+            vmem(4, 16, width, dtype=F32), vmem(hops, 16, width, dtype=F32), dma((hops,)), dma((hops,)),
+        ],
+        compiler_params=pltpu.CompilerParams(collective_id=3, has_side_effects=True, vmem_limit_bytes=62 << 20),
+        name="backward",
+    )(
+        rel_bias, inputs, weights, gain_a, gain_f, router, near, slot_col, routes,
+        normed, q, k, v, att, lse, mixed, normed_f, cotangent, outs, grows, gates, jnp.asarray(picks),
+    )
+    kinds = [
+        jnp.transpose(gw[..., at * BLOCK : (at + 1) * BLOCK], (2, 0, 1, 3)).reshape(rows // 2, width) for at in range(3)
+    ]
+    grad_output = jnp.transpose(go[0, :, :, : width // 2], (1, 0, 2)).reshape(rows // 2, width)
+    grad_router = go[0, 0, :, width // 2 : width // 2 + experts]
+    device = lax.axis_index("wide") * narrow + lax.axis_index("narrow")
+    gains = lax.dynamic_slice(small, (HEADS, device * (rows // 2)), (2, rows // 2))
+    grad_rel = small[:HEADS, :bucket_count].T
+    return result, grad_inputs, kinds, grad_output, grad_router, gains[1], gains[0], grad_rel
 
 
 def in_vmem(count):
@@ -736,48 +1115,53 @@
         name="forward",
     )(rel_bias, inputs, weights, gain_a, gain_f, router, near, slot_row)
 
-    if narrow == 4 and wide % 2 == 0 and slots % 16 == 0 and local * slots % BLOCK == 0:
+    moving = narrow == 4 and wide % 2 == 0 and slots % 16 == 0 and local * slots % BLOCK == 0
+    moving = moving and width % (wide * 2 * 16) == 0 and count == SEQ_LEN
+    if moving:
         outs, back, gates, gin, gout = moving_experts(
             sent.reshape(wide, local, slots, width),
             jnp.moveaxis(cot_all.reshape(narrow, wide, local, slots, width), 2, 0),
             expert_in, expert_out, router, wide, narrow,
         )
-        grows_back = back.reshape(total, width)
-        gates = gates.reshape(1, total)
-        outs_back = collect(
-            jnp.moveaxis(outs.reshape(local, narrow * wide, slots, width), 0, 1)
-        )
-    else:
-        rows_all = spread(sent)
-        sources = wide * narrow
-        block = pl.BlockSpec((sources, 1, slots, width), lambda e: (0, e, 0, 0))
-        w_in_spec = pl.BlockSpec((1, width, hidden_width), lambda e: (e, 0, 0))
-        w_out_spec = pl.BlockSpec((1, hidden_width, width), lambda e: (e, 0, 0))
-        first_expert = (lax.axis_index("wide") * local).astype(jnp.int32)[None]
-        back, grows, gin, gout = pl.pallas_call(
-            expert_kernel,
-            grid=(local,),
-            out_shape=(
-                jax.ShapeDtypeStruct(rows_all.shape, BF16),
-                jax.ShapeDtypeStruct(rows_all.shape, BF16),
-                jax.ShapeDtypeStruct(expert_in.shape, F32),
-                jax.ShapeDtypeStruct(expert_out.shape, F32),
-            ),
-            in_specs=[
-                smem, block, block, w_in_spec, w_out_spec, pl.BlockSpec((width, experts), lambda e: (0, 0)),
-            ],
-            out_specs=(block, block, w_in_spec, w_out_spec),
-            scratch_shapes=[
-                pltpu.VMEM((sources * slots, hidden_width), BF16),
-                pltpu.VMEM((sources * slots, hidden_width), BF16),
-                pltpu.VMEM((sources * slots, width), BF16),
-            ],
-            compiler_params=params,
-            name="experts",
-        )(first_expert, rows_all, cot_all, expert_in, expert_out, router)
-        outs_back = collect(back)
-        grows_back = collect(grows)
-        gates = jnp.sum(outs_back.astype(F32) * cot_sent.astype(F32), axis=1)[None, :]
+        result, grad_inputs, kinds, grad_output, grad_router, grad_gain_a, grad_gain_f, grad_rel = moving_backward(
+            rel_bias, inputs, weights, gain_a, gain_f, router, near_back, slot_col, routes,
+            normed, q, k, v, att, lse, mixed, normed_f, cotangent, outs, back.reshape(total, width),
+            gates.reshape(1, total), wide, slots,
+        )
+        return (
+            result, grad_inputs, grad_gain_a, *kinds, grad_output, grad_rel, grad_gain_f, grad_router, gin, gout,
+        )
+
+    rows_all = spread(sent)
+    sources = wide * narrow
+    block = pl.BlockSpec((sources, 1, slots, width), lambda e: (0, e, 0, 0))
+    w_in_spec = pl.BlockSpec((1, width, hidden_width), lambda e: (e, 0, 0))
+    w_out_spec = pl.BlockSpec((1, hidden_width, width), lambda e: (e, 0, 0))
+    first_expert = (lax.axis_index("wide") * local).astype(jnp.int32)[None]
+    back, grows, gin, gout = pl.pallas_call(
+        expert_kernel,
+        grid=(local,),
+        out_shape=(
+            jax.ShapeDtypeStruct(rows_all.shape, BF16),
+            jax.ShapeDtypeStruct(rows_all.shape, BF16),
+            jax.ShapeDtypeStruct(expert_in.shape, F32),
+            jax.ShapeDtypeStruct(expert_out.shape, F32),
+        ),
+        in_specs=[
+            smem, block, block, w_in_spec, w_out_spec, pl.BlockSpec((width, experts), lambda e: (0, 0)),
+        ],
+        out_specs=(block, block, w_in_spec, w_out_spec),
+        scratch_shapes=[
+            pltpu.VMEM((sources * slots, hidden_width), BF16),
+            pltpu.VMEM((sources * slots, hidden_width), BF16),
+            pltpu.VMEM((sources * slots, width), BF16),
+        ],
+        compiler_params=params,
+        name="experts",
+    )(first_expert, rows_all, cot_all, expert_in, expert_out, router)
+    outs_back = collect(back)
+    grows_back = collect(grows)
+    gates = jnp.sum(outs_back.astype(F32) * cot_sent.astype(F32), axis=1)[None, :]
 
     wide_t = lambda dtype: pltpu.VMEM((width, count), dtype)
     tall = lambda dtype: pltpu.VMEM((count, width), dtype)

time: 632 us -> 389 us (0.62)
  waiting for transfers between devices: 272 us -> 0.04 us
  Pallas kernels: 178 us -> 255 us
  blocking collectives: 132 us -> 94.3 us
    reduce_scatter x2 -> x0, waiting for transfers between devices: 166 us -> none  [the longest x1 109 us: shards(): gw = lax.psum_scatter(gw, BOTH, scatter_dimension=0, tiled=True).astype(F32)]
    pallas_call x1, Pallas kernels: 31.1 us -> 108 us  [moving_backward(): pl.pallas_call(moving_backward_kernel, out_shape=(sds((count, width), BF1...]
    unnamed x6 -> x2, waiting for transfers between devices: 69.5 us -> 0.03 us
    psum x1 -> x0, blocking collectives: 37.4 us -> none  [shards(): grad_rel = lax.psum(grad_rel, BOTH)]
    all_to_all x1 -> x0, waiting for transfers between devices: 36 us -> none  [collect(): back = lax.all_to_all(own, 'wide', split_axis=0, concat_axis=0, tiled=True)]
  transfers between devices with their start and end apart: 6 -> 2, of which waited for: 4 -> 0; matrix products, arithmetic and copies ran while one was open for 2% -> 2% of each run, Pallas kernels for 8% -> 8%
where the time goes in v3:
time: 389 us; the launch traced here: 388 us
  Pallas kernels  255 us (66%)
  blocking collectives  94.3 us (24%)
  local copies, waits for them, and re-layouts  20.4 us (5%)
  between operations  14.8 us (4%)
    pallas_call x1, Pallas kernels, moving_backward(): pl.pallas_call(moving_backward_kernel, out_shape=(sds((count, width), BF1...  108 us
    pallas_call x1, Pallas kernels, moving_experts(): pl.pallas_call(moving_expert_kernel, out_shape=(sds((local, narrow, wide,...  99.3 us
    all_to_all x1, blocking collectives, spread(): lax.all_to_all(rows.reshape(wide, local * slots, width), 'wide', split_ax...  54 us
    all_gather x1, blocking collectives, shards(): lax.all_gather(jnp.concatenate([w_router, gain_attn[:, None], gain_ffn[:,...  40.3 us
    pallas_call x1, Pallas kernels, shards(): pl.pallas_call(forward_kernel, out_shape=(rows_t(BF16), rows_t(BF16), row...  26.1 us
    pallas_call x1, Pallas kernels, moving_experts(): pl.pallas_call(weight_grad_kernel, grid=(local,), out_shape=(sds(expert_i...  17.7 us
  transfers between devices with their start and end apart: 2, of which 0 were waited for; matrix products, arithmetic and copies ran while one was open for 2% of the time, Pallas kernels for 8%

profile of v3, /device:TPU:0, one launch (start us, length us, event | category | flops | bytes accessed | tf_op | source)
XLA Modules:
  0.0 388.4 jit_solution(4692593485271466772)
XLA Ops:
  7.3 1.6 pad_maximum_fusion
  8.9 0.0 all-gather.5.cloned.1.call-start
  9.6 1.5 copy.48.refs_1_.routes_ref
  11.1 3.7 places.1
  14.8 54.0 %all_to_all.5 = bf16[8,128,768]{2,1,0:T(8,128)(2,1)} all-to-all(bf16[8,128,768]{2,1,0:T(8,128)(2,1)} %bitcast.55), channel_id=1, replica_groups=mesh['wide'=8,'narrow'=4] {'wide'}, dimensions={0} | all-to-all | bytes 3145728 | tf_op jit(solution)/shard_map/all_to_all | solution.py:1090
  68.8 0.7 copy.51.rel_ref
  69.5 0.1 copy.47
  69.6 0.1 copy.46
  69.7 0.1 pad_maximum_fusion.1
  69.8 40.3 %all_gather.10 = bf16[768,34]{1,0:T(8,128)(2,1)S(1)} all-gather(bf16[24,34]{1,0:T(8,128)(2,1)S(1)} %pad_maximum_fusion.1), channel_id=1, replica_groups=mesh['wide'=8,'narrow'=4] {'wide','narrow'}, dimensions={0}, use_global_device_ids=true | all-gather | bytes 53856 | tf_op jit(solution)/shard_map/all_gather | solution.py:1067
  110.1 0.3 convert_reduce_fusion
  110.4 0.6 reshape.100.gain_a
  111.0 0.6 reshape.101.gain_f
  111.6 1.0 convolution_bitcast_fusion.1.near_ref
  112.6 1.0 convolution_bitcast_fusion.near_ref
  113.5 26.1 %forward.1 = (bf16[512,768]{1,0:T(8,128)(2,1)}, bf16[512,768]{1,0:T(8,128)(2,1)}, bf16[512,768]{1,0:T(8,128)(2,1)}, bf16[512,768]{1,0:T(8,128)(2,1)}, bf16[512,7...) custom-call(f32[32,12]{1,0:T(8,128)} %copy.51.rel_ref, ...), custom_call_target="tpu_custom_call" | custom-call | tf_op jit(solution)/shard_map/forward/pallas_call | solution.py:1106
  139.7 6.2 %copy.59 = bf16[4,8,4,32,768]{4,3,1,0,2:T(8,128)(2,1)} copy(bf16[4,8,4,32,768]{4,3,2,1,0:T(8,128)(2,1)} %bitcast.48) | data formatting | bytes 12582912 | tf_op jit(solution)/shard_map/reshape;reshape | solution.py:1123
  145.9 99.3 %experts.1 = (bf16[4,4,8,32,768]{4,3,2,1,0:T(8,128)(2,1)}, bf16[4,4,256,768]{3,2,1,0:T(8,128)(2,1)}, bf16[4,4,256,768]{3,2,1,0:T(8,128)(2,1)}, bf16[4,4,256,768]...) custom-call(bf16[8,4,32,768]{3,2,1,0:T(8,128)(2,1)} %bitcast.54, ...), custom_call_target="tpu_custom_call" | custom-call | tf_op jit(solution)/shard_map/experts/pallas_call | solution.py:506
  245.2 107.9 %backward.1 = (bf16[512,768]{1,0:T(8,128)(2,1)}, f32[512,768]{1,0:T(8,128)}, f32[3,2,24,384]{3,2,1,0:T(8,128)}, f32[1,2,24,512]{3,2,1,0:T(8,128)}, f32[16,768]{1,0:T(8,128)}) custom-call(f32[32,12]{1,0:T(8,128)} %copy.51.rel_ref, bf16[512,768]{1,0:T(8,128)(2,1)} %x_ref.3, bf16[768,3072]{1,0:T(8,128)(2,1)} %all-gather.3.cloned.1.call-done.w_ref, ...), custom_call_target="tpu_custom_call" | custom-call | tf_op jit(solution)/shard_map/backward/pallas_call | solution.py:1010
  353.2 0.9 slice_bitcast_fusion
  354.1 1.3 slice_bitcast_fusion.4
  355.4 1.3 slice_bitcast_fusion.5
  356.7 0.8 constant_dynamic-slice_fusion
  357.4 0.5 slice_bitcast_fusion.6
  358.0 1.0 slice_bitcast_fusion.1
  359.0 0.7 reshape.92
  359.7 0.7 reshape.93
  360.4 0.7 reshape.94
  361.1 0.6 copy.57
  361.8 17.7 %weight_grads.1 = (f32[4,768,768]{2,1,0:T(8,128)}, f32[4,768,768]{2,1,0:T(8,128)}) custom-call(bf16[4,1024,768]{2,1,0:T(8,128)(2,1)} %bitcast.49, bf16[4,1024,768]{2,1,0:T(8,128)(2,1)} %bitcast.50, bf16[4,1024,768]{2,1,0:T(8,128)(2,1)} %bitcast.51, bf16[4,1024,768]{2,1,0:T(8,128)(2,1)} %bitcast.52), custom_call_target="tpu_custom_call" | custom-call | tf_op jit(solution)/shard_map/weight_grads/pallas_call | solution.py:552
  379.5 0.9 copy.63
  380.4 1.1 copy.64
  (26 shorter events, 0.2 us)
Async XLA Ops:
  7.2 104.4 %copy-start.4 = (f32[512,32]{1,0:T(8,128)S(1)}, f32[512,32]{1,0:T(8,128)}, u32[]{:S(2)}) copy-start(f32[512,32]{1,0:T(8,128)} %constant.26.clone) | copy-start | bytes 196612
  7.2 105.4 %copy-start.3 = (f32[512,32]{1,0:T(8,128)S(1)}, f32[512,32]{1,0:T(8,128)}, u32[]{:S(2)}) copy-start(f32[512,32]{1,0:T(8,128)} %constant.25.clone) | copy-start | bytes 196612
  7.2 61.6 %copy-start.5 = (f32[32,12]{0,1:T(8,128)S(1)}, f32[32,12]{0,1:T(8,128)}, u32[]{:S(2)}) copy-start(f32[32,12]{0,1:T(8,128)} %param.23) | copy-start | bytes 4612
  7.2 62.3 %copy-start.7 = (bf16[24]{0:T(256)(128)(2,1)S(1)}, bf16[24]{0:T(256)(128)(2,1)}, u32[]{:S(2)}) copy-start(bf16[24]{0:T(256)(128)(2,1)} %param.24) | copy-start | bytes 148
  7.2 62.4 %copy-start.8 = (bf16[24]{0:T(256)(128)(2,1)S(1)}, bf16[24]{0:T(256)(128)(2,1)}, u32[]{:S(2)}) copy-start(bf16[24]{0:T(256)(128)(2,1)} %param.18) | copy-start | bytes 148
  7.2 62.5 %copy-start.6 = (bf16[24,32]{1,0:T(8,128)(2,1)S(1)}, bf16[24,32]{1,0:T(8,128)(2,1)}, u32[]{:S(2)}) copy-start(bf16[24,32]{1,0:T(8,128)(2,1)} %param.25) | copy-start | bytes 4612
  7.2 106.3 %all-gather.3.cloned.1.call-start = ((), (), s32[]{:S(2)}) async-start(), calls=%async_computation.1 | async-start | bytes 4866048 | tf_op jit(solution)/shard_map/all_gather | solution.py:1066
  8.9 130.8 %all-gather.5.cloned.1.call-start = ((), (), s32[]{:S(2)}) async-start(), calls=%async_computation.2 | async-start | bytes 7864320 | tf_op jit(solution)/shard_map/all_gather | solution.py:1093
  110.1 3.4 copy-start
  361.8 17.7 %copy-start.2 = (bf16[512,768]{1,0:T(8,128)(2,1)S(1)}, bf16[512,768]{1,0:T(8,128)(2,1)}, u32[]{:S(2)}) copy-start(bf16[512,768]{1,0:T(8,128)(2,1)} %get-tuple-element.83) | copy-start | bytes 2359300
  361.8 18.6 %copy-start.1 = (f32[512,768]{1,0:T(8,128)S(1)}, f32[512,768]{1,0:T(8,128)}, u32[]{:S(2)}) copy-start(f32[512,768]{1,0:T(8,128)} %get-tuple-element.84) | copy-start | bytes 4718596
Sparse Core Ops, SparseCore 0:
  11.6 74.1 all-gather.2
  87.3 45.4 all-gather.4

commit v4 on v3

--- a/solution.py
+++ b/solution.py
@@ -128,45 +128,55 @@
     cot_out[...] = dot_nn(picks, cot_ref[...]).astype(BF16)
 
 
+def pair_forward(at, rel_ref, near_ref, q_ref, k_ref, v_ref, att_ref, lse_ref):
+    count, width = q_ref.shape
+    head_dim = width // HEADS
+    blocks = count // BLOCK
+    bucket_count = rel_ref.shape[0]
+    lanes = lax.broadcasted_iota(jnp.int32, (1, BLOCK), 1)
+    first = lanes < head_dim
+    cols = pl.ds(pl.multiple_of(at * BLOCK, BLOCK), BLOCK)
+    k_pair, v_pair = k_ref[:, cols], v_ref[:, cols]
+    nears = [toeplitz_near(near_ref[pl.ds(2 * at + half, 1), :]) for half in range(2)]
+    for row in range(blocks):
+        rows = slice(row * BLOCK, (row + 1) * BLOCK)
+        q_rows = q_ref[rows, cols] * jnp.asarray(head_dim**-0.5, BF16)
+        found = []
+        log_sums = lse_ref[rows, :]
+        for half in range(2):
+            head = 2 * at + half
+            low, high = rel_ref[bucket_count // 2 - 1, head], rel_ref[bucket_count - 1, head]
+            mask = first if half == 0 else jnp.logical_not(first)
+            scores = dot_nt(jnp.where(mask, q_rows, jnp.zeros_like(q_rows)), k_pair)
+            scores = scores + bias_rows(nears[half], low, high, row, blocks)
+            peak = jnp.max(scores, axis=-1, keepdims=True)
+            exponent = jnp.exp(scores - peak)
+            total = jnp.sum(exponent, axis=-1, keepdims=True)
+            found.append(dot_nn((exponent * (1.0 / total)).astype(BF16), v_pair))
+            log_sums = jnp.where(lanes == head, peak + jnp.log(total), log_sums)
+        lse_ref[rows, :] = log_sums
+        att_ref[rows, cols] = jnp.where(first, found[0], found[1]).astype(BF16)
+
+
+def slot_rows(slot_row, values, total):
+    picks = lax.broadcasted_iota(jnp.int32, (total, slot_row.shape[1]), 0) == slot_row
+    return dot_nn(picks.astype(BF16), values).astype(BF16)
+
+
 def forward_kernel(
     rel_ref, x_ref, w_ref, gain_a, gain_f, router_ref, near_ref, slot_row,
     normed_ref, q_ref, k_ref, v_ref, att_ref, lse_ref, mixed_ref, normed_f, sent_ref,
 ):
-    count, width = x_ref.shape
-    head_dim = width // HEADS
-    blocks = count // BLOCK
-    bucket_count = rel_ref.shape[0]
+    width = x_ref.shape[1]
     tokens = x_ref[...].astype(F32)
     normed = (tokens * inverse_rms(tokens) * gain_a[...]).astype(BF16)
     normed_ref[...] = normed
     for out, at in ((q_ref, 0), (k_ref, 1), (v_ref, 2)):
         out[...] = dot_nn(normed, w_ref[:, at * width : (at + 1) * width]).astype(BF16)
     lse_ref[...] = jnp.zeros_like(lse_ref)
-    first = lax.broadcasted_iota(jnp.int32, (1, BLOCK), 1) < head_dim
-    lanes = lax.broadcasted_iota(jnp.int32, (1, BLOCK), 1)
 
     def pair(at, carry):
-        cols = pl.ds(pl.multiple_of(at * BLOCK, BLOCK), BLOCK)
-        k_pair, v_pair = k_ref[:, cols], v_ref[:, cols]
-        nears = [toeplitz_near(near_ref[pl.ds(2 * at + half, 1), :]) for half in range(2)]
-        for row in range(blocks):
-            rows = slice(row * BLOCK, (row + 1) * BLOCK)
-            q_rows = q_ref[rows, cols] * jnp.asarray(head_dim**-0.5, BF16)
-            found = []
-            log_sums = lse_ref[rows, :]
-            for half in range(2):
-                head = 2 * at + half
-                low, high = rel_ref[bucket_count // 2 - 1, head], rel_ref[bucket_count - 1, head]
-                mask = first if half == 0 else jnp.logical_not(first)
-                scores = dot_nt(jnp.where(mask, q_rows, jnp.zeros_like(q_rows)), k_pair)
-                scores = scores + bias_rows(nears[half], low, high, row, blocks)
-                peak = jnp.max(scores, axis=-1, keepdims=True)
-                exponent = jnp.exp(scores - peak)
-                total = jnp.sum(exponent, axis=-1, keepdims=True)
-                found.append(dot_nn((exponent * (1.0 / total)).astype(BF16), v_pair))
-                log_sums = jnp.where(lanes == head, peak + jnp.log(total), log_sums)
-            lse_ref[rows, :] = log_sums
-            att_ref[rows, cols] = jnp.where(first, found[0], found[1]).astype(BF16)
+        pair_forward(at, rel_ref, near_ref, q_ref, k_ref, v_ref, att_ref, lse_ref)
         return carry
 
     lax.fori_loop(0, HEADS // 2, pair, 0)
@@ -174,9 +184,7 @@
     mixed_ref[...] = mixed
     normed_2 = (mixed * inverse_rms(mixed) * gain_f[...]).astype(BF16)
     normed_f[...] = normed_2
-    total_slots = sent_ref.shape[0]
-    picks = (lax.broadcasted_iota(jnp.int32, (total_slots, count), 0) == slot_row[...]).astype(BF16)
-    sent_ref[...] = dot_nn(picks, normed_2).astype(BF16)
+    sent_ref[...] = slot_rows(slot_row[...], normed_2, sent_ref.shape[0])
 
 
 def expert_kernel(
@@ -238,22 +246,35 @@
 class Place:
     def __init__(self, wide):
         self.wide = wide
+        self.run = wide // 2
+        self.deep = wide // 2
         self.w, self.n = lax.axis_index("wide"), lax.axis_index("narrow")
         self.x, self.c = self.n // 2, lax.rem(self.n, 2)
+        self.z, self.y = self.w // 2, lax.rem(self.w, 2)
         self.core = (self.w, self.x * 2 + 1 - self.c)
         self.side = (self.w, (1 - self.x) * 2 + self.c)
-        self.deep = wide // 2
-        self.z, self.y = self.w // 2, lax.rem(self.w, 2)
         self.row = (self.z * 2 + 1 - self.y, self.n)
 
-    def at(self, step):
-        return lax.rem(self.w + step, self.wide)
-
-    def peer(self, step):
-        return (self.at(step), self.n)
+    def flip(self, j):
+        found, bit = self.w, 1
+        while bit <= j:
+            if j & bit:
+                found = found + bit - 2 * bit * lax.rem(self.w // bit, 2)
+            bit *= 2
+        return found
+
+    def peer(self, j):
+        return (self.flip(j), self.n)
+
+    def span(self, far):
+        half = self.w // self.run
+        return pl.ds((1 - half if far else half) * self.run, self.run)
+
+    def steps(self, far):
+        return range(self.run, self.wide) if far else range(1, self.run)
 
     def partners(self):
-        return [self.peer(k) for k in range(1, self.wide)] + [self.core, self.side]
+        return [self.peer(j) for j in range(1, self.wide)] + [self.core, self.side]
 
 
 class Spread:
@@ -262,66 +283,376 @@
         self.wide_s, self.wide_r, self.side_s, self.side_r = wide_s, wide_r, side_s, side_r
         self.core_s, self.core_r = core_s, core_r
 
-    def hop(self, e, k):
+    def hop(self, e, j):
         p = self.place
         return remote(
-            self.sent.at[p.at(k), e], self.held.at[e, p.n, p.w], self.wide_s.at[e, k], self.wide_r.at[e, k], p.peer(k)
+            self.sent.at[p.flip(j), e], self.held.at[e, p.n, p.w], self.wide_s.at[e, j], self.wide_r.at[e, j], p.peer(j)
         )
 
-    def start(self, e):
-        for k in range(1, self.place.wide):
-            self.hop(e, k).start()
-
-    def half(self, e, h):
+    def start(self, e, far):
+        for j in self.place.steps(far):
+            self.hop(e, j).start()
+
+    def beside(self, e, far):
         p = self.place
-        run = p.wide // 2
-        rows = self.held.at[e, p.n, pl.ds(h * run, run)]
-        return remote(rows, rows, self.side_s.at[e, h], self.side_r.at[e, h], p.side)
-
-    def over(self, e, far):
+        rows = self.held.at[e, p.n, p.span(far)]
+        return remote(rows, rows, self.side_s.at[e, far], self.side_r.at[e, far], p.side)
+
+    def over(self, e, other, far):
         p = self.place
-        m = (1 - p.x) * 2 + p.c if far else p.n
+        rows = self.held.at[e, (1 - p.x) * 2 + p.c if other else p.n, p.span(far)]
+        at = 2 * other + far
+        return remote(rows, rows, self.core_s.at[e, at], self.core_r.at[e, at], p.core)
+
+    def forward(self, e, far):
+        for j in self.place.steps(far):
+            self.hop(e, j).wait_recv()
+        self.beside(e, far).start()
+        self.over(e, 0, far).start()
+
+    def pass_on(self, e):
+        for far in range(2):
+            self.beside(e, far).wait_recv()
+            self.over(e, 1, far).start()
+
+    def arrive(self, e):
+        for other in range(2):
+            for far in range(2):
+                self.over(e, other, far).wait_recv()
+
+    def drain(self, e):
+        for j in range(1, self.place.wide):
+            self.hop(e, j).wait_send()
+        for far in range(2):
+            self.beside(e, far).wait_send()
+            self.over(e, 0, far).wait_send()
+            self.over(e, 1, far).wait_send()
+
+
+class Collect:
+    def __init__(self, place, to_core, from_core, from_side, returned, semaphores):
+        self.place, self.to_core, self.from_core = place, to_core, from_core
+        self.from_side, self.returned = from_side, returned
+        self.core_s, self.core_r, self.side_s, self.side_r, self.wide_s, self.wide_r = semaphores
+
+    def core(self, e, other):
         return remote(
-            self.held.at[e, m], self.held.at[e, m], self.core_s.at[e, far], self.core_r.at[e, far], p.core
+            self.to_core(e, other), self.from_core.at[e, other], self.core_s.at[e, other], self.core_r.at[e, other],
+            self.place.core,
         )
 
-    def forward(self, e):
+    def beside(self, e, far):
+        rows = self.place.span(far)
+        return remote(
+            self.from_core.at[e, 1, rows], self.from_side.at[e, rows], self.side_s.at[e, far], self.side_r.at[e, far],
+            self.place.side,
+        )
+
+    def back(self, e, j):
         p = self.place
-        run = p.wide // 2
-        for other in range(2):
-            h = p.w // run
-            h = 1 - h if other else h
-            for k in range(1, p.wide):
-                mine = (p.at(p.wide - k) // run) == h
-
-                @pl.when(mine)
-                def _():
-                    self.hop(e, k).wait_recv()
-
-            self.half(e, h).start()
-        self.over(e, 0).start()
-
-    def pass_on(self, e):
-        for h in range(2):
-            self.half(e, h).wait_recv()
-        self.over(e, 1).start()
+        return remote(
+            self.from_side.at[e, p.flip(j)], self.returned.at[p.w, e], self.wide_s.at[e, j], self.wide_r.at[e, j], p.peer(j)
+        )
+
+    def go_beside(self, e, part):
+        self.core(e, 1).wait_recv()
+        held = self.from_core[e, 1].astype(F32)
+        self.from_core[e, 1] = (part.astype(F32).reshape(held.shape) + held).astype(BF16)
+        self.beside(e, 1).start()
+        self.beside(e, 0).start()
+
+    def finish(self, e, far, part):
+        p = self.place
+        rows = p.span(far)
+        self.beside(e, far).wait_recv()
+        self.from_side[e, rows] = (part(rows) + self.from_side[e, rows].astype(F32)).astype(BF16)
+        for j in p.steps(far):
+            self.back(e, j).start()
+        if not far:
+            self.returned[p.w, e] = self.from_side[e, p.w]
+
+    def drain(self, e):
+        self.core(e, 0).wait_send()
+        self.core(e, 1).wait_send()
+        for far in range(2):
+            self.beside(e, far).wait_send()
+        for j in range(1, self.place.wide):
+            self.back(e, j).wait_send()
 
     def arrive(self, e):
-        self.over(e, 0).wait_recv()
-        self.over(e, 1).wait_recv()
-
-    def drain(self, e):
-        for k in range(1, self.place.wide):
-            self.hop(e, k).wait_send()
-        for h in range(2):
-            self.half(e, h).wait_send()
-            self.over(e, h).wait_send()
+        for j in range(1, self.place.wide):
+            self.back(e, j).wait_recv()
+
+
+class Gather:
+    def __init__(self, place, unit, held, halves, semaphores):
+        self.p, self.u, self.held, self.halves = place, unit, held, halves
+        self.s, self.r = semaphores
+
+    def piece(self, *place):
+        return self.held.at[self.u, self.p.c, *place] if self.halves else self.held.at[self.u, *place]
+
+    def column(self, y, x):
+        return self.piece(slice(None), y, x)
+
+    def copy(self, piece, slot, device):
+        return remote(piece, piece, self.s.at[self.u, slot], self.r.at[self.u, slot], device)
+
+    def to_z(self, k):
+        p = self.p
+        z = lax.rem(p.z + k, p.deep)
+        return self.copy(self.piece(p.z, p.y, p.x), k - 1, (z * 2 + p.y, p.n))
+
+    def to_x(self):
+        return self.copy(self.column(self.p.y, self.p.x), 3, self.p.side)
+
+    def to_y(self):
+        return self.copy(self.column(self.p.y, self.p.x), 4, self.p.row)
+
+    def corner(self):
+        return self.copy(self.column(self.p.y, 1 - self.p.x), 5, self.p.row)
+
+    def to_core(self, at):
+        p = self.p
+        y, x = ((p.y, p.x), (p.y, 1 - p.x), (1 - p.y, p.x), (1 - p.y, 1 - p.x))[at]
+        return self.copy(self.column(y, x), 6 + at, p.core)
+
+    def hand(self, at):
+        if self.halves:
+            self.to_core(at).start()
+
+    def start(self):
+        for k in range(1, self.p.deep):
+            self.to_z(k).start()
+
+    def spread(self):
+        for k in range(1, self.p.deep):
+            self.to_z(k).wait_recv()
+        self.to_x().start()
+        self.to_y().start()
+        self.hand(0)
+
+    def forward(self):
+        self.to_x().wait_recv()
+        self.corner().start()
+        self.hand(1)
+        self.to_y().wait_recv()
+        self.hand(2)
+
+    def end(self):
+        self.corner().wait_recv()
+        self.hand(3)
+
+    def arrive(self):
+        if self.halves:
+            for at in range(4):
+                self.to_core(at).wait_recv()
+
+    def drain(self):
+        for k in range(1, self.p.deep):
+            self.to_z(k).wait_send()
+        for copy in (self.to_x(), self.to_y(), self.corner()):
+            copy.wait_send()
+        if self.halves:
+            for at in range(4):
+                self.to_core(at).wait_send()
+
+
+def moving_forward_kernel(
+    rel_ref, capacity_ref, x_ref, q_part, k_part, v_part, o_part, small_part, near_ref, routes_ref, row_ref, cot_ref,
+    normed_ref, q_ref, k_ref, v_ref, att_ref, lse_ref, mixed_ref, normed_f, sent_ref, slot_col,
+    router_out, gains_out, weights_out, cot_out,
+    held, small, pair_send, pair_got, small_got, cot_sent, weight_s, pair_s, pair_r,
+    gs, gr, hs, hr, wide_s, wide_r, side_s, side_r, core_s, core_r,
+):
+    count, width = x_ref.shape
+    wide, local, slots, _ = cot_sent.shape
+    experts = router_out.shape[1]
+    total = wide * local * slots
+    units = HEADS // 4
+    rows = pair_send.shape[2]
+    p = Place(wide)
+    greet(p.partners())
+
+    def own_cols(u, half):
+        if u == units:
+            return o_part[:, half * (width // 2) : (half + 1) * (width // 2)]
+        cols = slice((2 * u + half) * BLOCK, (2 * u + half + 1) * BLOCK)
+        return jnp.concatenate([q_part[:, cols], k_part[:, cols], v_part[:, cols]], axis=1)
+
+    def swap_copies():
+        return [
+            remote(pair_send.at[0], pair_got.at[0], pair_s.at[0], pair_r.at[0], p.core),
+            remote(small_part, small_got, pair_s.at[1], pair_r.at[1], p.core),
+        ]
+
+    for u in range(units + 1):
+        pair_send[0, u] = jnp.where(p.c == 0, own_cols(u, 1), own_cols(u, 0))
+    for copy in swap_copies():
+        copy.start()
+    for copy in swap_copies():
+        copy.wait_recv()
+
+    def joined(mine, other):
+        mine, other = mine.astype(F32), other.astype(F32)
+        return jnp.concatenate(
+            [jnp.where(p.c == 0, mine, other), jnp.where(p.c == 0, other, mine)], axis=0
+        ).astype(BF16)
+
+    def gather(u):
+        return Gather(p, u, held, True, (gs, gr))
+
+    small_gather = Gather(p, 0, small, False, (hs, hr))
+    small[0, p.z, p.y, p.x] = joined(small_part[...], small_got[...])
+    small_gather.start()
+    for u in range(units + 1):
+        mine = jnp.where(p.c == 0, own_cols(u, 0), own_cols(u, 1))
+        held[u, p.c, p.z, p.y, p.x] = joined(mine, pair_got[0, u])
+        if u < 2:
+            gather(u).start()
+
+    limit = capacity_ref[0] * count // experts
+    slot_col[...], slot_row = slot_places(routes_ref, row_ref, limit, experts, slots, count)
+    cot_sent[...] = slot_rows(slot_row, cot_ref[...], total).reshape(cot_sent.shape)
+    moves = Spread(p, cot_sent, cot_out, wide_s, wide_r, side_s, side_r, core_s, core_r)
+
+    def own_rows(e):
+        return pltpu.make_async_copy(cot_sent.at[p.w, e], cot_out.at[e, p.n, p.w], weight_s.at[1 + e])
+
+    for e in range(local):
+        own_rows(e).start()
+    small_gather.spread()
+    gather(0).spread()
+    gather(2).start()
+    gather(1).spread()
+    gather(3).start()
+    small_gather.forward()
+    gather(0).forward()
+    for e in range(local):
+        moves.start(e, 0)
+    moves.start(0, 1)
+    small_gather.end()
+    small_all = small[0].reshape(width, BLOCK)
+    router_out[...] = small_all[:, :experts]
+    gains = small_all.astype(F32).T[experts : experts + 8, :]
+    gains_out[...] = gains
+    tokens = x_ref[...].astype(F32)
+    normed_ref[...] = (tokens * inverse_rms(tokens) * gains[0:1, :]).astype(BF16)
+    lse_ref[...] = jnp.zeros_like(lse_ref)
+    gather(1).forward()
+    for e in range(local):
+        own_rows(e).wait()
+    moves.forward(0, 0)
+    moves.start(1, 1)
+
+    def pair(at, weight):
+        cols = pl.ds(pl.multiple_of(at * BLOCK, BLOCK), BLOCK)
+        found = dot_nn(normed_ref[...], weight.reshape(width, 3 * BLOCK)).astype(BF16)
+        q_ref[:, cols], k_ref[:, cols], v_ref[:, cols] = (found[:, i * BLOCK : (i + 1) * BLOCK] for i in range(3))
+        pair_forward(at, rel_ref, near_ref, q_ref, k_ref, v_ref, att_ref, lse_ref)
+
+    def pairs(u, carry):
+        gather(u).end()
+        gather(u).arrive()
+
+        pair(2 * u, held[u, 0])
+
+        @pl.when(u + 2 <= units)
+        def _():
+            gather(u + 2).spread()
+
+        moves.forward(u, 1)
+
+        @pl.when(u + 2 < local)
+        def _():
+            moves.start(u + 2, 1)
+
+        moves.forward(u + 1, 0)
+        pair(2 * u + 1, held[u, 1])
+
+        @pl.when(u + 2 <= units)
+        def _():
+            gather(u + 2).forward()
+
+        moves.pass_on(u)
+        return carry
+
+    lax.fori_loop(0, units, pairs, 0)
+    gather(units).end()
+    moves.forward(local - 1, 1)
+    gather(units).arrive()
+    weights_copy = pltpu.make_async_copy(held, weights_out, weight_s.at[0])
+    weights_copy.start()
+    mixed = tokens_again(x_ref) + jnp.concatenate(
+        [dot_nn(att_ref[...], held[units, half].reshape(width, width // 2)) for half in range(2)], axis=1
+    )
+    mixed_ref[...] = mixed
+    normed_2 = (mixed * inverse_rms(mixed) * gains_out[1:2, :]).astype(BF16)
+    normed_f[...] = normed_2
+    sent_ref[...] = slot_rows(slot_row, normed_2, total).reshape(sent_ref.shape)
+    moves.pass_on(local - 1)
+    for copy in swap_copies():
+        copy.wait_send()
+    small_gather.drain()
+    for u in range(units + 1):
+        gather(u).drain()
+    for e in range(local):
+        moves.arrive(e)
+        moves.drain(e)
+    weights_copy.wait()
+
+
+def tokens_again(x_ref):
+    return x_ref[...].astype(F32)
+
+
+def moving_forward(
+    rel_bias, capacity, inputs, w_query, w_key, w_value, w_output, w_router, gain_attn, gain_ffn, near, routes, cotangent,
+    wide, narrow, local, slots,
+):
+    count, width = inputs.shape
+    experts = w_router.shape[1]
+    shard = w_query.shape[0]
+    deep, units = wide // 2, HEADS // 4
+    half = width // 2
+    sds = jax.ShapeDtypeStruct
+    rows_t = lambda dtype, cols=width: sds((count, cols), dtype)
+    smem, any_spec = pl.BlockSpec(memory_space=pltpu.SMEM), pl.BlockSpec(memory_space=pl.ANY)
+    vmem = lambda *shape, dtype=BF16: pltpu.VMEM(shape, dtype)
+    dma = pltpu.SemaphoreType.DMA
+    small = jnp.concatenate(
+        [w_router, gain_attn[:, None], gain_ffn[:, None], jnp.zeros((shard, BLOCK - experts - 2), BF16)], axis=1
+    )
+    return pl.pallas_call(
+        moving_forward_kernel,
+        out_shape=(
+            rows_t(BF16), rows_t(BF16), rows_t(BF16), rows_t(BF16), rows_t(BF16), rows_t(F32, BLOCK), rows_t(F32),
+            rows_t(BF16), sds((wide, local, slots, width), BF16), sds((count, 1), jnp.int32),
+            sds((width, experts), BF16), sds((8, width), F32),
+            sds((units + 1, 2, deep, 2, 2, 2 * shard, half), BF16),
+            sds((local, narrow, wide, slots, width), BF16),
+        ),
+        in_specs=[smem, smem] + in_vmem(10),
+        out_specs=tuple(in_vmem(12)) + (any_spec, any_spec),
+        scratch_shapes=[
+            vmem(units + 1, 2, deep, 2, 2, 2 * shard, half), vmem(1, deep, 2, 2, 2 * shard, BLOCK),
+            vmem(1, units + 1, shard, half), vmem(1, units + 1, shard, half), vmem(shard, BLOCK),
+            vmem(wide, local, slots, width), dma((1 + local,)), dma((2,)), dma((2,)),
+            dma((units + 1, 10)), dma((units + 1, 10)), dma((1, 10)), dma((1, 10)),
+            dma((local, wide)), dma((local, wide)), dma((local, 2)), dma((local, 2)), dma((local, 4)), dma((local, 4)),
+        ],
+        compiler_params=pltpu.CompilerParams(collective_id=1, has_side_effects=True, vmem_limit_bytes=62 << 20),
+        name="forward",
+    )(
+        rel_bias, capacity, inputs, w_query, w_key, w_value, w_output, small, near, routes, routes.reshape(1, count),
+        cotangent,
+    )
 
 
 def moving_expert_kernel(
     sent, cot_hbm, in_hbm, out_hbm, router_ref,
     rows_o, sg_o, hidden_o, gpre_o, outs_o, back_o, gate_o,
-    held, cot, w_in, w_out, sg, hidden, gpre, outs, to_core, from_core, to_side, from_side, near_sum, ready,
+    held, cot, w_in, w_out, sg, hidden, gpre, outs, to_core, from_core, from_side, near_sum,
     gate_sum, gate_core, gate_from_core, gate_side, gate_from_side, gate_ready,
     load_s, store_s, wide_s, wide_r, side_s, side_r, core_s, core_r,
     rc_s, rc_r, rx_s, rx_r, rw_s, rw_r, gc_s, gc_r, gx_s, gx_r, gw_s, gw_r,
@@ -332,8 +663,9 @@
     p = Place(wide)
     moves = Spread(p, sent, held, wide_s, wide_r, side_s, side_r, core_s, core_r)
     greet(p.partners())
-    for e in range(local):
-        moves.start(e)
+    moves.start(0, 1)
+    moves.start(0, 0)
+    moves.start(1, 0)
 
     def loads(e):
         return [
@@ -357,7 +689,14 @@
             copy.start()
         held[e, p.n, p.w] = sent[p.w, e]
     gate_sum[...] = jnp.zeros_like(gate_sum)
-    moves.forward(0)
+    moves.forward(0, 0)
+    moves.forward(1, 0)
+    moves.start(1, 1)
+    moves.start(2, 0)
+    moves.forward(0, 1)
+    moves.start(2, 1)
+    moves.start(3, 0)
+    moves.forward(2, 0)
     moves.pass_on(0)
 
     def chunk(e, m):
@@ -381,7 +720,7 @@
         gpre_rows = (dot_nt(sg_rows, w_out[e]) * slope).astype(BF16)
         gpre[b, m] = gpre_rows
         out_rows = dot_nn(hidden_rows, w_out[e])
-        outs[b, m] = out_rows.astype(BF16)
+        outs[b, m] = out_rows.astype(BF16).reshape(wide, slots, width)
         gate_rows = jnp.sum(out_rows * cot_rows, axis=-1, keepdims=True)
         row = lax.broadcasted_iota(jnp.int32, (step, local * slots), 0)
         lane = lax.broadcasted_iota(jnp.int32, (step, local * slots), 1)
@@ -389,21 +728,12 @@
         gate_sum[m] += jnp.sum(spread.reshape(wide, slots, local * slots), axis=1)
         return dot_nt(gpre_rows, w_in[e])
 
-    def core_copy(e, far):
-        return remote(to_core.at[e, far], from_core.at[e, far], rc_s.at[e, far], rc_r.at[e, far], p.core)
-
-    def side_copy(e):
-        return remote(to_side.at[e], from_side.at[e], rx_s.at[e], rx_r.at[e], p.side)
-
-    def back_copy(e, k):
-        return remote(ready.at[e, p.at(k)], back_o.at[p.w, e], rw_s.at[e, k], rw_r.at[e, k], p.peer(k))
-
-    def finish(e):
-        side_copy(e).wait_recv()
-        ready[e] = (near_sum[...] + from_side[e].astype(F32)).astype(BF16).reshape(wide, slots, width)
-        for k in range(1, wide):
-            back_copy(e, k).start()
-        back_o[p.w, e] = ready[e, p.w]
+    back = Collect(
+        p, lambda e, other: to_core.at[e, other], from_core, from_side, back_o, (rc_s, rc_r, rx_s, rx_r, rw_s, rw_r)
+    )
+
+    def own_sums(rows):
+        return near_sum[rows]
 
     far_x = (1 - p.x) * 2
 
@@ -417,32 +747,38 @@
                 copy.wait()
 
         moves.arrive(e)
-        to_core[e, 1] = chunk(e, far_x + 1 - p.c).astype(BF16)
-        core_copy(e, 1).start()
+        to_core[e, 1] = chunk(e, far_x + 1 - p.c).astype(BF16).reshape(wide, slots, width)
+        back.core(e, 1).start()
 
         @pl.when(e + 1 < local)
         def _():
-            moves.forward(e + 1)
-
-        far_part = chunk(e, far_x + p.c)
-        core_copy(e, 1).wait_recv()
-        to_side[e] = (far_part + from_core[e, 1].astype(F32)).astype(BF16)
-        side_copy(e).start()
+            moves.forward(e + 1, 1)
+
+        @pl.when(e + 3 < local)
+        def _():
+            moves.start(e + 3, 1)
+
+        back.go_beside(e, chunk(e, far_x + p.c))
 
         @pl.when(e > 0)
         def _():
-            finish(e - 1)
-
-        to_core[e, 0] = chunk(e, p.x * 2 + 1 - p.c).astype(BF16)
-        core_copy(e, 0).start()
+            back.finish(e - 1, 1, own_sums)
+            back.finish(e - 1, 0, own_sums)
+
+        to_core[e, 0] = chunk(e, p.x * 2 + 1 - p.c).astype(BF16).reshape(wide, slots, width)
+        back.core(e, 0).start()
 
         @pl.when(e + 1 < local)
         def _():
             moves.pass_on(e + 1)
 
+        @pl.when(e + 3 < local)
+        def _():
+            moves.forward(e + 3, 0)
+
         near_part = chunk(e, p.n)
-        core_copy(e, 0).wait_recv()
-        near_sum[...] = near_part + from_core[e, 0].astype(F32)
+        back.core(e, 0).wait_recv()
+        near_sum[...] = near_part.reshape(wide, slots, width) + from_core[e, 0].astype(F32)
         for copy in stores(e):
             copy.start()
         return carry
@@ -456,13 +792,14 @@
     gate_side[...] = gate_sum[far_x + p.c] + gate_from_core[1]
     gates_side = remote(gate_side, gate_from_side, gx_s, gx_r, p.side)
     gates_side.start()
-    finish(local - 1)
+    back.finish(local - 1, 1, own_sums)
+    back.finish(local - 1, 0, own_sums)
     gates_side.wait_recv()
     gates = gate_sum[p.n] + gate_from_core[0] + gate_from_side[...]
     for v in range(wide):
         gate_ready[v] = gates[v : v + 1, :]
     gates_wide = [
-        remote(gate_ready.at[p.at(k)], gate_o.at[p.w], gw_s.at[k], gw_r.at[k], p.peer(k)) for k in range(1, wide)
+        remote(gate_ready.at[p.flip(j)], gate_o.at[p.w], gw_s.at[j], gw_r.at[j], p.peer(j)) for j in range(1, wide)
     ]
     for copy in gates_wide:
         copy.start()
@@ -472,9 +809,8 @@
 
     def drain(e, carry):
         moves.drain(e)
-        core_copy(e, 0).wait_send()
-        core_copy(e, 1).wait_send()
-        side_copy(e).wait_send()
+        back.drain(e)
+        back.arrive(e)
         stores(e)[0].wait()
 
         @pl.when(e >= local - 2)
@@ -482,8 +818,6 @@
             for copy in stores(e)[1:]:
                 copy.wait()
 
-        for k in range(1, wide):
-            back_copy(e, k).wait()
         return carry
 
     lax.fori_loop(0, local, drain, 0)
@@ -510,7 +844,7 @@
             sds((local, narrow, step, width), BF16),
             sds((local, narrow, step, hidden_width), BF16),
             sds((local, narrow, step, hidden_width), BF16),
-            sds((local, narrow, step, width), BF16),
+            sds((local, narrow, wide, slots, width), BF16),
             sds((wide, local, slots, width), BF16),
             sds((wide, 1, local * slots), F32),
         ),
@@ -524,13 +858,11 @@
             pltpu.VMEM((2, narrow, step, width), BF16),
             pltpu.VMEM((2, narrow, step, hidden_width), BF16),
             pltpu.VMEM((2, narrow, step, hidden_width), BF16),
-            pltpu.VMEM((2, narrow, step, width), BF16),
-            pltpu.VMEM((local, 2, step, width), BF16),
-            pltpu.VMEM((local, 2, step, width), BF16),
-            pltpu.VMEM((local, step, width), BF16),
-            pltpu.VMEM((local, step, width), BF16),
-            pltpu.VMEM((step, width), F32),
+            pltpu.VMEM((2, narrow, wide, slots, width), BF16),
+            pltpu.VMEM((local, 2, wide, slots, width), BF16),
+            pltpu.VMEM((local, 2, wide, slots, width), BF16),
             pltpu.VMEM((local, wide, slots, width), BF16),
+            pltpu.VMEM((wide, slots, width), F32),
             pltpu.VMEM((narrow, wide, local * slots), F32),
             pltpu.VMEM((2, wide, local * slots), F32),
             pltpu.VMEM((2, wide, local * slots), F32),
@@ -538,8 +870,8 @@
             pltpu.VMEM((wide, local * slots), F32),
             pltpu.VMEM((wide, 1, local * slots), F32),
             dma((local, 3)), dma((local, 5)), dma((local, wide)), dma((local, wide)),
-            dma((local, 2)), dma((local, 2)), dma((local, 2)), dma((local, 2)),
-            dma((local, 2)), dma((local, 2)), dma((local,)), dma((local,)), dma((local, wide)), dma((local, wide)),
+            dma((local, 2)), dma((local, 2)), dma((local, 4)), dma((local, 4)),
+            dma((local, 2)), dma((local, 2)), dma((local, 2)), dma((local, 2)), dma((local, wide)), dma((local, wide)),
             dma, dma, dma, dma, dma((wide,)), dma((wide,)),
         ],
         compiler_params=pltpu.CompilerParams(
@@ -703,27 +1035,40 @@
 class Sums:
     def __init__(self, place, unit, buffers, semaphores, out):
         self.p, self.unit, self.out = place, unit, out
-        self.send, self.core, self.kept, self.from_y, self.over_x, self.from_x, self.over_z, self.from_z, self.last = buffers
+        self.send, self.core, self.first_in, self.second_in, self.z_in, self.last = buffers
         self.s, self.r = semaphores
-        self.deep = self.send.shape[1]
+        self.deep = place.deep
+        p, c = place, place.c
+        self.first, self.second = p.y + c * (p.x - p.y), p.x + c * (p.y - p.x)
+        row, side = p.row, p.side
+        self.first_peer = tuple(a + c * (b - a) for a, b in zip(row, side))
+        self.second_peer = tuple(b + c * (a - b) for a, b in zip(row, side))
+
+    def store(self, buffer, part, core):
+        rows, cols = buffer.shape[-2:]
+        blocks = part.reshape(self.deep, 2, 2, rows, cols)
+        for y in range(2):
+            for x in range(2):
+                first, second = (y, x) if y == x else (y + core * (x - y), x + core * (y - x))
+                buffer[self.unit, first, second] = blocks[:, y, x].astype(buffer.dtype)
 
     def to_core(self):
         u, p = self.unit, self.p
         return remote(self.send.at[u], self.core.at[u], self.s.at[u, 0], self.r.at[u, 0], p.core)
 
     def to_y(self):
-        u, p = self.unit, self.p
-        return remote(self.kept.at[u, 1 - p.y], self.from_y.at[u], self.s.at[u, 1], self.r.at[u, 1], p.row)
+        u = self.unit
+        return remote(self.core.at[u, 1 - self.first], self.first_in.at[u], self.s.at[u, 1], self.r.at[u, 1], self.first_peer)
 
     def to_x(self):
-        u, p = self.unit, self.p
-        return remote(self.over_x.at[u, 1 - p.x], self.from_x.at[u], self.s.at[u, 2], self.r.at[u, 2], p.side)
+        u = self.unit
+        return remote(self.first_in.at[u, 1 - self.second], self.second_in.at[u], self.s.at[u, 2], self.r.at[u, 2], self.second_peer)
 
     def to_z(self, k):
         u, p = self.unit, self.p
         z = lax.rem(p.z + k, p.deep)
         return remote(
-            self.over_z.at[u, z], self.from_z.at[u, k], self.s.at[u, 3 + k], self.r.at[u, 3 + k], (z * 2 + p.y, p.n)
+            self.second_in.at[u, z], self.z_in.at[u, k], self.s.at[u, 3 + k], self.r.at[u, 3 + k], (z * 2 + p.y, p.n)
         )
 
     def to_last(self):
@@ -731,35 +1076,41 @@
         return remote(self.last.at[u, 1 - p.c], self.out.at[u, p.c], self.s.at[u, 3], self.r.at[u, 3], p.core)
 
     def begin(self, part):
-        self.send[self.unit] = part.astype(BF16).reshape(self.send.shape[1:])
+        self.store(self.send, part, 1 - self.p.c)
         self.to_core().start()
 
     def stage_core(self, part):
         u = self.unit
         self.to_core().wait_recv()
-        kept = part.reshape(self.core.shape[1:]) + self.core[u].astype(F32)
-        self.kept[u] = kept.astype(BF16)
+        rows, cols = self.core.shape[-2:]
+        blocks = part.reshape(self.deep, 2, 2, rows, cols)
+        c = self.p.c
+        for y in range(2):
+            for x in range(2):
+                first, second = (y, x) if y == x else (y + c * (x - y), x + c * (y - x))
+                kept = blocks[:, y, x] + self.core[u, first, second].astype(F32)
+                self.core[u, first, second] = kept.astype(BF16)
         self.to_y().start()
 
     def stage_y(self):
         u = self.unit
         self.to_y().wait_recv()
-        self.over_x[u] = (self.kept[u, self.p.y].astype(F32) + self.from_y[u].astype(F32)).astype(BF16)
+        self.first_in[u] = (self.core[u, self.first].astype(F32) + self.first_in[u].astype(F32)).astype(BF16)
         self.to_x().start()
 
     def stage_x(self):
         u = self.unit
         self.to_x().wait_recv()
-        self.over_z[u] = (self.over_x[u, self.p.x].astype(F32) + self.from_x[u].astype(F32)).astype(BF16)
+        self.second_in[u] = (self.first_in[u, self.second].astype(F32) + self.second_in[u].astype(F32)).astype(BF16)
         for k in range(1, self.p.deep):
             self.to_z(k).start()
 
     def stage_z(self):
         u = self.unit
-        total = self.over_z[u, self.p.z].astype(F32)
+        total = self.second_in[u, self.p.z].astype(F32)
         for k in range(1, self.p.deep):
             self.to_z(k).wait_recv()
-            total = total + self.from_z[u, k].astype(F32)
+            total = total + self.z_in[u, k].astype(F32)
         self.last[u] = total.reshape(self.last.shape[1:])
         self.to_last().start()
         self.out[u, self.p.c] = self.last[u, self.p.c]
@@ -776,68 +1127,73 @@
     deep = wide // 2
     vmem = lambda *shape, dtype=BF16: pltpu.VMEM((units, *shape), dtype)
     return [
-        vmem(2, 2, deep, rows, cols), vmem(2, 2, deep, rows, cols), vmem(2, 2, deep, rows, cols),
-        vmem(2, deep, rows, cols), vmem(2, deep, rows, cols), vmem(deep, rows, cols), vmem(deep, rows, cols),
+        vmem(2, 2, deep, rows, cols), vmem(2, 2, deep, rows, cols), vmem(2, deep, rows, cols), vmem(deep, rows, cols),
         vmem(deep, rows, cols), vmem(2, rows // 2, cols, dtype=F32),
         pltpu.SemaphoreType.DMA((units, 3 + deep)), pltpu.SemaphoreType.DMA((units, 3 + deep)),
     ]
 
 
 def moving_backward_kernel(
-    rel_ref, x_ref, w_ref, gain_a, gain_f, router_ref, near_ref, slot_col, routes_ref,
-    normed_ref, q_ref, k_ref, v_ref, att_ref, lse_ref, mixed_ref, normed_f, cot_ref, outs_hbm, grows_ref, gates_ref, picks_ref,
+    rel_ref, x_hbm, w_hbm, normed_hbm, q_hbm, k_hbm, v_hbm, att_hbm, lse_hbm, outs_hbm,
+    gains_ref, router_ref, near_ref, slot_col, routes_ref, mixed_ref, normed_f, cot_ref, grows_ref, gates_ref, picks_ref,
     result_ref, gx_ref, gw_out, go_out, small_out,
-    q_t, k_t, normed_t, datt, datt_t, delta, lse_t, gq, gk, gv, gmixed, dst, gnear, gfar,
-    own, from_core, to_side, from_side, near_sum, ready, returned, own_s, rc_s, rc_r, rx_s, rx_r, rw_s, rw_r,
-    u1, u2, u3, u4, u5, u6, u7, u8, u9, us, ur, o1, o2, o3, o4, o5, o6, o7, o8, o9, os, orr,
+    x_ref, w_ref, normed_ref, q_ref, k_ref, v_ref, att_ref, lse_ref, load_s,
+    q_t, k_t, normed_t, datt, datt_t, delta, lse_t, gq, gk, gv, gmixed, gnormed, dst, gnear, gfar,
+    own, from_core, from_side, returned, own_s, rc_s, rc_r, rx_s, rx_r, rw_s, rw_r,
+    u1, u2, u3, u4, u5, u6, us, ur, o1, o2, o3, o4, o5, o6, os, orr,
     small, small_in, ss, sr,
 ):
-    count, width = x_ref.shape
-    local, _, step, _ = outs_hbm.shape
-    wide, _, slots, _ = returned.shape
+    count, width = x_hbm.shape
+    wide, local, slots, _ = returned.shape
     total = wide * local * slots
     p = Place(wide)
     far_x = (1 - p.x) * 2
+    units = HEADS // 4
+    gain_a, gain_f = gains_ref.at[0:1, :], gains_ref.at[1:2, :]
+    loads = [
+        pltpu.make_async_copy(source, target, load_s.at[at])
+        for at, (source, target) in enumerate((
+            (att_hbm, att_ref), (w_hbm, w_ref), (q_hbm, q_ref), (k_hbm, k_ref), (normed_hbm, normed_ref),
+            (lse_hbm, lse_ref), (v_hbm, v_ref), (x_hbm, x_ref),
+        ))
+    ]
+
+    def partial(e, other, core):
+        return outs_hbm.at[e, (far_x if other else p.x * 2) + core]
+
+    back = Collect(
+        p, lambda e, other: partial(e, other, 1 - p.c), from_core, from_side, returned, (rc_s, rc_r, rx_s, rx_r, rw_s, rw_r)
+    )
+
+    def own_copy(e, other):
+        return pltpu.make_async_copy(partial(e, other, p.c), own.at[e, other], own_s.at[e, other])
+
+    for other in (1, 0):
+        for e in range(local):
+            own_copy(e, other).start()
+    for copy in loads:
+        copy.start()
     greet(p.partners())
-
-    def core_copy(e, far):
-        m = (far_x if far else p.x * 2) + 1 - p.c
-        return remote(outs_hbm.at[e, m], from_core.at[e, far], rc_s.at[e, far], rc_r.at[e, far], p.core)
-
-    def own_copy(e, far):
-        m = (far_x if far else p.x * 2) + p.c
-        return pltpu.make_async_copy(outs_hbm.at[e, m], own.at[e, far], own_s.at[e, far])
-
-    def side_copy(e):
-        return remote(to_side.at[e], from_side.at[e], rx_s.at[e], rx_r.at[e], p.side)
-
-    def back_copy(e, k):
-        return remote(ready.at[e, p.at(k)], returned.at[p.w, e], rw_s.at[e, k], rw_r.at[e, k], p.peer(k))
-
-    for far in (1, 0):
+    for other in (1, 0):
         for e in range(local):
-            core_copy(e, far).start()
-            own_copy(e, far).start()
+            back.core(e, other).start()
 
     def over_side(e):
-        core_copy(e, 1).wait_recv()
         own_copy(e, 1).wait()
-        to_side[e] = (own[e, 1].astype(F32) + from_core[e, 1].astype(F32)).astype(BF16)
-        side_copy(e).start()
-
-    def nearby(e):
-        core_copy(e, 0).wait_recv()
+        back.go_beside(e, own[e, 1])
+
+    def finish(e):
+        back.core(e, 0).wait_recv()
         own_copy(e, 0).wait()
-        near_sum[e] = own[e, 0].astype(F32) + from_core[e, 0].astype(F32)
-
-    def finish(e):
-        side_copy(e).wait_recv()
-        ready[e] = (near_sum[e] + from_side[e].astype(F32)).astype(BF16).reshape(wide, slots, width)
-        for k in range(1, wide):
-            back_copy(e, k).start()
-        returned[p.w, e] = ready[e, p.w]
+
+        def own_sums(rows):
+            return own[e, 0, rows].astype(F32) + from_core[e, 0, rows].astype(F32)
+
+        back.finish(e, 1, own_sums)
+        back.finish(e, 0, own_sums)
 
     probs, chosen, gate = routed_gate(normed_f, router_ref, routes_ref)
+    over_side(0)
     owned = slot_owners(slot_col, total)
     grad_router, grad_mixed, grad_gain_f = ffn_backward(
         probs, chosen, gate, owned, gates_ref, normed_f, router_ref, grows_ref, mixed_ref[...], cot_ref, gain_f
@@ -845,10 +1201,10 @@
     gmixed[...] = grad_mixed
     small[0] = jnp.zeros_like(small[0])
     small[0, HEADS : HEADS + 1, :] = grad_gain_f
-    for e in range(local):
-        over_side(e)
+    over_side(1)
+    loads[0].wait()
     branch = grad_mixed.astype(BF16)
-    o_sums = Sums(p, 0, (o1, o2, o3, o4, o5, o6, o7, o8, o9), (os, orr), go_out)
+    o_sums = Sums(p, 0, (o1, o2, o3, o4, o5, o6), (os, orr), go_out)
     half_cols = width // 2
     router_cols = go_out.shape[-1] - half_cols
     router_wide = jnp.concatenate(
@@ -858,13 +1214,16 @@
     def output_part(core):
         low, high = branch[:, :half_cols], branch[:, half_cols:]
         part = dot_tn(att_ref[...], jnp.where(core == 0, low, high))
-        return order_rows(jnp.concatenate([part, jnp.where(core == 0, router_wide, 0.0)], axis=1), p)
+        return jnp.concatenate([part, jnp.where(core == 0, router_wide, 0.0)], axis=1)
 
     o_sums.begin(output_part(1 - p.c))
-    datt[...] = dot_nt(branch, w_ref[:, 3 * width : 4 * width]).astype(BF16)
-    for e in range(local):
-        nearby(e)
+    loads[1].wait()
+    datt[...] = (
+        dot_nt(branch[:, :half_cols], w_ref[units, 0]) + dot_nt(branch[:, half_cols:], w_ref[units, 1])
+    ).astype(BF16)
     o_sums.stage_core(output_part(p.c))
+    for copy in loads[2:]:
+        copy.wait()
     attention_setup(q_ref, k_ref, normed_ref, att_ref, lse_ref, datt, q_t, k_t, normed_t, datt_t, delta, lse_t)
 
     def pair(at):
@@ -874,12 +1233,15 @@
         )
         cols = pl.ds(pl.multiple_of(at * BLOCK, BLOCK), BLOCK)
         grads = jnp.concatenate([gq[:, cols], gk[:, cols], gv[:, cols]], axis=1)
-        return order_rows(dot_nn(normed_t[...], grads), p)
+        gnormed[...] += dot_nt(grads, w_ref[at // 2, lax.rem(at, 2)])
+        return dot_nn(normed_t[...], grads)
 
     def unit(u):
-        return Sums(p, u, (u1, u2, u3, u4, u5, u6, u7, u8, u9), (us, ur), gw_out)
-
-    units = HEADS // 4
+        return Sums(p, u, (u1, u2, u3, u4, u5, u6), (us, ur), gw_out)
+
+    gnormed[...] = jnp.zeros_like(gnormed)
+    finish(0)
+    over_side(2)
 
     def pairs(u, carry):
         unit(u).begin(pair(2 * u + 1 - p.c))
@@ -890,26 +1252,26 @@
 
         @pl.when(u == 1)
         def _():
+            o_sums.stage_x()
+
+        @pl.when(u == 2)
+        def _():
             o_sums.stage_z()
+
+        unit(u).stage_core(pair(2 * u + p.c))
+        finish(u + 1)
+
+        @pl.when(u + 3 < local)
+        def _():
+            over_side(u + 3)
 
         @pl.when(u >= 1)
         def _():
             unit(u - 1).stage_y()
-            finish(u - 1)
 
         @pl.when(u >= 2)
         def _():
-            unit(u - 2).stage_z()
-
-        unit(u).stage_core(pair(2 * u + p.c))
-
-        @pl.when(u == 0)
-        def _():
-            o_sums.stage_x()
-
-        @pl.when(u >= 1)
-        def _():
-            unit(u - 1).stage_x()
+            unit(u - 2).stage_x()
 
         return carry
 
@@ -921,7 +1283,9 @@
     bucket_count = rel_ref.shape[0]
     rel = near_grads + jnp.where(buckets == bucket_count // 2 - 1, low_sum, 0.0)
     small[0, :HEADS, :BLOCK] = rel + jnp.where(buckets == bucket_count - 1, high_sum, 0.0)
-    gx_ref[...], grad_gain_a = input_backward(x_ref, w_ref, gain_a, gmixed, gq, gk, gv)
+    tokens = x_ref[...].astype(F32)
+    grad_norm, grad_gain_a = norm_backward(tokens, inverse_rms(tokens), gain_a[...], gnormed[...])
+    gx_ref[...] = gmixed[...] + grad_norm
     small[0, HEADS + 1 : HEADS + 2, :] = grad_gain_a
 
     def small_copy(stage, device, slot):
@@ -948,29 +1312,24 @@
     small_start(0)
     last = unit(units - 1)
     last.stage_y()
-    for e in range(units - 1, local):
-        finish(e)
+    unit(units - 2).stage_x()
     small[1] = small_end(0)
     small_start(1)
-    unit(units - 2).stage_z()
-    last.stage_x()
+    unit(units - 3).stage_z()
     small[2] = small_end(1)
     small_start(2)
+    last.stage_x()
+    unit(units - 2).stage_z()
     small[3] = small_end(2)
     small_start(3)
+    for e in range(local):
+        back.arrive(e)
+    combined = dot_nn(owned.astype(BF16), returned[...].reshape(total, width))
+    result_ref[...] = (mixed_ref[...] + gate * combined).astype(BF16)
     last.stage_z()
     small_out[...] = small_end(3)
     for e in range(local):
-        for k in range(1, wide):
-            back_copy(e, k).wait_recv()
-    combined = dot_nn(owned.astype(BF16), returned[...].reshape(total, width))
-    result_ref[...] = (mixed_ref[...] + gate * combined).astype(BF16)
-    for e in range(local):
-        core_copy(e, 0).wait_send()
-        core_copy(e, 1).wait_send()
-        side_copy(e).wait_send()
-        for k in range(1, wide):
-            back_copy(e, k).wait_send()
+        back.drain(e)
     o_sums.drain()
     for u in range(units):
         unit(u).drain()
@@ -979,19 +1338,12 @@
             copy.wait_send()
 
 
-def order_rows(part, place):
-    width, cols = part.shape
-    rows = width // (place.deep * 4)
-    blocks = part.reshape(place.deep, 2, 2, rows, cols)
-    return jnp.transpose(blocks, (1, 2, 0, 3, 4)).reshape(width, cols)
-
-
 def moving_backward(
-    rel_bias, inputs, weights, gain_a, gain_f, router, near, slot_col, routes,
+    rel_bias, inputs, weights, gains, router, near, slot_col, routes,
     normed, q, k, v, att, lse, mixed, normed_f, cotangent, outs, grows, gates, wide, slots,
 ):
     count, width = inputs.shape
-    local, narrow, step, _ = outs.shape
+    local, narrow = outs.shape[:2]
     experts = router.shape[1]
     bucket_count = rel_bias.shape[0]
     deep, rows = wide // 2, width // (wide * 2)
@@ -1013,16 +1365,18 @@
             sds((count, width), BF16), sds((count, width), F32), sds((units, 2, rows // 2, pair_cols), F32),
             sds((1, 2, rows // 2, out_cols), F32), sds((16, width), F32),
         ),
-        in_specs=[smem] + in_vmem(17) + [any_spec] + in_vmem(3),
+        in_specs=[smem] + [any_spec] * 9 + in_vmem(11),
         out_specs=tuple(in_vmem(5)),
         scratch_shapes=[
+            tall(BF16), pltpu.VMEM(weights.shape, BF16), tall(BF16), tall(BF16), tall(BF16), tall(BF16), tall(BF16),
+            vmem(count, BLOCK, dtype=F32), dma((8,)),
             wide_t(BF16), wide_t(BF16), wide_t(BF16), tall(BF16), wide_t(BF16),
             vmem(HEADS, count, dtype=F32), vmem(BLOCK, count, dtype=F32),
-            tall(BF16), tall(BF16), tall(BF16), tall(F32), vmem(count, count),
+            tall(BF16), tall(BF16), tall(BF16), tall(F32), tall(F32), vmem(count, count),
             vmem(HEADS, 4 * BLOCK, dtype=F32), vmem(HEADS, 2 * BLOCK, dtype=F32),
-            vmem(local, 2, step, width), vmem(local, 2, step, width), vmem(local, step, width), vmem(local, step, width),
-            vmem(local, step, width, dtype=F32), vmem(local, wide, slots, width), vmem(wide, local, slots, width),
-            dma((local, 2)), dma((local, 2)), dma((local, 2)), dma((local,)), dma((local,)),
+            vmem(local, 2, wide, slots, width), vmem(local, 2, wide, slots, width), vmem(local, wide, slots, width),
+            vmem(wide, local, slots, width),
+            dma((local, 2)), dma((local, 2)), dma((local, 2)), dma((local, 2)), dma((local, 2)),
             dma((local, wide)), dma((local, wide)),
             *sum_buffers(units, wide, rows, pair_cols), *sum_buffers(1, wide, rows, out_cols),
             vmem(4, 16, width, dtype=F32), vmem(hops, 16, width, dtype=F32), dma((hops,)), dma((hops,)),
@@ -1030,8 +1384,8 @@
         compiler_params=pltpu.CompilerParams(collective_id=3, has_side_effects=True, vmem_limit_bytes=62 << 20),
         name="backward",
     )(
-        rel_bias, inputs, weights, gain_a, gain_f, router, near, slot_col, routes,
-        normed, q, k, v, att, lse, mixed, normed_f, cotangent, outs, grows, gates, jnp.asarray(picks),
+        rel_bias, inputs, weights, normed, q, k, v, att, lse, outs,
+        gains, router, near, slot_col, routes, mixed, normed_f, cotangent, grows, gates, jnp.asarray(picks),
     )
     kinds = [
         jnp.transpose(gw[..., at * BLOCK : (at + 1) * BLOCK], (2, 0, 1, 3)).reshape(rows // 2, width) for at in range(3)
@@ -1039,9 +1393,9 @@
     grad_output = jnp.transpose(go[0, :, :, : width // 2], (1, 0, 2)).reshape(rows // 2, width)
     grad_router = go[0, 0, :, width // 2 : width // 2 + experts]
     device = lax.axis_index("wide") * narrow + lax.axis_index("narrow")
-    gains = lax.dynamic_slice(small, (HEADS, device * (rows // 2)), (2, rows // 2))
+    gain_grads = lax.dynamic_slice(small, (HEADS, device * (rows // 2)), (2, rows // 2))
     grad_rel = small[:HEADS, :bucket_count].T
-    return result, grad_inputs, kinds, grad_output, grad_router, gains[1], gains[0], grad_rel
+    return result, grad_inputs, kinds, grad_output, grad_router, gain_grads[1], gain_grads[0], grad_rel
 
 
 def in_vmem(count):
@@ -1062,6 +1416,26 @@
     params = pltpu.CompilerParams(vmem_limit_bytes=60 << 20)
     smem = pl.BlockSpec(memory_space=pltpu.SMEM)
 
+    near = jnp.dot(near_picks(bucket_count, 1), rel_bias, precision=HIGHEST).T
+    near_back = jnp.dot(near_picks(bucket_count, -1), rel_bias, precision=HIGHEST).T
+
+    moving = narrow == 4 and wide & (wide - 1) == 0 and local == HEADS // 4 + 1 and slots % 16 == 0 and local * slots % BLOCK == 0
+    moving = moving and width % (wide * 2 * 16) == 0 and count == SEQ_LEN and experts + 8 <= BLOCK
+    if moving:
+        normed, q, k, v, att, lse, mixed, normed_f, sent, slot_col, router, gains, weights, cot_all = moving_forward(
+            rel_bias, capacity, inputs, w_query, w_key, w_value, w_output, w_router, gain_attn, gain_ffn, near, routes,
+            cotangent, wide, narrow, local, slots,
+        )
+        outs, back, gates, gin, gout = moving_experts(sent, cot_all, expert_in, expert_out, router, wide, narrow)
+        result, grad_inputs, kinds, grad_output, grad_router, grad_gain_a, grad_gain_f, grad_rel = moving_backward(
+            rel_bias, inputs, weights.reshape(HEADS // 4 + 1, 2, width, width // 2), gains, router, near_back,
+            slot_col, routes, normed, q, k, v, att, lse, mixed, normed_f, cotangent, outs,
+            back.reshape(total, width), gates.reshape(1, total), wide, slots,
+        )
+        return (
+            result, grad_inputs, grad_gain_a, *kinds, grad_output, grad_rel, grad_gain_f, grad_router, gin, gout,
+        )
+
     packed = jnp.concatenate([w_query, w_key, w_value, w_output], axis=1)
     weights = lax.all_gather(packed, BOTH, axis=0, tiled=True)
     small = lax.all_gather(
@@ -1070,9 +1444,6 @@
     router = small[:, :experts]
     gain_a = small[:, experts].astype(F32)[None, :]
     gain_f = small[:, experts + 1].astype(F32)[None, :]
-    near = jnp.dot(near_picks(bucket_count, 1), rel_bias, precision=HIGHEST).T
-    near_back = jnp.dot(near_picks(bucket_count, -1), rel_bias, precision=HIGHEST).T
-
     slot_col, slot_row, cot_sent = pl.pallas_call(
         lambda *refs: place_kernel(slots, experts, *refs),
         out_shape=(
@@ -1114,23 +1485,6 @@
         compiler_params=params,
         name="forward",
     )(rel_bias, inputs, weights, gain_a, gain_f, router, near, slot_row)
-
-    moving = narrow == 4 and wide % 2 == 0 and slots % 16 == 0 and local * slots % BLOCK == 0
-    moving = moving and width % (wide * 2 * 16) == 0 and count == SEQ_LEN
-    if moving:
-        outs, back, gates, gin, gout = moving_experts(
-            sent.reshape(wide, local, slots, width),
-            jnp.moveaxis(cot_all.reshape(narrow, wide, local, slots, width), 2, 0),
-            expert_in, expert_out, router, wide, narrow,
-        )
-        result, grad_inputs, kinds, grad_output, grad_router, grad_gain_a, grad_gain_f, grad_rel = moving_backward(
-            rel_bias, inputs, weights, gain_a, gain_f, router, near_back, slot_col, routes,
-            normed, q, k, v, att, lse, mixed, normed_f, cotangent, outs, back.reshape(total, width),
-            gates.reshape(1, total), wide, slots,
-        )
-        return (
-            result, grad_inputs, grad_gain_a, *kinds, grad_output, grad_rel, grad_gain_f, grad_router, gin, gout,
-        )
 
     rows_all = spread(sent)
     sources = wide * narrow

time: 389 us -> 304 us (0.78)
  blocking collectives: 94.3 us -> 0 us
  Pallas kernels: 255 us -> 283 us
  between operations: 14.8 us -> 1.39 us
  local copies, waits for them, and re-layouts: 20.4 us -> 15.1 us
    pallas_call x2 -> x1, Pallas kernels: 29.8 us -> 86.6 us  [moving_forward(): pl.pallas_call(moving_forward_kernel, out_shape=(rows_t(BF16), rows_t(BF1...]
    all_to_all x1 -> x0, blocking collectives: 54 us -> none  [spread(): lax.all_to_all(rows.reshape(wide, local * slots, width), 'wide', split_ax...]
    all_gather x1 -> x0, blocking collectives: 40.3 us -> none  [shards(): lax.all_gather(jnp.concatenate([w_router, gain_attn[:, None], gain_ffn[:,...]
    pallas_call x1, Pallas kernels: 108 us -> 81.2 us  [moving_backward(): pl.pallas_call(moving_backward_kernel, out_shape=(sds((count, width), BF1...]
    another operation x1 -> x0, local copies, waits for them, and re-layouts: 6.22 us -> none  [shards(): cot_all.reshape(narrow, wide, local, slots, width)]
  transfers between devices with their start and end apart: 2 -> 0, of which waited for: 0 -> 0; matrix products, arithmetic and copies ran while one was open for 2% -> 0% of each run, Pallas kernels for 8% -> 0%
where the time goes in v4:
time: 304 us
  Pallas kernels  283 us (93%)
  local copies, waits for them, and re-layouts  15.1 us (5%)
    pallas_call x1, Pallas kernels, moving_experts(): pl.pallas_call(moving_expert_kernel, out_shape=(sds((local, narrow, wide,...  97.6 us
    pallas_call x1, Pallas kernels, moving_forward(): pl.pallas_call(moving_forward_kernel, out_shape=(rows_t(BF16), rows_t(BF1...  86.6 us
    pallas_call x1, Pallas kernels, moving_backward(): pl.pallas_call(moving_backward_kernel, out_shape=(sds((count, width), BF1...  81.2 us
    pallas_call x1, Pallas kernels, moving_experts(): pl.pallas_call(weight_grad_kernel, grid=(local,), out_shape=(sds(expert_i...  17.7 us

profile of v4, /device:TPU:0, one launch (start us, length us, event | category | flops | bytes accessed | tf_op | source)
XLA Modules:
  0.0 303.8 jit_solution(7754259512210283608)
XLA Ops:
  0.6 1.4 copy.39.rel_ref
  2.7 0.7 copy.36
  3.4 0.7 copy.35
  4.2 0.1 pad.3.clone
  4.3 1.4 maximum_maximum_fusion.small_part
  5.6 1.9 convolution_bitcast_fusion.1.near_ref
  7.5 1.5 copy.38.routes_ref
  9.1 86.6 %forward.1 = (bf16[512,768]{1,0:T(8,128)(2,1)}, bf16[512,768]{1,0:T(8,128)(2,1)}, bf16[512,768]{1,0:T(8,128)(2,1)}, bf16[512,768]{1,0:T(8,128)(2,1)}, bf16[512,7...) custom-call(f32[32,12]{1,0:T(8,128)} %copy.39.rel_ref, ...), custom_call_target="tpu_custom_call" | custom-call | tf_op jit(solution)/shard_map/forward/pallas_call | solution.py:626
  95.7 0.0 copy-start.2
  95.7 0.0 copy-start.3
  95.7 97.6 %experts.1 = (bf16[4,4,8,32,768]{4,3,2,1,0:T(8,128)(2,1)}, bf16[4,4,256,768]{3,2,1,0:T(8,128)(2,1)}, bf16[4,4,256,768]{3,2,1,0:T(8,128)(2,1)}, bf16[4,4,256,768]...) custom-call(bf16[8,4,32,768]{3,2,1,0:T(8,128)(2,1)} %get-tuple-eleme, ...), custom_call_target="tpu_custom_call" | custom-call | tf_op jit(solution)/shard_map/experts/pallas_call | solution.py:840
  193.3 0.0 copy-done.2
  193.3 0.0 copy-done.3
  193.3 1.0 convolution_bitcast_fusion.near_ref
  194.3 81.2 %backward.1 = (bf16[512,768]{1,0:T(8,128)(2,1)}, f32[512,768]{1,0:T(8,128)}, f32[3,2,24,384]{3,2,1,0:T(8,128)}, f32[1,2,24,512]{3,2,1,0:T(8,128)}, f32[16,768]{1,0:T(8,128)}) custom-call(f32[32,12]{1,0:T(8,128)} %copy.39.rel_ref, bf16[512,768]{1,0:T(8,128)(2,1)} %x_hbm.1, bf16[4,2,768,384]{3,2,1,0:T(8,128)(2,1)} %bitcast.42, ...), custom_call_target="tpu_custom_call" | custom-call | tf_op jit(solution)/shard_map/backward/pallas_call | solution.py:1362
  275.4 0.8 constant_dynamic-slice_fusion
  276.2 0.5 slice_bitcast_fusion.6
  276.7 1.0 slice_bitcast_fusion.1
  277.8 0.7 reshape.64
  278.5 0.7 reshape.65
  279.2 0.7 reshape.66
  279.9 0.9 slice_bitcast_fusion
  280.8 0.6 copy.45
  281.5 1.3 slice_bitcast_fusion.5
  282.8 1.3 slice_bitcast_fusion.4
  284.1 0.0 copy-start.1
  284.1 0.0 copy-start
  284.1 17.7 %weight_grads.1 = (f32[4,768,768]{2,1,0:T(8,128)}, f32[4,768,768]{2,1,0:T(8,128)}) custom-call(bf16[4,1024,768]{2,1,0:T(8,128)(2,1)} %bitcast.38, bf16[4,1024,768]{2,1,0:T(8,128)(2,1)} %bitcast.39, bf16[4,1024,768]{2,1,0:T(8,128)(2,1)} %bitcast.40, bf16[4,1024,768]{2,1,0:T(8,128)(2,1)} %bitcast.41), custom_call_target="tpu_custom_call" | custom-call | tf_op jit(solution)/shard_map/weight_grads/pallas_call | solution.py:884
  301.8 0.0 copy-done.1
  301.8 0.9 copy.49
  302.6 0.0 copy-done
  302.6 1.1 copy.50
  (4 shorter events, 0.1 us)
Async XLA Ops:
  95.7 97.6 %copy-start.2 = (f32[512,32]{1,0:T(8,128)S(1)}, f32[512,32]{1,0:T(8,128)}, u32[]{:S(2)}) copy-start(f32[512,32]{1,0:T(8,128)} %constant.28.clone) | copy-start | bytes 196612
  95.7 97.6 %copy-start.3 = (f32[32,12]{0,1:T(8,128)S(1)}, f32[32,12]{0,1:T(8,128)}, u32[]{:S(2)}) copy-start(f32[32,12]{0,1:T(8,128)} %param.23) | copy-start | bytes 4612
  284.1 17.7 %copy-start.1 = (bf16[512,768]{1,0:T(8,128)(2,1)S(1)}, bf16[512,768]{1,0:T(8,128)(2,1)}, u32[]{:S(2)}) copy-start(bf16[512,768]{1,0:T(8,128)(2,1)} %get-tuple-element.85) | copy-start | bytes 2359300
  284.1 18.6 %copy-start = (f32[512,768]{1,0:T(8,128)S(1)}, f32[512,768]{1,0:T(8,128)}, u32[]{:S(2)}) copy-start(f32[512,768]{1,0:T(8,128)} %get-tuple-element.86) | copy-start | bytes 4718596
